TPU v7x, 32 devices: a whole 2x2x4 slice. The times are simulated.
32 devices in a mesh: section: 2 (over y), inst: 2 (over x), tensor: 8 (over z, core).
Axes of the slice: x: 2, y: 2, z: 4, core: 2. Of those that a mesh axis runs over, the one named last changes fastest.
Arguments:
- hidden_in: bfloat16 [64, 8192], P('inst', 'tensor'), may hold values from -3 to 3
- queries: bfloat16 [2, 64, 8192], P('section', 'inst', 'tensor'), may hold values from -24 to 24
- new_kv: bfloat16 [2, 64, 2048], P('section', 'inst'), may hold values from -8 to 8
- kv_pages: bfloat16 [2, 16, 256, 2048], P('section', 'inst', 'tensor'), may hold values from -8 to 8
- out_weight: bfloat16 [2, 8192, 8192], P('section', 'tensor'), may hold values from -0.09375 to 0.09375
- move_pages: int32 [2, 2, 1], P('inst'), may hold values from 0 to 7, as said below
- page_table: int32 [16, 4], P('inst'), may hold values from 0 to 9, as said below
- lengths: int32 [16], P('inst'), may hold values from 256 to 1024, as said below
Outputs:
- residual: bfloat16 [2, 64, 8192], P('section', 'inst', 'tensor')
Inputs may be any that keep to these rules, and one draw needn't show every extreme that they name: `move_pages`: source page ids of the move; pages may repeat. `page_table`: pages may be shared between requests of one instance; the first page of every request is one received in the move, from source instance r % 8 % 2. `lengths`: every request has at least one full page.
All inputs are finite; a program needn't handle non-finite values.
Results may differ from a plain program's by a relative error of at most 0.015.
Values may be sent and summed in bfloat16 or wider, within the bound.
No kernel may reach another device: no remote copies, remote signals or barrier semaphores. Data moves between devices by JAX's collectives and lax.ppermute only.
A program may use at most 128 MiB of HBM per device.

v0:
```python
import jax
import jax.numpy as jnp
from jax import lax
from jax.sharding import PartitionSpec as P

HEADS = 64
KVH = 8
HD = 128
STEPS = 4


def passed_along(value, axis, steps):
    count = lax.axis_size(axis)
    initial, last = (max(0, -steps), min(count, count - steps))
    return lax.ppermute(value, axis, [(source, source + steps) for source in range(initial, last)])


def local(hidden_in, queries, new_kv, kv_pages, out_weight, move_pages, page_table, lengths):
    tensor_count = lax.axis_size("tensor")
    tensor_rank = lax.axis_index("tensor")
    section_rank = lax.axis_index("section")
    group_size = HEADS // KVH
    heads_per = HEADS // tensor_count
    score_scale = 1.0 / HD**0.5
    own_pages = kv_pages[0]
    slice_tokens = own_pages.shape[1]
    width = own_pages.shape[2]
    request_count = page_table.shape[0]
    table_width = page_table.shape[1]
    row_count = request_count * STEPS
    outgoing = own_pages[move_pages[0]]
    arrived = lax.all_to_all(outgoing, "inst", split_axis=0, concat_axis=0, tiled=True)
    page_pool = jnp.concatenate([own_pages, arrived.reshape(-1, slice_tokens, width)], axis=0)
    whole_queries = lax.all_gather(queries[0], "tensor", axis=1, tiled=True)
    grouped_queries = whole_queries.reshape(request_count, STEPS, KVH, group_size, HD)
    step_ids = jnp.arange(STEPS, dtype=jnp.int32)
    fresh_tokens = new_kv[0].reshape(request_count, STEPS, KVH, 2 * HD)
    cached_tokens = page_pool[page_table.reshape(-1)].reshape(
        request_count, table_width * slice_tokens, KVH, 2 * HD
    )
    all_tokens = jnp.concatenate([cached_tokens, fresh_tokens], axis=1)
    key_part = all_tokens[..., :HD]
    value_part = all_tokens[..., HD:]
    page_ids = jnp.arange(table_width, dtype=jnp.int32)[:, None]
    offsets = jnp.arange(slice_tokens, dtype=jnp.int32)[None, :]
    positions = (
        page_ids * (slice_tokens * tensor_count) + tensor_rank * slice_tokens + offsets
    ).reshape(-1)
    cached_live = positions[None, :] < lengths[:, None]
    fresh_live = (step_ids[None, :] <= step_ids[:, None]) & (tensor_rank == 0)
    live_mask = jnp.concatenate(
        [
            jnp.broadcast_to(cached_live[:, None, :], (request_count, STEPS, cached_live.shape[1])),
            jnp.broadcast_to(fresh_live[None, :, :], (request_count, STEPS, STEPS)),
        ],
        axis=2,
    )
    live_mask = live_mask[:, :, None, None, :]
    scores = (
        jnp.einsum(
            "rsgqd,rtgd->rsgqt", grouped_queries, key_part, preferred_element_type=jnp.float32
        )
        * score_scale
    )
    scores = jnp.where(live_mask, scores, jnp.float32(-1e30))
    row_max = jnp.max(scores, axis=-1)
    expo = jnp.where(live_mask, jnp.exp(scores - row_max[..., None]), jnp.float32(0.0))
    weight_sum = jnp.sum(expo, axis=-1)
    weighted = jnp.einsum(
        "rsgqt,rtgd->rsgqd",
        expo.astype(jnp.bfloat16),
        value_part,
        preferred_element_type=jnp.float32,
    )
    row_max = row_max.reshape(row_count, HEADS)
    weight_sum = weight_sum.reshape(row_count, HEADS)
    weighted = weighted.reshape(row_count, HEADS, HD)
    got_acc, got_max, got_sum = (
        lax.all_to_all(weighted[None], "tensor", split_axis=2, concat_axis=0, tiled=True),
        lax.all_to_all(
            row_max[None, :, :, None], "tensor", split_axis=2, concat_axis=0, tiled=True
        ),
        lax.all_to_all(
            weight_sum[None, :, :, None], "tensor", split_axis=2, concat_axis=0, tiled=True
        ),
    )
    overall_max = jnp.max(got_max, axis=0)
    rescale = jnp.exp(got_max - overall_max[None])
    own_sum = jnp.sum(got_sum * rescale, axis=0)
    own_acc = jnp.sum(got_acc * rescale, axis=0)
    attended = own_acc / own_sum
    attended = attended.astype(jnp.bfloat16).reshape(row_count, heads_per * HD)
    partial_term = jnp.dot(attended, out_weight[0], preferred_element_type=jnp.float32)
    projected = lax.psum_scatter(
        partial_term.astype(jnp.bfloat16), "tensor", scatter_dimension=1, tiled=True
    ).astype(jnp.float32)
    after_first = (hidden_in.astype(jnp.float32) + projected).astype(jnp.bfloat16)
    handed_over = passed_along(after_first, "section", 1)
    after_second = (handed_over.astype(jnp.float32) + projected).astype(jnp.bfloat16)
    result = jnp.where(section_rank == 0, after_first, after_second)
    return result[None]


def solution(mesh):
    return jax.shard_map(
        local,
        mesh=mesh,
        in_specs=(
            P("inst", "tensor"),
            P("section", "inst", "tensor"),
            P("section", "inst", None),
            P("section", "inst", "tensor", None),
            P("section", "tensor", None),
            P("inst", None, None),
            P("inst", None),
            P("inst"),
        ),
        out_specs=P("section", "inst", "tensor"),
        check_vma=False,
    )
```

profile of v0, /device:TPU:0, one launch (start us, length us, event | category | flops | bytes accessed | tf_op | source)
XLA Modules:
  0.0 149.2 jit_solution(7566383617139320563)
XLA Ops:
  6.5 0.7 fusion.26
  7.3 2.5 %gather_fusion = bf16[2,32,2048]{2,1,0:T(8,128)(2,1)} fusion(bf16[8,32,2048]{2,1,0:T(8,128)(2,1)} %bitcast.93, s32[1024]{0:T(1024)S(1)} %pad_clamp_fusion.1), kind=kCustom, calls=%fused_computation | custom fusion | bytes 524296 | tf_op jit(solution)/shard_map/gather | solution.py:31
  9.8 4.2 %all-to-all-start = ((bf16[2,1,32,2048]{3,2,1,0:T(8,128)(2,1)}), bf16[2,1,32,2048]{3,2,1,0:T(8,128)(2,1)S(1)}, u32[]{:S(2)}, u32[]{:S(2)}) async-start(bf16[2,1,32,2048]{3,2,1,0:T(8,128)(2,1)} %bitcast.3), calls=%async_computation | async-start | bytes 524288 | tf_op jit(solution)/shard_map/all_to_all | solution.py:32
  14.0 0.8 copy.48
  15.0 16.0 %all-gather = bf16[1,32,8192]{2,1,0:T(8,128)(2,1)S(1)} all-gather(bf16[1,32,1024]{2,1,0:T(8,128)(2,1)} %param.9), channel_id=2, replica_groups=mesh['section'=2,'inst'=2,'tensor'=8] {'tensor'}, dimensions={2}, use_global_device_ids=true | all-gather | bytes 589824 | tf_op jit(solution)/shard_map/all_gather | solution.py:34
  31.0 0.7 broadcast_compare_fusion
  31.8 0.9 copy.63
  33.0 2.7 %gather_fusion.1 = bf16[32,32,2048]{2,1,0:T(8,128)(2,1)} fusion(bf16[10,32,2048]{2,1,0:T(8,128)(2,1)S(1)} %pad_maximum_fusion, s32[1024]{0:T(1024)S(1)} %pad_clamp_fusion), kind=kCustom, calls=%fused_computation.1 | custom fusion | bytes 8388736 | tf_op jit(solution)/shard_map/gather | solution.py:38
  35.8 3.7 %copy.62 = bf16[128,8,8,256]{3,2,1,0:T(8,128)(2,1)S(1)} copy(bf16[128,8,8,256]{3,1,2,0:T(8,128)(2,1)} %bitcast.88) | data formatting | bytes 8388608
  39.4 0.9 copy_dynamic-update-slice_fusion
  40.4 1.7 %fusion.7 = (f32[8,4,8,8]{3,1,2,0:T(4,128)S(1)}, f32[8,8,132,4,8]{2,4,3,1,0:T(8,128)S(1)}) fusion(pred[8,4,132]{2,1,0:T(4,128)(4,1)S(1)} %pad_add_fusion, bf16[8,4,8,8,128]{4,3,2,1,0:T(8,128)(2,1)S(1)} %bitcast.99, bf16[8,132,8,256]{3,1,2,0:T(8,128)(2,1)S(1)} %copy_dynamic-update-slice_fusion.1), kind=kOutput, calls=%fused_computation.12 | convolution fusion | flops 70014976 | bytes 3850240 | tf_op jit(solution)/shard_map/rsgqd,rtgd->rsgqt/dot_general | solution.py:60
  43.3 0.8 reduce.3
  44.0 0.7 reshape.213
  44.7 4.6 %all-to-all-start.2 = ((f32[8,1,256]{2,1,0:T(1,128)}), f32[8,1,256]{2,1,0:T(1,128)S(1)}, u32[]{:S(2)}, u32[]{:S(2)}) async-start(f32[8,1,256]{2,1,0:T(1,128)} %reshape.213), calls=%async_computation.2 | async-start | bytes 16384 | tf_op jit(solution)/shard_map/all_to_all | solution.py:80
  49.4 1.1 fusion.8
  50.6 0.8 reduce.5
  51.4 0.7 reshape.215
  52.1 2.9 %all-to-all-done.2 = f32[8,1,256]{2,1,0:T(1,128)S(1)} async-done(((f32[8,1,256]{2,1,0:T(1,128)}), f32[8,1,256]{2,1,0:T(1,128)S(1)}, u32[]{:S(2)}, u32[]{:S(2)}) %all-to-all-start.2) | async-done | bytes 8224 | tf_op jit(solution)/shard_map/all_to_all | solution.py:80
  55.0 3.3 %all-to-all-start.3 = ((f32[8,1,256]{2,1,0:T(1,128)}), f32[8,1,256]{2,1,0:T(1,128)S(1)}, u32[]{:S(2)}, u32[]{:S(2)}) async-start(f32[8,1,256]{2,1,0:T(1,128)} %reshape.215), calls=%async_computation.3 | async-start | bytes 16384 | tf_op jit(solution)/shard_map/all_to_all | solution.py:83
  58.3 2.4 %fusion.10 = f32[8,4,8,8,128]{4,3,1,2,0:T(8,128)S(1)} fusion(bf16[8,132,8,256]{3,1,2,0:T(8,128)(2,1)} %copy-done, f32[8,8,132,4,8]{2,4,3,1,0:T(8,128)S(1)} %get-tuple-element.6, f32[8,4,8,8]{3,1,2,0:T(4,128)S(1)} %get-tuple-element.5, pred[8,4,132]{2,1,0:T(4,128)(4,1)S(1)} %pad_add_fusion), kind=kOutput, calls=%fused_computation.15 | convolution fusion | flops 70557696 | bytes 4370560 | tf_op jit(solution)/shard_map/rsgqt,rtgd->rsgqd/dot_general | solution.py:69
  60.8 1.6 %copy.53 = f32[1,32,64,128]{3,1,0,2:T(8,128)} copy(f32[1,32,64,128]{3,2,1,0:T(8,128)S(1)} %bitcast.91) | data formatting | bytes 2097152 | tf_op jit(solution)/shard_map/broadcast_in_dim;reshape | solution.py:79
  62.4 1.4 all-to-all-done.3
  63.8 3.6 %all-to-all-start.1 = ((f32[1,32,64,128]{3,1,0,2:T(8,128)}), f32[1,32,64,128]{3,1,0,2:T(8,128)S(1)}, u32[]{:S(2)}, u32[]{:S(2)}) async-start(f32[1,32,64,128]{3,1,0,2:T(8,128)} %copy.53), calls=%async_computation.1 | async-start | bytes 2097152 | tf_op jit(solution)/shard_map/all_to_all | solution.py:79
  67.5 0.7 reduce.4
  68.3 0.7 reduce.6
  69.2 24.8 %all-to-all-done.1 = f32[1,32,64,128]{3,1,0,2:T(8,128)S(1)} async-done(((f32[1,32,64,128]{3,1,0,2:T(8,128)}), f32[1,32,64,128]{3,1,0,2:T(8,128)S(1)}, u32[]{:S(2)}, u32[]{:S(2)}) %all-to-all-start.1) | async-done | bytes 1048608 | tf_op jit(solution)/shard_map/all_to_all | solution.py:79
  94.4 9.7 %fusion.2 = bf16[32,8192]{1,0:T(8,128)(2,1)} fusion(bf16[1,1024,8192]{2,1,0:T(8,128)(2,1)} %param.12, f32[32,8,128]{2,0,1:T(8,128)S(1)} %multiply_reduce_fusion, f32[32,8]{0,1:T(8,128)S(1)} %multiply_reduce_fusion.1), kind=kOutput, calls=%fused_computation.4 | convolution fusion | flops 537198592 | bytes 17433600 | tf_op jit(solution)/shard_map/dot_general | solution.py:93
  104.1 30.6 %reduce-scatter.2.cloned.1.call-done = bf16[32,1024]{1,0:T(8,128)(2,1)} async-done(((bf16[32,8192]{1,0:T(8,128)(2,1)}), bf16[32,1024]{1,0:T(8,128)(2,1)}) %reduce-scatter.2.cloned.1.call-update) | async-done | bytes 65552 | tf_op jit(solution)/shard_map/reduce_scatter | solution.py:94
  134.7 0.9 fusion.18
  135.6 3.4 %collective-permute-start = (bf16[32,1024]{1,0:T(8,128)(2,1)S(1)}, bf16[32,1024]{1,0:T(8,128)(2,1)S(1)}, u32[]{:S(2)}, u32[]{:S(2)}) collective-permute-start(bf16[32,1024]{1,0:T(8,128)(2,1)S(1)} %fusion.18), channel_id=1, source_target_pairs={{0,16},{1,17},{2,18},{3,19},{4,20},{5,21},{6,22},{7,23},{8,24},{9,... | collective-permute-start | bytes 196616 | tf_op jit(solution)/shard_map/ppermute | solution.py:15
  139.0 1.9 %collective-permute-done = bf16[32,1024]{1,0:T(8,128)(2,1)S(1)} collective-permute-done((bf16[32,1024]{1,0:T(8,128)(2,1)S(1)}, bf16[32,1024]{1,0:T(8,128)(2,1)S(1)}, u32[]{:S(2)}, u32[]{:S(2)}) %collective-permute-start) | collective-permute-done | bytes 65568 | tf_op jit(solution)/shard_map/ppermute | solution.py:15
  140.9 1.5 %fusion.21 = bf16[1,32,1024]{2,1,0:T(8,128)(2,1)} fusion(bf16[32,1024]{1,0:T(8,128)(2,1)S(1)} %fusion.18, bf16[32,1024]{1,0:T(8,128)(2,1)} %reduce-scatter.2.cloned.1.call-done, bf16[32,1024]{1,0:T(8,128)(2,1)S(1)} %collective-permute-done, pred[]{:T(512)S(6)} %eq.6), kind=kLoop, calls=%fused_computation.31 | loop fusion | flops 163840 | bytes 262145 | tf_op jit(solution)/shard_map/broadcast_in_dim | solution.py:101
  (37 shorter events, 2.7 us)
Async XLA Ops:
  6.5 26.4 %copy-start.1 = (bf16[1,8,32,2048]{3,2,1,0:T(8,128)(2,1)S(1)}, bf16[1,8,32,2048]{3,2,1,0:T(8,128)(2,1)}, u32[]{:S(2)}) copy-start(bf16[1,8,32,2048]{3,2,1,0:T(8,128)(2,1)} %param.11) | copy-start | bytes 3145732
  9.8 23.1 %all-to-all-start = ((bf16[2,1,32,2048]{3,2,1,0:T(8,128)(2,1)}), bf16[2,1,32,2048]{3,2,1,0:T(8,128)(2,1)S(1)}, u32[]{:S(2)}, u32[]{:S(2)}) async-start(bf16[2,1,32,2048]{3,2,1,0:T(8,128)(2,1)} %bitcast.3), calls=%async_computation | async-start | bytes 524288 | tf_op jit(solution)/shard_map/all_to_all | solution.py:32
  40.4 2.0 %copy-start = (bf16[8,132,8,256]{3,1,2,0:T(8,128)(2,1)}, bf16[8,132,8,256]{3,1,2,0:T(8,128)(2,1)S(1)}, u32[]{:S(2)}) copy-start(bf16[8,132,8,256]{3,1,2,0:T(8,128)(2,1)S(1)} %copy_dynamic-update-slice_fusion.1) | copy-start | bytes 12976132
  44.7 10.2 %all-to-all-start.2 = ((f32[8,1,256]{2,1,0:T(1,128)}), f32[8,1,256]{2,1,0:T(1,128)S(1)}, u32[]{:S(2)}, u32[]{:S(2)}) async-start(f32[8,1,256]{2,1,0:T(1,128)} %reshape.213), calls=%async_computation.2 | async-start | bytes 16384 | tf_op jit(solution)/shard_map/all_to_all | solution.py:80
  55.0 8.9 %all-to-all-start.3 = ((f32[8,1,256]{2,1,0:T(1,128)}), f32[8,1,256]{2,1,0:T(1,128)S(1)}, u32[]{:S(2)}, u32[]{:S(2)}) async-start(f32[8,1,256]{2,1,0:T(1,128)} %reshape.215), calls=%async_computation.3 | async-start | bytes 16384 | tf_op jit(solution)/shard_map/all_to_all | solution.py:83
  63.8 30.2 %all-to-all-start.1 = ((f32[1,32,64,128]{3,1,0,2:T(8,128)}), f32[1,32,64,128]{3,1,0,2:T(8,128)S(1)}, u32[]{:S(2)}, u32[]{:S(2)}) async-start(f32[1,32,64,128]{3,1,0,2:T(8,128)} %copy.53), calls=%async_computation.1 | async-start | bytes 2097152 | tf_op jit(solution)/shard_map/all_to_all | solution.py:79
  67.5 67.3 %reduce-scatter.2.cloned.1.call-start = ((), (), s32[]{:S(2)}) async-start(), calls=%async_computation.5 | async-start | bytes 589824 | tf_op jit(solution)/shard_map/reduce_scatter | solution.py:94
  94.4 40.3 %copy-start.2 = (bf16[32,1024]{1,0:T(8,128)(2,1)S(1)}, bf16[32,1024]{1,0:T(8,128)(2,1)}, u32[]{:S(2)}) copy-start(bf16[32,1024]{1,0:T(8,128)(2,1)} %param.8) | copy-start | bytes 196612
  135.6 5.3 %collective-permute-start = (bf16[32,1024]{1,0:T(8,128)(2,1)S(1)}, bf16[32,1024]{1,0:T(8,128)(2,1)S(1)}, u32[]{:S(2)}, u32[]{:S(2)}) collective-permute-start(bf16[32,1024]{1,0:T(8,128)(2,1)S(1)} %fusion.18), channel_id=1, source_target_pairs={{0,16},{1,17},{2,18},{3,19},{4,20},{5,21},{6,22},{7,23},{8,24},{9,... | collective-permute-start | bytes 196616 | tf_op jit(solution)/shard_map/ppermute | solution.py:15
Sparse Core Ops, SparseCore 0:
  104.2 30.4 reduce-scatter.1
where the time goes:
time: 150 us; the launch traced here: 149 us
  waiting for transfers between devices  61.6 us (41%)
  starting transfers between devices  19.2 us (13%)
  local copies, waits for them, and re-layouts  16.4 us (11%)
  blocking collectives  16 us (11%)
  matrix products  13.7 us (9%)
  between operations  13.7 us (9%)
  other arithmetic  8.48 us (6%)
    reduce_scatter x1, waiting for transfers between devices, local(): lax.psum_scatter(partial_term.astype(jnp.bfloat16), 'tensor', scatter_dim...  30.6 us
    all_to_all x1, waiting for transfers between devices, local(): lax.all_to_all(weighted[None], 'tensor', split_axis=2, concat_axis=0, til...  24.8 us
    all_gather x1, blocking collectives, local(): whole_queries = lax.all_gather(queries[0], 'tensor', axis=1, tiled=True)  16 us
    dot_general x1, matrix products, local(): jnp.dot(attended, out_weight[0], preferred_element_type=jnp.float32)  9.66 us
    unnamed x16, local copies, waits for them, and re-layouts  8.85 us
    all_to_all x1, starting transfers between devices, local(): lax.all_to_all(row_max[None, :, :, None], 'tensor', split_axis=2, concat_...  4.64 us
    all_to_all x1, starting transfers between devices, local(): lax.all_to_all(outgoing, 'inst', split_axis=0, concat_axis=0, tiled=True)  4.21 us
    all_to_all x1, starting transfers between devices, local(): lax.all_to_all(weighted[None], 'tensor', split_axis=2, concat_axis=0, til...  3.63 us
  transfers between devices with their start and end apart: 6, of which 5 were waited for; matrix products, arithmetic and copies ran while one was open for 8% of the time, Pallas kernels for 0%

commit v1 on v0

v1 whole, which is shorter than its diff:
```python
import functools
import math

import jax
import jax.numpy as jnp
from jax import lax
from jax.experimental import pallas as pl
from jax.experimental.pallas import tpu as pltpu
from jax.sharding import PartitionSpec as P

HEADS = 64
KVH = 8
HD = 128
STEPS = 4
GROUP = HEADS // KVH
MASKED = -1e30
LOG2E = 1.4426950408889634


def swapped(value, mask):
    count = lax.axis_size("tensor")
    return lax.ppermute(value, "tensor", [(source, source ^ mask) for source in range(count)])


def attend_kernel(
    requests, page_tokens, pages, tensor_count, inst_count, capacity, query_count, piece_count, *refs
):
    place, table, lengths, moves = refs[:4]
    queries = refs[4 : 4 + query_count]
    pieces = refs[4 + query_count : 4 + query_count + piece_count]
    outputs = refs[4 + query_count + piece_count :]
    tensor_rank, inst_rank = place[0], place[1]
    per = max(1, tensor_count // KVH)
    head_rank = tensor_rank // per
    partner = tensor_rank ^ per
    rows = requests * STEPS
    slots = table.shape[1]
    page_size = page_tokens * tensor_count

    row = lax.broadcasted_iota(jnp.int32, (rows, 1), 0)
    row_request, row_step = row // STEPS, row % STEPS
    row_length = jnp.zeros((rows, 1), jnp.int32)
    row_pages = [jnp.zeros((rows, 1), jnp.int32) for _ in range(slots)]
    for request in range(requests):
        here = row_request == request
        row_length = jnp.where(here, lengths[request], row_length)
        for slot in range(slots):
            page = table[request, slot]
            arrived = page - pages
            for own in range(capacity):
                page = jnp.where(arrived == inst_rank * capacity + own, moves[inst_rank, own], page)
            row_pages[slot] = jnp.where(here, page, row_pages[slot])

    def times_used(page, token):
        used = jnp.zeros((rows, page.shape[1]), jnp.float32)
        for slot in range(slots):
            live = (row_pages[slot] == page) & (token + slot * page_size < row_length)
            used = used + jnp.where(live, 1.0, 0.0)
        return used

    def column(count):
        return lax.broadcasted_iota(jnp.int32, (1, count), 1)

    def arrived_page(block):
        shift = block // capacity + 1
        source = inst_rank - shift
        source = jnp.where(source < 0, source + inst_count, source)
        return pages + source * capacity + block % capacity

    use = []
    own_columns = pages * page_tokens
    moved_columns = (inst_count - 1) * capacity * page_tokens
    for rank in (tensor_rank, partner):
        spot = column(own_columns)
        use.append(times_used(spot // page_tokens, rank * page_tokens + spot % page_tokens))
    for rank in (tensor_rank, partner):
        spot = column(moved_columns)
        use.append(
            times_used(arrived_page(spot // page_tokens), rank * page_tokens + spot % page_tokens)
        )
    spot = column(rows)
    fresh = (spot // STEPS == row_request) & (spot % STEPS <= row_step)
    fresh = fresh & ((tensor_rank == 0) | (tensor_rank == per))
    use.append(jnp.where(fresh, 1.0, 0.0))
    use = jnp.concatenate(use, axis=1)
    columns = use.shape[1]
    use = use[None]

    heads_per = HEADS // tensor_count
    lane = lax.broadcasted_iota(jnp.int32, (rows, HD), 1)
    factor = LOG2E / math.sqrt(HD)
    for group in range(query_count // per):
        kv_head = head_rank ^ (2 * group)
        base = pl.multiple_of(kv_head * (2 * HD), 2 * HD)
        keys = jnp.concatenate([piece[:, pl.ds(base, HD)] for piece in pieces], axis=0)
        values = jnp.concatenate(
            [piece[:, pl.ds(pl.multiple_of(base + HD, HD), HD)] for piece in pieces], axis=0
        )
        blocks = []
        for low in range(per):
            block = queries[group * per + low]
            blocks += [block[:, head * HD : (head + 1) * HD] for head in range(heads_per)]
        stacked = jnp.concatenate(blocks, axis=0)
        scores = lax.dot_general(
            stacked, keys, (((1,), (1,)), ((), ())), preferred_element_type=jnp.float32
        )
        scores = scores.reshape(GROUP, rows, columns)
        scores = jnp.where(use > 0.0, scores, MASKED)
        row_max = jnp.max(scores, axis=-1, keepdims=True)
        expo = jnp.exp2((scores - row_max) * factor) * use
        total = jnp.sum(expo, axis=-1, keepdims=True)
        weighted = jnp.dot(
            expo.astype(jnp.bfloat16).reshape(GROUP * rows, columns),
            values,
            preferred_element_type=jnp.float32,
        )
        weighted = (weighted.reshape(GROUP, rows, HD) / total).astype(jnp.bfloat16)
        level = row_max * factor + jnp.log2(total)
        for low in range(per):
            out = outputs[group * per + low]
            stat = jnp.zeros((rows, HD), jnp.float32)
            for head in range(heads_per):
                at = low * heads_per + head
                out[:, head * HD : (head + 1) * HD] = weighted[at]
                stat = jnp.where(lane % heads_per == head, level[at], stat)
            top = stat.astype(jnp.bfloat16).astype(jnp.float32)
            rest = stat - top
            middle = rest.astype(jnp.bfloat16).astype(jnp.float32)
            stat = jnp.where(
                lane < heads_per, top, jnp.where(lane < 2 * heads_per, middle, rest - middle)
            )
            out[:, heads_per * HD :] = stat.astype(jnp.bfloat16)


def combine(parts, heads_per):
    levels = []
    for part in parts:
        stat = part[:, heads_per * HD :].astype(jnp.float32)
        levels.append(
            stat
            + pltpu.roll(stat, HD - heads_per, 1)
            + pltpu.roll(stat, HD - 2 * heads_per, 1)
        )
    top = functools.reduce(jnp.maximum, levels)
    shares = [jnp.exp2(level - top) for level in levels]
    total = sum(shares[1:], shares[0])
    shares = [share / total for share in shares]
    heads = []
    for head in range(heads_per):
        terms = [
            share[:, head : head + 1] * part[:, head * HD : (head + 1) * HD].astype(jnp.float32)
            for share, part in zip(shares, parts)
        ]
        heads.append(sum(terms[1:], terms[0]).astype(jnp.bfloat16))
    return jnp.concatenate(heads, axis=1)


def first_project_kernel(heads_per, part_count, place, *refs):
    parts, (weight, out, attended) = refs[:part_count], refs[part_count:]

    @pl.when(pl.program_id(0) == 0)
    def _():
        attended[...] = combine(parts, heads_per)

    out[0] = jnp.dot(
        attended[...], weight[0], preferred_element_type=jnp.float32
    ).astype(jnp.bfloat16)


def second_project_kernel(place, attended, other, weight, out, own):
    total = jnp.dot(attended[...], weight[0], preferred_element_type=jnp.float32)
    total = total + other[0].astype(jnp.float32)
    out[0] = total.astype(jnp.bfloat16)

    @pl.when(pl.program_id(0) == 0)
    def _():
        own[...] = total


def local(hidden_in, queries, new_kv, kv_pages, out_weight, move_pages, page_table, lengths):
    tensor_count = lax.axis_size("tensor")
    inst_count = lax.axis_size("inst")
    tensor_rank = lax.axis_index("tensor")
    inst_rank = lax.axis_index("inst")
    section_rank = lax.axis_index("section")
    per = max(1, tensor_count // KVH)
    heads_per = HEADS // tensor_count
    requests = page_table.shape[0]
    rows = requests * STEPS
    own_pages = kv_pages[0]
    pages, page_tokens, width = own_pages.shape
    capacity = move_pages.shape[2]
    moves = move_pages[0]
    peers = [mask for mask in range(tensor_count) if mask & per == 0]

    own_queries = queries[0]
    all_queries = [own_queries] + [swapped(own_queries, mask) for mask in peers[1:]]
    own_flat = own_pages.reshape(pages * page_tokens, width)
    partner_flat = swapped(own_flat, per)
    arrived = []
    for shift in range(1, inst_count):
        leaving = own_pages[moves[(inst_rank + shift) % inst_count]]
        pairs = [(source, (source + shift) % inst_count) for source in range(inst_count)]
        arrived.append(lax.ppermute(leaving.reshape(-1, width), "inst", pairs))
    arrived = arrived[0] if len(arrived) == 1 else jnp.concatenate(arrived, axis=0)
    partner_arrived = swapped(arrived, per)
    pieces = [own_flat, partner_flat, arrived, partner_arrived, new_kv[0]]
    if arrived.shape[0] % 16:
        pieces = pieces[:2] + [jnp.concatenate([arrived, partner_arrived], axis=0)] + pieces[4:]

    place = jnp.stack([tensor_rank, inst_rank]).astype(jnp.int32)
    smem = pl.BlockSpec(memory_space=pltpu.SMEM)
    vmem = pl.BlockSpec(memory_space=pltpu.VMEM)
    part_shape = jax.ShapeDtypeStruct((rows, heads_per * HD + HD), jnp.bfloat16)
    parts = pl.pallas_call(
        functools.partial(
            attend_kernel,
            requests,
            page_tokens,
            pages,
            tensor_count,
            inst_count,
            capacity,
            len(peers),
            len(pieces),
        ),
        out_shape=[part_shape] * len(peers),
        in_specs=[smem] * 4 + [vmem] * (len(peers) + len(pieces)),
        out_specs=[vmem] * len(peers),
        compiler_params=pltpu.CompilerParams(vmem_limit_bytes=32 * 1024 * 1024),
        name="attend",
    )(place, page_table, lengths, moves, *all_queries, *pieces)
    parts = [parts[0]] + [swapped(part, mask) for part, mask in zip(parts[1:], peers[1:])]

    depth, features = out_weight.shape[1:]
    chunk = features // tensor_count
    half = tensor_count // 2
    part_spec = pl.BlockSpec(part_shape.shape, lambda step, place: (0, 0))
    attended_spec = pl.BlockSpec((rows, depth), lambda step, place: (0, 0))
    chunk_spec = pl.BlockSpec((1, rows, chunk), lambda step, place: (step, 0, 0))
    away, attended = pl.pallas_call(
        functools.partial(first_project_kernel, heads_per, len(peers)),
        grid_spec=pltpu.PrefetchScalarGridSpec(
            num_scalar_prefetch=1,
            grid=(half,),
            in_specs=[part_spec] * len(peers)
            + [pl.BlockSpec((1, depth, chunk), lambda step, place: (0, 0, place[0] ^ (2 * step + 1)))],
            out_specs=[chunk_spec, attended_spec],
        ),
        out_shape=[
            jax.ShapeDtypeStruct((half, rows, chunk), jnp.bfloat16),
            jax.ShapeDtypeStruct((rows, depth), jnp.bfloat16),
        ],
        compiler_params=pltpu.CompilerParams(vmem_limit_bytes=32 * 1024 * 1024),
        name="project_away",
    )(place, *parts, out_weight)
    other = swapped(away, 1)
    paired, own = pl.pallas_call(
        second_project_kernel,
        grid_spec=pltpu.PrefetchScalarGridSpec(
            num_scalar_prefetch=1,
            grid=(half,),
            in_specs=[
                attended_spec,
                chunk_spec,
                pl.BlockSpec((1, depth, chunk), lambda step, place: (0, 0, place[0] ^ (2 * step))),
            ],
            out_specs=[chunk_spec, pl.BlockSpec((rows, chunk), lambda step, place: (0, 0))],
        ),
        out_shape=[
            jax.ShapeDtypeStruct((half, rows, chunk), jnp.bfloat16),
            jax.ShapeDtypeStruct((rows, chunk), jnp.float32),
        ],
        compiler_params=pltpu.CompilerParams(vmem_limit_bytes=32 * 1024 * 1024),
        name="project_home",
    )(place, attended, other, out_weight)
    projected = own
    for at in range(1, half):
        projected = projected + swapped(paired[at], 2 * at).astype(jnp.float32)
    after_first = (hidden_in.astype(jnp.float32) + projected).astype(jnp.bfloat16)
    handed_over = lax.ppermute(after_first, "section", [(0, 1), (1, 0)])
    after_second = (handed_over.astype(jnp.float32) + projected).astype(jnp.bfloat16)
    result = jnp.where(section_rank == 0, after_first, after_second)
    return result[None]


def solution(mesh):
    return jax.shard_map(
        local,
        mesh=mesh,
        in_specs=(
            P("inst", "tensor"),
            P("section", "inst", "tensor"),
            P("section", "inst", None),
            P("section", "inst", "tensor", None),
            P("section", "tensor", None),
            P("inst", None, None),
            P("inst", None),
            P("inst"),
        ),
        out_specs=P("section", "inst", "tensor"),
        check_vma=False,
    )
```

time: 150 us -> 72.3 us (0.48)
  waiting for transfers between devices: 61.6 us -> 24.4 us
  blocking collectives: 16 us -> 0 us
  matrix products: 13.7 us -> 0 us
  between operations: 13.7 us -> 1.95 us
  Pallas kernels: 0 us -> 8.87 us
  other arithmetic: 8.48 us -> 0.8 us
  local copies, waits for them, and re-layouts: 16.4 us -> 18.8 us
  starting transfers between devices: 19.2 us -> 17 us
    reduce_scatter x1 -> x0, waiting for transfers between devices: 30.6 us -> none  [local(): lax.psum_scatter(partial_term.astype(jnp.bfloat16), 'tensor', scatter_dim...]
    all_to_all x4 -> x0, waiting for transfers between devices: 29.1 us -> none  [the longest x1 24.8 us: local(): lax.all_to_all(weighted[None], 'tensor', split_axis=2, concat_axis=0, til...]
    ppermute x1 -> x14, waiting for transfers between devices: 1.88 us -> 24.4 us  [the longest x12 17.5 us: swapped(): lax.ppermute(value, 'tensor', [(source, source ^ mask) for source in rang...]
    all_gather x1 -> x0, blocking collectives: 16 us -> none  [local(): whole_queries = lax.all_gather(queries[0], 'tensor', axis=1, tiled=True)]
    all_to_all x4 -> x0, starting transfers between devices: 15.8 us -> none  [the longest x1 4.64 us: local(): lax.all_to_all(row_max[None, :, :, None], 'tensor', split_axis=2, concat_...]
    dot_general x3 -> x0, matrix products: 13.7 us -> none  [the longest x1 9.66 us: local(): jnp.dot(attended, out_weight[0], preferred_element_type=jnp.float32)]
    ppermute x1 -> x14, starting transfers between devices: 3.37 us -> 17 us  [the longest x12 12.9 us: swapped(): lax.ppermute(value, 'tensor', [(source, source ^ mask) for source in rang...]
    pallas_call x0 -> x3, Pallas kernels: none -> 8.87 us  [the longest x1 3.34 us: local(): pl.pallas_call(functools.partial(first_project_kernel, heads_per, len(pee...]
  transfers between devices with their start and end apart: 6 -> 14, of which waited for: 5 -> 10; matrix products, arithmetic and copies ran while one was open for 8% -> 5% of each run, Pallas kernels for 0% -> 0%
where the time goes in v1:
time: 72.3 us; the launch traced here: 71.9 us
  waiting for transfers between devices  24.4 us (34%)
  local copies, waits for them, and re-layouts  18.8 us (26%)
  starting transfers between devices  17 us (24%)
  Pallas kernels  8.87 us (12%)
  between operations  1.95 us (3%)
  other arithmetic  0.8 us (1%)
    ppermute x12, waiting for transfers between devices, swapped(): lax.ppermute(value, 'tensor', [(source, source ^ mask) for source in rang...  17.5 us
    unnamed x15, local copies, waits for them, and re-layouts  15.9 us
    ppermute x12, starting transfers between devices, swapped(): lax.ppermute(value, 'tensor', [(source, source ^ mask) for source in rang...  12.9 us
    ppermute x1, waiting for transfers between devices, local(): arrived.append(lax.ppermute(leaving.reshape(-1, width), 'inst', pairs))  4.17 us
    pallas_call x1, Pallas kernels, local(): pl.pallas_call(functools.partial(first_project_kernel, heads_per, len(pee...  3.34 us
    pallas_call x1, Pallas kernels, local(): pl.pallas_call(second_project_kernel, grid_spec=pltpu.PrefetchScalarGridS...  3.01 us
    ppermute x1, waiting for transfers between devices, local(): handed_over = lax.ppermute(after_first, 'section', [(0, 1), (1, 0)])  2.75 us
    ppermute x1, starting transfers between devices, local(): arrived.append(lax.ppermute(leaving.reshape(-1, width), 'inst', pairs))  2.55 us
  transfers between devices with their start and end apart: 14, of which 10 were waited for; matrix products, arithmetic and copies ran while one was open for 5% of the time, Pallas kernels for 0%

profile of v1, /device:TPU:0, one launch (start us, length us, event | category | flops | bytes accessed | tf_op | source)
XLA Modules:
  0.0 71.9 jit_solution(3653854096757393785)
XLA Ops:
  0.5 1.2 %constant_dynamic-slice_fusion = s32[1,1,1]{1,2,0:T(1,128)} fusion(s32[1,2,1]{1,2,0:T(1,128)} %param.13, s32[]{:T(128)S(6)} %select_n.23), kind=kLoop, calls=%fused_computation.10 | loop fusion | bytes 12 | tf_op jit(solution)/shard_map/dynamic_slice | solution.py:202
  3.6 0.9 %dynamic-slice_bitcast_fusion = bf16[32,2048]{1,0:T(8,128)(2,1)S(1)} fusion(bf16[1,8,32,2048]{3,2,1,0:T(8,128)(2,1)} %param.11, s32[]{:T(128)} %bitcast.6), kind=kLoop, calls=%fused_computation | loop fusion | bytes 262148 | tf_op jit(solution)/shard_map/reshape | solution.py:204
  4.5 2.6 %collective-permute-start.4 = (bf16[32,2048]{1,0:T(8,128)(2,1)S(1)}, bf16[32,2048]{1,0:T(8,128)(2,1)S(1)}, u32[]{:S(2)}, u32[]{:S(2)}) collective-permute-start(bf16[32,2048]{1,0:T(8,128)(2,1)S(1)} %dynamic-slice_bitcast_fusion), channel_id=1, source_target_pairs={{0,8},{8,0},{1,9},{9,1},{2,10},{10,2},{3,11},{11,3},{4,12},{12,4},... | collective-permute-start | bytes 393224 | tf_op jit(solution)/shard_map/ppermute | solution.py:204
  7.1 4.2 %collective-permute-done.4.refs_10_ = bf16[32,2048]{1,0:T(8,128)(2,1)S(1)} collective-permute-done((bf16[32,2048]{1,0:T(8,128)(2,1)S(1)}, bf16[32,2048]{1,0:T(8,128)(2,1)S(1)}, u32[]{:S(2)}, u32[]{:S(2)}) %collective-permute-start.4) | collective-permute-done | bytes 131104 | tf_op jit(solution)/shard_map/ppermute | solution.py:204
  11.2 3.9 %collective-permute-start.2 = (bf16[32,1024]{1,0:T(8,128)(2,1)}, bf16[32,1024]{1,0:T(8,128)(2,1)S(1)}, u32[]{:S(2)}, u32[]{:S(2)}) collective-permute-start(bf16[32,1024]{1,0:T(8,128)(2,1)} %bitcast.21), channel_id=1, source_target_pairs={{0,6},{1,7},{2,4},{3,5},{4,2},{5,3},{6,0},{7,1},{8,14},{9,15},{10,... | collective-permute-start | bytes 196616 | tf_op jit(solution)/shard_map/ppermute | solution.py:22
  15.1 0.6 collective-permute-start
  15.6 0.7 %copy.10.refs_3_ = s32[2,1]{1,0:T(2,128)S(1)} copy(s32[2,1]{0,1:T(1,128)} %bitcast.25) | data formatting | bytes 16 | tf_op jit(solution)/shard_map/squeeze | solution.py:193
  16.4 0.8 %copy.9.refs_1_ = s32[8,4]{1,0:T(8,128)S(1)} copy(s32[8,4]{0,1:T(4,128)} %param.14) | data formatting | bytes 256 | tf_op args[6]
  17.2 1.0 %collective-permute-done.2.refs_7_ = bf16[32,1024]{1,0:T(8,128)(2,1)S(1)} collective-permute-done((bf16[32,1024]{1,0:T(8,128)(2,1)}, bf16[32,1024]{1,0:T(8,128)(2,1)S(1)}, u32[]{:S(2)}, u32[]{:S(2)}) %collective-permute-start.2) | collective-permute-done | bytes 65568 | tf_op jit(solution)/shard_map/ppermute | solution.py:22
  18.2 3.2 %collective-permute-done.1.refs_6_ = bf16[32,1024]{1,0:T(8,128)(2,1)S(1)} collective-permute-done((bf16[32,1024]{1,0:T(8,128)(2,1)}, bf16[32,1024]{1,0:T(8,128)(2,1)S(1)}, u32[]{:S(2)}, u32[]{:S(2)}) %collective-permute-start.1) | collective-permute-done | bytes 65568 | tf_op jit(solution)/shard_map/ppermute | solution.py:22
  21.4 1.2 %copy-done.2 = bf16[1,8,32,2048]{3,2,1,0:T(8,128)(2,1)S(1)} copy-done((bf16[1,8,32,2048]{3,2,1,0:T(8,128)(2,1)S(1)}, bf16[1,8,32,2048]{3,2,1,0:T(8,128)(2,1)}, u32[]{:S(2)}) %copy-start.2) | copy-done | bytes 1048600
  22.7 0.9 %copy-done.3 = bf16[1,32,2048]{2,1,0:T(8,128)(2,1)S(1)} copy-done((bf16[1,32,2048]{2,1,0:T(8,128)(2,1)S(1)}, bf16[1,32,2048]{2,1,0:T(8,128)(2,1)}, u32[]{:S(2)}) %copy-start.3) | copy-done | bytes 131096
  23.6 0.8 %copy-done.4 = bf16[1,32,1024]{2,1,0:T(8,128)(2,1)S(1)} copy-done((bf16[1,32,1024]{2,1,0:T(8,128)(2,1)S(1)}, bf16[1,32,1024]{2,1,0:T(8,128)(2,1)}, u32[]{:S(2)}) %copy-start.4) | copy-done | bytes 65560
  24.4 0.7 copy-done.5
  25.1 2.5 %attend.1 = (bf16[32,1152]{1,0:T(8,128)(2,1)S(1)}, bf16[32,1152]{1,0:T(8,128)(2,1)S(1)}, bf16[32,1152]{1,0:T(8,128)(2,1)S(1)}, bf16[32,1152]{1,0:T(8,128)(2,1)S(1)}) custom-call(s32[2]{0:T(128)S(1)} %pad_add_fusion.refs_0_.place, s32[8,4]{1,0:T(8,128)S(1)} %copy.9.refs_1_, s32[8]{0:T(128)S(1)} %copy-done.5, s32[2,1]{1,0:T(2,128)S(1)} %copy.10.refs_3_, ...), custom_call_target="tpu_custom_call" | custom-call | tf_op jit(solution)/shard_map/attend/pallas_call | solution.py:215
  27.6 1.3 %collective-permute-start.6 = (bf16[32,1152]{1,0:T(8,128)(2,1)S(1)}, bf16[32,1152]{1,0:T(8,128)(2,1)S(1)}, u32[]{:S(2)}, u32[]{:S(2)}) collective-permute-start(bf16[32,1152]{1,0:T(8,128)(2,1)S(1)} %get-tuple-element.14), channel_id=1, source_target_pairs={{0,2},{1,3},{2,0},{3,1},{4,6},{5,7},{6,4},{7,5},{8,10},{9,11},{10,... | collective-permute-start | bytes 221192 | tf_op jit(solution)/shard_map/ppermute | solution.py:22
  28.9 1.8 %collective-permute-start.7 = (bf16[32,1152]{1,0:T(8,128)(2,1)S(1)}, bf16[32,1152]{1,0:T(8,128)(2,1)S(1)}, u32[]{:S(2)}, u32[]{:S(2)}) collective-permute-start(bf16[32,1152]{1,0:T(8,128)(2,1)S(1)} %get-tuple-element.15), channel_id=1, source_target_pairs={{0,4},{1,5},{2,6},{3,7},{4,0},{5,1},{6,2},{7,3},{8,12},{9,13},{10,... | collective-permute-start | bytes 221192 | tf_op jit(solution)/shard_map/ppermute | solution.py:22
  30.7 1.4 %collective-permute-start.8 = (bf16[32,1152]{1,0:T(8,128)(2,1)S(1)}, bf16[32,1152]{1,0:T(8,128)(2,1)S(1)}, u32[]{:S(2)}, u32[]{:S(2)}) collective-permute-start(bf16[32,1152]{1,0:T(8,128)(2,1)S(1)} %get-tuple-element.16), channel_id=1, source_target_pairs={{0,6},{1,7},{2,4},{3,5},{4,2},{5,3},{6,0},{7,1},{8,14},{9,15},{10,... | collective-permute-start | bytes 221192 | tf_op jit(solution)/shard_map/ppermute | solution.py:22
  32.4 4.9 %collective-permute-done.7.refs_2_ = bf16[32,1152]{1,0:T(8,128)(2,1)S(1)} collective-permute-done((bf16[32,1152]{1,0:T(8,128)(2,1)S(1)}, bf16[32,1152]{1,0:T(8,128)(2,1)S(1)}, u32[]{:S(2)}, u32[]{:S(2)}) %collective-permute-start.7) | collective-permute-done | bytes 73760 | tf_op jit(solution)/shard_map/ppermute | solution.py:22
  37.4 5.8 %copy-done = bf16[1,1024,8192]{2,1,0:T(8,128)(2,1)S(1)} copy-done((bf16[1,1024,8192]{2,1,0:T(8,128)(2,1)S(1)}, bf16[1,1024,8192]{2,1,0:T(8,128)(2,1)}, u32[]{:S(2)}) %copy-start) | copy-done | bytes 16777240
  43.1 3.3 %project_away.1 = (bf16[4,32,1024]{2,1,0:T(8,128)(2,1)S(1)}, bf16[32,1024]{1,0:T(8,128)(2,1)S(1)}) custom-call(s32[2]{0:T(128)S(1)} %pad_add_fusion.refs_0_.place, bf16[32,1152]{1,0:T(8,128)(2,1)S(1)} %get-tuple-element.13.refs_0_, bf16[32,1152]{1,0:T(8,128)(2,1)S(1)} %collective-permute-done.6.refs_1_, bf16[32,1152]{1,0:T(8,128)(2,1)S(1)} %collective-permute-done.7.refs_2_, ...), custom_call_target="tpu_custom_call" | custom-call | tf_op jit(solution)/shard_map/project_away/pallas_call | solution.py:241
  46.5 1.5 %collective-permute-done.9.other = bf16[4,32,1024]{2,1,0:T(8,128)(2,1)S(1)} collective-permute-done((bf16[4,32,1024]{2,1,0:T(8,128)(2,1)S(1)}, bf16[4,32,1024]{2,1,0:T(8,128)(2,1)S(1)}, u32[]{:S(2)}, u32[]{:S(2)}) %collective-permute-start.9) | collective-permute-done | bytes 262176 | tf_op jit(solution)/shard_map/ppermute | solution.py:22
  48.0 5.8 %copy-done.1 = bf16[1,1024,8192]{2,1,0:T(8,128)(2,1)S(1)} copy-done((bf16[1,1024,8192]{2,1,0:T(8,128)(2,1)S(1)}, bf16[1,1024,8192]{2,1,0:T(8,128)(2,1)}, u32[]{:S(2)}) %copy-start.1) | copy-done | bytes 16777240
  53.8 3.0 %project_home.1 = (bf16[4,32,1024]{2,1,0:T(8,128)(2,1)S(1)}, f32[32,1024]{1,0:T(8,128)S(1)}) custom-call(s32[2]{0:T(128)S(1)} %pad_add_fusion.refs_0_.place, bf16[32,1024]{1,0:T(8,128)(2,1)S(1)} %get-tuple-element.17.attended, bf16[4,32,1024]{2,1,0:T(8,128)(2,1)S(1)} %collective-permute-done.9.other, bf16[1,1024,8192]{2,1,0:T(8,128)(2,1)S(1)} %copy-done.1), custom_call_target="tpu_custom_call" | custom-call | tf_op jit(solution)/shard_map/project_home/pallas_call | solution.py:258
  56.8 1.4 %collective-permute-start.10 = (bf16[32,1024]{1,0:T(8,128)(2,1)S(1)}, bf16[32,1024]{1,0:T(8,128)(2,1)S(1)}, u32[]{:S(2)}, u32[]{:S(2)}) collective-permute-start(bf16[32,1024]{1,0:T(8,128)(2,1)S(1)} %get-tuple-element.32), channel_id=1, source_target_pairs={{0,2},{1,3},{2,0},{3,1},{4,6},{5,7},{6,4},{7,5},{8,10},{9,11},{10,... | collective-permute-start | bytes 196616 | tf_op jit(solution)/shard_map/ppermute | solution.py:22
  58.3 1.9 %collective-permute-start.12 = (bf16[32,1024]{1,0:T(8,128)(2,1)S(1)}, bf16[32,1024]{1,0:T(8,128)(2,1)S(1)}, u32[]{:S(2)}, u32[]{:S(2)}) collective-permute-start(bf16[32,1024]{1,0:T(8,128)(2,1)S(1)} %get-tuple-element.33), channel_id=1, source_target_pairs={{0,6},{1,7},{2,4},{3,5},{4,2},{5,3},{6,0},{7,1},{8,14},{9,15},{10,... | collective-permute-start | bytes 196616 | tf_op jit(solution)/shard_map/ppermute | solution.py:22
  60.4 0.8 %collective-permute-done.10 = bf16[32,1024]{1,0:T(8,128)(2,1)S(1)} collective-permute-done((bf16[32,1024]{1,0:T(8,128)(2,1)S(1)}, bf16[32,1024]{1,0:T(8,128)(2,1)S(1)}, u32[]{:S(2)}, u32[]{:S(2)}) %collective-permute-start.10) | collective-permute-done | bytes 65568 | tf_op jit(solution)/shard_map/ppermute | solution.py:22
  61.2 3.5 %collective-permute-done.12 = bf16[32,1024]{1,0:T(8,128)(2,1)S(1)} collective-permute-done((bf16[32,1024]{1,0:T(8,128)(2,1)S(1)}, bf16[32,1024]{1,0:T(8,128)(2,1)S(1)}, u32[]{:S(2)}, u32[]{:S(2)}) %collective-permute-start.12) | collective-permute-done | bytes 65568 | tf_op jit(solution)/shard_map/ppermute | solution.py:22
  64.7 2.1 %collective-permute-done.11 = bf16[32,1024]{1,0:T(8,128)(2,1)S(1)} collective-permute-done((bf16[32,1024]{1,0:T(8,128)(2,1)S(1)}, bf16[32,1024]{1,0:T(8,128)(2,1)S(1)}, u32[]{:S(2)}, u32[]{:S(2)}) %collective-permute-start.11) | collective-permute-done | bytes 65568 | tf_op jit(solution)/shard_map/ppermute | solution.py:22
  66.9 1.6 %collective-permute-start.13 = (bf16[32,1024]{1,0:T(8,128)(2,1)S(1)}, bf16[32,1024]{1,0:T(8,128)(2,1)S(1)}, u32[]{:S(2)}, u32[]{:S(2)}) collective-permute-start(bf16[32,1024]{1,0:T(8,128)(2,1)S(1)} %add_convert_fusion.1), channel_id=1, source_target_pairs={{0,16},{16,0},{1,17},{17,1},{2,18},{18,2},{3,19},{19,3},{4,20},{20... | collective-permute-start | bytes 196616 | tf_op jit(solution)/shard_map/ppermute | solution.py:281
  68.5 2.7 %collective-permute-done.13 = bf16[32,1024]{1,0:T(8,128)(2,1)S(1)} collective-permute-done((bf16[32,1024]{1,0:T(8,128)(2,1)S(1)}, bf16[32,1024]{1,0:T(8,128)(2,1)S(1)}, u32[]{:S(2)}, u32[]{:S(2)}) %collective-permute-start.13) | collective-permute-done | bytes 65568 | tf_op jit(solution)/shard_map/ppermute | solution.py:281
  71.2 0.7 fusion.1
  (21 shorter events, 1.3 us)
Async XLA Ops:
  0.0 21.4 %collective-permute-start.3 = (bf16[256,2048]{1,0:T(8,128)(2,1)}, bf16[256,2048]{1,0:T(8,128)(2,1)S(1)}, u32[]{:S(2)}, u32[]{:S(2)}) collective-permute-start(bf16[256,2048]{1,0:T(8,128)(2,1)} %bitcast.18), channel_id=1, source_target_pairs={{0,1},{1,0},{2,3},{3,2},{4,5},{5,4},{6,7},{7,6},{8,9},{9,8},{10,11... | collective-permute-start | bytes 3145736 | tf_op jit(solution)/shard_map/ppermute | solution.py:22
  4.5 6.7 %collective-permute-start.4 = (bf16[32,2048]{1,0:T(8,128)(2,1)S(1)}, bf16[32,2048]{1,0:T(8,128)(2,1)S(1)}, u32[]{:S(2)}, u32[]{:S(2)}) collective-permute-start(bf16[32,2048]{1,0:T(8,128)(2,1)S(1)} %dynamic-slice_bitcast_fusion), channel_id=1, source_target_pairs={{0,8},{8,0},{1,9},{9,1},{2,10},{10,2},{3,11},{11,3},{4,12},{12,4},... | collective-permute-start | bytes 393224 | tf_op jit(solution)/shard_map/ppermute | solution.py:204
  11.2 10.2 %collective-permute-start.5 = (bf16[32,2048]{1,0:T(8,128)(2,1)S(1)}, bf16[32,2048]{1,0:T(8,128)(2,1)S(1)}, u32[]{:S(2)}, u32[]{:S(2)}) collective-permute-start(bf16[32,2048]{1,0:T(8,128)(2,1)S(1)} %collective-permute-done.4.refs_10_), channel_id=1, source_target_pairs={{0,1},{1,0},{2,3},{3,2},{4,5},{5,4},{6,7},{7,6},{8,9},{9,8},{10,11... | collective-permute-start | bytes 393224 | tf_op jit(solution)/shard_map/ppermute | solution.py:22
  11.2 7.0 %collective-permute-start.2 = (bf16[32,1024]{1,0:T(8,128)(2,1)}, bf16[32,1024]{1,0:T(8,128)(2,1)S(1)}, u32[]{:S(2)}, u32[]{:S(2)}) collective-permute-start(bf16[32,1024]{1,0:T(8,128)(2,1)} %bitcast.21), channel_id=1, source_target_pairs={{0,6},{1,7},{2,4},{3,5},{4,2},{5,3},{6,0},{7,1},{8,14},{9,15},{10,... | collective-permute-start | bytes 196616 | tf_op jit(solution)/shard_map/ppermute | solution.py:22
  15.1 6.3 %collective-permute-start.1 = (bf16[32,1024]{1,0:T(8,128)(2,1)}, bf16[32,1024]{1,0:T(8,128)(2,1)S(1)}, u32[]{:S(2)}, u32[]{:S(2)}) collective-permute-start(bf16[32,1024]{1,0:T(8,128)(2,1)} %bitcast.22), channel_id=1, source_target_pairs={{0,4},{1,5},{2,6},{3,7},{4,0},{5,1},{6,2},{7,3},{8,12},{9,13},{10,... | collective-permute-start | bytes 196616 | tf_op jit(solution)/shard_map/ppermute | solution.py:22
  15.1 6.3 %collective-permute-start = (bf16[32,1024]{1,0:T(8,128)(2,1)}, bf16[32,1024]{1,0:T(8,128)(2,1)S(1)}, u32[]{:S(2)}, u32[]{:S(2)}) collective-permute-start(bf16[32,1024]{1,0:T(8,128)(2,1)} %bitcast.23), channel_id=1, source_target_pairs={{0,2},{1,3},{2,0},{3,1},{4,6},{5,7},{6,4},{7,5},{8,10},{9,11},{10,... | collective-permute-start | bytes 196616 | tf_op jit(solution)/shard_map/ppermute | solution.py:22
  21.4 1.2 %copy-start.2 = (bf16[1,8,32,2048]{3,2,1,0:T(8,128)(2,1)S(1)}, bf16[1,8,32,2048]{3,2,1,0:T(8,128)(2,1)}, u32[]{:S(2)}) copy-start(bf16[1,8,32,2048]{3,2,1,0:T(8,128)(2,1)} %param.11) | copy-start | bytes 3145732
  22.7 0.9 %copy-start.3 = (bf16[1,32,2048]{2,1,0:T(8,128)(2,1)S(1)}, bf16[1,32,2048]{2,1,0:T(8,128)(2,1)}, u32[]{:S(2)}) copy-start(bf16[1,32,2048]{2,1,0:T(8,128)(2,1)} %param.10) | copy-start | bytes 393220
  23.6 0.8 %copy-start.4 = (bf16[1,32,1024]{2,1,0:T(8,128)(2,1)S(1)}, bf16[1,32,1024]{2,1,0:T(8,128)(2,1)}, u32[]{:S(2)}) copy-start(bf16[1,32,1024]{2,1,0:T(8,128)(2,1)} %param.9) | copy-start | bytes 196612
  24.4 0.7 copy-start.5
  27.6 4.8 %collective-permute-start.6 = (bf16[32,1152]{1,0:T(8,128)(2,1)S(1)}, bf16[32,1152]{1,0:T(8,128)(2,1)S(1)}, u32[]{:S(2)}, u32[]{:S(2)}) collective-permute-start(bf16[32,1152]{1,0:T(8,128)(2,1)S(1)} %get-tuple-element.14), channel_id=1, source_target_pairs={{0,2},{1,3},{2,0},{3,1},{4,6},{5,7},{6,4},{7,5},{8,10},{9,11},{10,... | collective-permute-start | bytes 221192 | tf_op jit(solution)/shard_map/ppermute | solution.py:22
  28.9 8.5 %collective-permute-start.7 = (bf16[32,1152]{1,0:T(8,128)(2,1)S(1)}, bf16[32,1152]{1,0:T(8,128)(2,1)S(1)}, u32[]{:S(2)}, u32[]{:S(2)}) collective-permute-start(bf16[32,1152]{1,0:T(8,128)(2,1)S(1)} %get-tuple-element.15), channel_id=1, source_target_pairs={{0,4},{1,5},{2,6},{3,7},{4,0},{5,1},{6,2},{7,3},{8,12},{9,13},{10,... | collective-permute-start | bytes 221192 | tf_op jit(solution)/shard_map/ppermute | solution.py:22
  30.7 6.7 %collective-permute-start.8 = (bf16[32,1152]{1,0:T(8,128)(2,1)S(1)}, bf16[32,1152]{1,0:T(8,128)(2,1)S(1)}, u32[]{:S(2)}, u32[]{:S(2)}) collective-permute-start(bf16[32,1152]{1,0:T(8,128)(2,1)S(1)} %get-tuple-element.16), channel_id=1, source_target_pairs={{0,6},{1,7},{2,4},{3,5},{4,2},{5,3},{6,0},{7,1},{8,14},{9,15},{10,... | collective-permute-start | bytes 221192 | tf_op jit(solution)/shard_map/ppermute | solution.py:22
  37.4 5.8 %copy-start = (bf16[1,1024,8192]{2,1,0:T(8,128)(2,1)S(1)}, bf16[1,1024,8192]{2,1,0:T(8,128)(2,1)}, u32[]{:S(2)}) copy-start(bf16[1,1024,8192]{2,1,0:T(8,128)(2,1)} %weight.1) | copy-start | bytes 50331652
  43.1 23.7 %copy-start.6 = (bf16[32,1024]{1,0:T(8,128)(2,1)S(1)}, bf16[32,1024]{1,0:T(8,128)(2,1)}, u32[]{:S(2)}) copy-start(bf16[32,1024]{1,0:T(8,128)(2,1)} %param.8) | copy-start | bytes 196612
  46.5 1.6 %collective-permute-start.9 = (bf16[4,32,1024]{2,1,0:T(8,128)(2,1)S(1)}, bf16[4,32,1024]{2,1,0:T(8,128)(2,1)S(1)}, u32[]{:S(2)}, u32[]{:S(2)}) collective-permute-start(bf16[4,32,1024]{2,1,0:T(8,128)(2,1)S(1)} %get-tuple-element.18), channel_id=1, source_target_pairs={{0,1},{1,0},{2,3},{3,2},{4,5},{5,4},{6,7},{7,6},{8,9},{9,8},{10,11... | collective-permute-start | bytes 786440 | tf_op jit(solution)/shard_map/ppermute | solution.py:22
  48.0 5.8 %copy-start.1 = (bf16[1,1024,8192]{2,1,0:T(8,128)(2,1)S(1)}, bf16[1,1024,8192]{2,1,0:T(8,128)(2,1)}, u32[]{:S(2)}) copy-start(bf16[1,1024,8192]{2,1,0:T(8,128)(2,1)} %weight.1) | copy-start | bytes 50331652
  56.8 4.3 %collective-permute-start.10 = (bf16[32,1024]{1,0:T(8,128)(2,1)S(1)}, bf16[32,1024]{1,0:T(8,128)(2,1)S(1)}, u32[]{:S(2)}, u32[]{:S(2)}) collective-permute-start(bf16[32,1024]{1,0:T(8,128)(2,1)S(1)} %get-tuple-element.32), channel_id=1, source_target_pairs={{0,2},{1,3},{2,0},{3,1},{4,6},{5,7},{6,4},{7,5},{8,10},{9,11},{10,... | collective-permute-start | bytes 196616 | tf_op jit(solution)/shard_map/ppermute | solution.py:22
  58.3 6.5 %collective-permute-start.12 = (bf16[32,1024]{1,0:T(8,128)(2,1)S(1)}, bf16[32,1024]{1,0:T(8,128)(2,1)S(1)}, u32[]{:S(2)}, u32[]{:S(2)}) collective-permute-start(bf16[32,1024]{1,0:T(8,128)(2,1)S(1)} %get-tuple-element.33), channel_id=1, source_target_pairs={{0,6},{1,7},{2,4},{3,5},{4,2},{5,3},{6,0},{7,1},{8,14},{9,15},{10,... | collective-permute-start | bytes 196616 | tf_op jit(solution)/shard_map/ppermute | solution.py:22
  60.1 6.7 %collective-permute-start.11 = (bf16[32,1024]{1,0:T(8,128)(2,1)S(1)}, bf16[32,1024]{1,0:T(8,128)(2,1)S(1)}, u32[]{:S(2)}, u32[]{:S(2)}) collective-permute-start(bf16[32,1024]{1,0:T(8,128)(2,1)S(1)} %get-tuple-element.34), channel_id=1, source_target_pairs={{0,4},{1,5},{2,6},{3,7},{4,0},{5,1},{6,2},{7,3},{8,12},{9,13},{10,... | collective-permute-start | bytes 196616 | tf_op jit(solution)/shard_map/ppermute | solution.py:22
  66.9 4.3 %collective-permute-start.13 = (bf16[32,1024]{1,0:T(8,128)(2,1)S(1)}, bf16[32,1024]{1,0:T(8,128)(2,1)S(1)}, u32[]{:S(2)}, u32[]{:S(2)}) collective-permute-start(bf16[32,1024]{1,0:T(8,128)(2,1)S(1)} %add_convert_fusion.1), channel_id=1, source_target_pairs={{0,16},{16,0},{1,17},{17,1},{2,18},{18,2},{3,19},{19,3},{4,20},{20... | collective-permute-start | bytes 196616 | tf_op jit(solution)/shard_map/ppermute | solution.py:281

commit v2 on v0

v2 whole, which is shorter than its diff:
```python
import functools
import math

import jax
import jax.numpy as jnp
from jax import lax
from jax.experimental import pallas as pl
from jax.experimental.pallas import tpu as pltpu
from jax.sharding import PartitionSpec as P

HEADS = 64
KVH = 8
HD = 128
STEPS = 4
GROUP = HEADS // KVH
MASKED = -1e30
LOG2E = 1.4426950408889634
MEGA = 1024 * 1024


def swapped(value, mask):
    count = lax.axis_size("tensor")
    return lax.ppermute(value, "tensor", [(source, source ^ mask) for source in range(count)])


def in_hbm(value):
    return pltpu.with_memory_space_constraint(value, pltpu.HBM)


def weight_copies(weight, out, semaphores, masks):
    rank = lax.axis_index("tensor")
    chunk = out.shape[2]
    copies = []
    for at, mask in enumerate(masks):
        start = pl.multiple_of((rank ^ mask) * chunk, chunk)
        copies.append(
            pltpu.make_async_copy(
                weight.at[0, :, pl.ds(start, chunk)], out.at[at], semaphores.at[at]
            )
        )
    return copies


def pick_kernel(capacity, moves_hbm, pages, *refs):
    outputs, (moves, moves_semaphore, semaphores) = refs[:-3], refs[-3:]
    moves_copy = pltpu.make_async_copy(moves_hbm, moves, moves_semaphore)
    moves_copy.start()
    moves_copy.wait()
    tensor_count, inst_count = lax.axis_size("tensor"), lax.axis_size("inst")
    per = max(1, tensor_count // KVH)
    side = lax.axis_index("tensor") // per % 2
    copies = []
    for shift in range(1, inst_count):
        target = lax.axis_index("inst") + shift
        target = jnp.where(target >= inst_count, target - inst_count, target)
        for slot in range(capacity):
            page = moves[target * capacity + slot]
            for other in range(2):
                out = outputs[2 * (shift - 1) + other]
                for pair in range(KVH // 2):
                    head = 2 * pair + (side if other == 0 else 1 - side)
                    start = pl.multiple_of(head * (2 * HD), 2 * HD)
                    copies.append(
                        pltpu.make_async_copy(
                            pages.at[page, :, pl.ds(start, 2 * HD)],
                            out.at[slot, :, 2 * HD * pair : 2 * HD * (pair + 1)],
                            semaphores.at[len(copies)],
                        )
                    )
    for copy in copies:
        copy.start()
    for copy in copies:
        copy.wait()


def packed_level(level, lane, heads_per):
    top = level.astype(jnp.bfloat16).astype(jnp.float32)
    rest = level - top
    middle = rest.astype(jnp.bfloat16).astype(jnp.float32)
    level = jnp.where(lane < heads_per, top, jnp.where(lane < 2 * heads_per, middle, rest - middle))
    return level.astype(jnp.bfloat16)


def count_kernel(shape, weight_masks, table_hbm, lengths_hbm, moves_hbm, weight, *refs):
    use_out, weight_out, table, lengths, moves, semaphores, weight_semaphores = refs
    pages, page_tokens, capacity = shape
    tensor_count, inst_count = lax.axis_size("tensor"), lax.axis_size("inst")
    tensor_rank, inst_rank = lax.axis_index("tensor"), lax.axis_index("inst")
    per = max(1, tensor_count // KVH)
    partner = tensor_rank ^ per
    rows, columns = use_out.shape
    slots, requests = table.shape
    page_size = page_tokens * tensor_count
    copies = [
        pltpu.make_async_copy(source, target, semaphores.at[at])
        for at, (source, target) in enumerate(
            ((table_hbm, table), (lengths_hbm, lengths), (moves_hbm, moves))
        )
    ]
    load_copies = weight_copies(weight, weight_out, weight_semaphores, weight_masks)
    for copy in copies + load_copies:
        copy.start()
    for copy in copies:
        copy.wait()

    row = lax.broadcasted_iota(jnp.int32, (rows, 1), 0)
    row_request, row_step = row // STEPS, row % STEPS
    row_length = jnp.zeros((rows, 1), jnp.int32)
    row_pages = [jnp.zeros((rows, 1), jnp.int32) for _ in range(slots)]
    for request in range(requests):
        here = row_request == request
        row_length = jnp.where(here, lengths[request], row_length)
        for slot in range(slots):
            page = table[slot, request]
            arrived = page - pages
            for own in range(capacity):
                page = jnp.where(
                    arrived == inst_rank * capacity + own, moves[inst_rank * capacity + own], page
                )
            row_pages[slot] = jnp.where(here, page, row_pages[slot])

    column = lax.broadcasted_iota(jnp.int32, (1, columns), 1)
    own_columns = pages * page_tokens
    block_columns = capacity * page_tokens
    moved = column - 2 * own_columns
    block = moved // block_columns
    source = inst_rank - block // 2 - 1
    source = jnp.where(source < 0, source + inst_count, source)
    resident = moved < 0
    page = jnp.where(
        resident,
        column % own_columns // page_tokens,
        pages + source * capacity + moved // page_tokens % capacity,
    )
    side = jnp.where(resident, column // own_columns, block % 2)
    token = jnp.where(side == 0, tensor_rank, partner) * page_tokens + column % page_tokens
    use = jnp.zeros((rows, columns), jnp.float32)
    for slot in range(slots):
        live = (row_pages[slot] == page) & (token + slot * page_size < row_length)
        use = use + jnp.where(live, 1.0, 0.0)
    fresh = column - (columns - rows)
    fresh_live = (fresh // STEPS == row_request) & (fresh % STEPS <= row_step)
    fresh_live = fresh_live & ((tensor_rank == 0) | (tensor_rank == per))
    use_out[...] = jnp.where(fresh >= 0, jnp.where(fresh_live, 1.0, 0.0), use)
    for copy in load_copies:
        copy.wait()


def attend_kernel(masks, weight_masks, piece_count, *refs):
    tensor_count, tensor_rank = lax.axis_size("tensor"), lax.axis_index("tensor")
    use_ref, refs = refs[0], refs[1:]
    queries, refs = refs[: len(masks)], refs[len(masks) :]
    pieces, weight, refs = refs[:piece_count], refs[piece_count], refs[piece_count + 1 :]
    parts, refs = refs[: len(masks)], refs[len(masks) :]
    weight_out, own_queries, tokens, query_semaphore, semaphores, weight_semaphores = refs
    per = max(1, tensor_count // KVH)
    rows, columns = use_ref.shape
    heads_per = HEADS // tensor_count
    groups = len(masks) // per

    copies = []
    for group in range(groups):
        kv_head = (tensor_rank ^ masks[group * per]) // per
        filled = 0
        for at, piece in enumerate(pieces):
            halved = piece.shape[1] < KVH * 2 * HD
            start = pl.multiple_of((kv_head // 2 if halved else kv_head) * (2 * HD), 2 * HD)
            copies.append(
                pltpu.make_async_copy(
                    piece.at[:, pl.ds(start, 2 * HD)],
                    tokens.at[group, filled : filled + piece.shape[0], :],
                    semaphores.at[group, at],
                )
            )
            filled += piece.shape[0]
    load_copies = weight_copies(weight, weight_out, weight_semaphores, weight_masks)
    if masks[0] == 0:
        query_copy = pltpu.make_async_copy(queries[0], own_queries, query_semaphore)
        query_copy.start()
    for copy in copies + load_copies:
        copy.start()
    if masks[0] == 0:
        query_copy.wait()

    use = use_ref[...][None]
    lane = lax.broadcasted_iota(jnp.int32, (rows, HD), 1)
    factor = LOG2E / math.sqrt(HD)
    for group in range(groups):
        for copy in copies[group * piece_count : (group + 1) * piece_count]:
            copy.wait()
        blocks = []
        for at in range(group * per, group * per + per):
            block = own_queries if masks[at] == 0 else queries[at]
            blocks += [block[:, head * HD : (head + 1) * HD] for head in range(heads_per)]
        stacked = jnp.concatenate(blocks, axis=0)
        scores = lax.dot_general(
            stacked,
            tokens[group, :, :HD],
            (((1,), (1,)), ((), ())),
            preferred_element_type=jnp.float32,
        )
        scores = scores.reshape(GROUP, rows, columns)
        scores = jnp.where(use > 0.0, scores, MASKED)
        row_max = jnp.max(scores, axis=-1, keepdims=True)
        expo = jnp.exp2((scores - row_max) * factor) * use
        total = jnp.sum(expo, axis=-1, keepdims=True)
        weighted = jnp.dot(
            expo.astype(jnp.bfloat16).reshape(GROUP * rows, columns),
            tokens[group, :, HD:],
            preferred_element_type=jnp.float32,
        )
        weighted = (weighted.reshape(GROUP, rows, HD) / total).astype(jnp.bfloat16)
        level = row_max * factor + jnp.log2(total)
        for low in range(per):
            out = parts[group * per + low]
            levels = jnp.zeros((rows, HD), jnp.float32)
            for head in range(heads_per):
                at = low * heads_per + head
                out[:, head * HD : (head + 1) * HD] = weighted[at]
                levels = jnp.where(lane % heads_per == head, level[at], levels)
            out[:, heads_per * HD :] = packed_level(levels, lane, heads_per)
    for copy in load_copies:
        copy.wait()


def combined(parts, heads_per):
    levels = []
    for part in parts:
        level = part[:, heads_per * HD :].astype(jnp.float32)
        levels.append(
            level
            + pltpu.roll(level, HD - heads_per, 1)
            + pltpu.roll(level, HD - 2 * heads_per, 1)
        )
    top = functools.reduce(jnp.maximum, levels)
    shares = [jnp.exp2(level - top) for level in levels]
    total = sum(shares[1:], shares[0])
    shares = [share / total for share in shares]
    heads = []
    for head in range(heads_per):
        terms = [
            share[:, head : head + 1] * part[:, head * HD : (head + 1) * HD].astype(jnp.float32)
            for share, part in zip(shares, parts)
        ]
        heads.append(sum(terms[1:], terms[0]).astype(jnp.bfloat16))
    return jnp.concatenate(heads, axis=1)


def project(rows, weights, out):
    at = 0
    for weight in weights:
        for block in range(weight.shape[0]):
            product = jnp.dot(rows, weight[block], preferred_element_type=jnp.float32)
            out[at] = product.astype(out.dtype)
            at += 1


def project_away_kernel(heads_per, part_count, *refs):
    parts, (*weights, out, attended) = refs[:part_count], refs[part_count:]
    rows = combined(parts, heads_per)
    attended[...] = rows
    project(rows, weights, out)


def project_home_kernel(attended, *refs):
    project(attended[...], refs[:-1], refs[-1])


def add_kernel(home, sibling, *outputs):
    for at, out in enumerate(outputs):
        out[...] = (home[at + 1] + sibling[at + 1].astype(jnp.float32)).astype(out.dtype)


def local(hidden_in, queries, new_kv, kv_pages, out_weight, move_pages, page_table, lengths):
    tensor_count = lax.axis_size("tensor")
    inst_count = lax.axis_size("inst")
    section_rank = lax.axis_index("section")
    per = max(1, tensor_count // KVH)
    heads_per = HEADS // tensor_count
    requests, slots = page_table.shape
    rows = requests * STEPS
    own_pages = kv_pages[0]
    pages, page_tokens, width = own_pages.shape
    capacity = move_pages.shape[2]
    moves = in_hbm(move_pages.reshape(-1))
    depth, features = out_weight.shape[1:]
    chunk = features // tensor_count
    half = tensor_count // 2
    vmem = pl.BlockSpec(memory_space=pltpu.VMEM)
    hbm = pl.BlockSpec(memory_space=pltpu.HBM)
    anywhere = pl.BlockSpec(memory_space=pl.ANY)
    peers = [mask for mask in range(tensor_count) if mask & per == 0]

    if len(peers) == 4:
        peers = [0, 4, 2, 6]
    home_masks = [2 * mask for mask in range(half)]
    if half == 4:
        home_masks = [0, 4, 2, 6]
    away_masks = [mask ^ 1 for mask in home_masks]
    early = half // 4
    weight = in_hbm(out_weight)

    def weight_shape(count):
        return pltpu.VMEM((count, depth, chunk), jnp.bfloat16)

    own_queries = queries[0]
    all_queries = {mask: swapped(own_queries, mask) for mask in peers[1:]}
    all_queries[0] = in_hbm(own_queries)
    own_flat = own_pages.reshape(pages * page_tokens, width)
    partner_flat = swapped(own_flat, per)
    leaving = pl.pallas_call(
        functools.partial(pick_kernel, capacity),
        out_shape=[jax.ShapeDtypeStruct((capacity, page_tokens, width // 2), jnp.bfloat16)]
        * (2 * (inst_count - 1)),
        in_specs=[hbm] * 2,
        out_specs=[vmem] * (2 * (inst_count - 1)),
        scratch_shapes=[
            pltpu.SMEM(moves.shape, jnp.int32),
            pltpu.SemaphoreType.DMA,
            pltpu.SemaphoreType.DMA(((inst_count - 1) * capacity * KVH,)),
        ],
        compiler_params=pltpu.CompilerParams(vmem_limit_bytes=2 * MEGA),
        name="pick",
    )(moves, in_hbm(own_pages))
    arrived = []
    for shift in range(1, inst_count):
        for other in range(2):
            pairs = [
                (
                    inst * tensor_count + rank,
                    (inst + shift) % inst_count * tensor_count + (rank ^ (per * other)),
                )
                for inst in range(inst_count)
                for rank in range(tensor_count)
            ]
            sent = leaving[2 * (shift - 1) + other].reshape(capacity * page_tokens, width // 2)
            arrived.append(lax.ppermute(sent, ("inst", "tensor"), pairs))
    if page_tokens * capacity % 16:
        arrived = [jnp.concatenate(arrived, axis=0)]
    pieces = [in_hbm(own_flat), partner_flat, *arrived, in_hbm(new_kv[0])]
    piece_specs = [hbm, anywhere, *[anywhere] * len(arrived), hbm]
    columns = sum(piece.shape[0] for piece in pieces)

    use, away_weight = pl.pallas_call(
        functools.partial(count_kernel, (pages, page_tokens, capacity), away_masks),
        out_shape=[jax.ShapeDtypeStruct((rows, columns), jnp.float32), weight_shape(half)],
        in_specs=[hbm] * 4,
        out_specs=[vmem] * 2,
        scratch_shapes=[
            pltpu.SMEM((slots, requests), jnp.int32),
            pltpu.SMEM((requests,), jnp.int32),
            pltpu.SMEM(moves.shape, jnp.int32),
            pltpu.SemaphoreType.DMA((3,)),
            pltpu.SemaphoreType.DMA((half,)),
        ],
        compiler_params=pltpu.CompilerParams(vmem_limit_bytes=2 * MEGA),
        name="count_uses",
    )(in_hbm(page_table.T), in_hbm(lengths), moves, weight)

    part_shape = jax.ShapeDtypeStruct((rows, heads_per * HD + HD), jnp.bfloat16)

    def attend(masks, weight_masks):
        groups = len(masks) // per
        *parts, moved_weight = pl.pallas_call(
            functools.partial(attend_kernel, masks, weight_masks, len(pieces)),
            out_shape=[part_shape] * len(masks)
            + [weight_shape(len(weight_masks))],
            in_specs=[vmem] + [vmem if mask else hbm for mask in masks] + piece_specs + [hbm],
            out_specs=[vmem] * (len(masks) + 1),
            scratch_shapes=[
                pltpu.VMEM((rows, heads_per * HD), jnp.bfloat16),
                pltpu.VMEM((groups, columns, 2 * HD), jnp.bfloat16),
                pltpu.SemaphoreType.DMA,
                pltpu.SemaphoreType.DMA((groups, len(pieces))),
                pltpu.SemaphoreType.DMA((len(weight_masks),)),
            ],
            compiler_params=pltpu.CompilerParams(vmem_limit_bytes=8 * MEGA),
            name="attend",
        )(use, *[all_queries[mask] for mask in masks], *pieces, weight)
        return dict(zip(masks, parts)), moved_weight

    parts, home_first = attend(peers[per:], home_masks[:early])
    received = {mask: swapped(part, mask) for mask, part in parts.items()}
    parts, home_second = attend(peers[:per], home_masks[early:])
    received.update({mask: swapped(part, mask) for mask, part in parts.items() if mask})
    received = [parts[0]] + [received[mask] for mask in peers[1:]]

    project_params = pltpu.CompilerParams(vmem_limit_bytes=4 * MEGA)
    away, attended = pl.pallas_call(
        functools.partial(project_away_kernel, heads_per, half),
        in_specs=[vmem] * (half + 1),
        out_specs=[vmem] * 2,
        out_shape=[
            jax.ShapeDtypeStruct((half, rows, chunk), jnp.bfloat16),
            jax.ShapeDtypeStruct((rows, depth), jnp.bfloat16),
        ],
        compiler_params=project_params,
        name="project_away",
    )(*received, away_weight)
    sibling = swapped(away, 1)
    home = pl.pallas_call(
        project_home_kernel,
        in_specs=[vmem] * 3,
        out_specs=vmem,
        out_shape=jax.ShapeDtypeStruct((half, rows, chunk), jnp.float32),
        compiler_params=project_params,
        name="project_home",
    )(attended, home_first, home_second)
    sums = pl.pallas_call(
        add_kernel,
        in_specs=[vmem] * 2,
        out_specs=[vmem] * (half - 1),
        out_shape=[jax.ShapeDtypeStruct((rows, chunk), jnp.bfloat16)] * (half - 1),
        compiler_params=pltpu.CompilerParams(vmem_limit_bytes=2 * MEGA),
        name="add_sibling",
    )(home, sibling)
    projected = home[0] + sibling[0].astype(jnp.float32)
    for mask, total in zip(home_masks[1:], sums):
        projected = projected + swapped(total, mask).astype(jnp.float32)
    after_first = (hidden_in.astype(jnp.float32) + projected).astype(jnp.bfloat16)
    handed_over = lax.ppermute(after_first, "section", [(0, 1), (1, 0)])
    after_second = (handed_over.astype(jnp.float32) + projected).astype(jnp.bfloat16)
    result = jnp.where(section_rank == 0, after_first, after_second)
    return result[None]


def solution(mesh):
    return jax.shard_map(
        local,
        mesh=mesh,
        in_specs=(
            P("inst", "tensor"),
            P("section", "inst", "tensor"),
            P("section", "inst", None),
            P("section", "inst", "tensor", None),
            P("section", "tensor", None),
            P("inst", None, None),
            P("inst", None),
            P("inst"),
        ),
        out_specs=P("section", "inst", "tensor"),
        check_vma=False,
    )
```

time: 150 us -> 44.9 us (0.30)
  waiting for transfers between devices: 61.6 us -> 9.22 us
  local copies, waits for them, and re-layouts: 16.4 us -> 0.01 us
  blocking collectives: 16 us -> 0 us
  Pallas kernels: 0 us -> 14.5 us
  matrix products: 13.7 us -> 0 us
  between operations: 13.7 us -> 0.1 us
  other arithmetic: 8.48 us -> 0.74 us
    reduce_scatter x1 -> x0, waiting for transfers between devices: 30.6 us -> none  [local(): lax.psum_scatter(partial_term.astype(jnp.bfloat16), 'tensor', scatter_dim...]
    all_to_all x4 -> x0, waiting for transfers between devices: 29.1 us -> none  [the longest x1 24.8 us: local(): lax.all_to_all(weighted[None], 'tensor', split_axis=2, concat_axis=0, til...]
    ppermute x1 -> x14, starting transfers between devices: 3.37 us -> 20.2 us  [the longest x11 15.8 us: swapped(): lax.ppermute(value, 'tensor', [(source, source ^ mask) for source in rang...]
    all_gather x1 -> x0, blocking collectives: 16 us -> none  [local(): whole_queries = lax.all_gather(queries[0], 'tensor', axis=1, tiled=True)]
    all_to_all x4 -> x0, starting transfers between devices: 15.8 us -> none  [the longest x1 4.64 us: local(): lax.all_to_all(row_max[None, :, :, None], 'tensor', split_axis=2, concat_...]
    pallas_call x0 -> x7, Pallas kernels: none -> 14.5 us  [the longest x2 6.03 us: attend(): pl.pallas_call(functools.partial(attend_kernel, masks, weight_masks, len(...]
    dot_general x3 -> x0, matrix products: 13.7 us -> none  [the longest x1 9.66 us: local(): jnp.dot(attended, out_weight[0], preferred_element_type=jnp.float32)]
    unnamed x16 -> x2, local copies, waits for them, and re-layouts: 8.85 us -> 0.01 us
  transfers between devices with their start and end apart: 6 -> 14, of which waited for: 5 -> 5; matrix products, arithmetic and copies ran while one was open for 8% -> 0% of each run, Pallas kernels for 0% -> 22%
where the time goes in v2:
time: 44.9 us; the launch traced here: 44.7 us
  starting transfers between devices  20.2 us (45%)
  Pallas kernels  14.5 us (32%)
  waiting for transfers between devices  9.22 us (21%)
  other arithmetic  0.74 us (2%)
    ppermute x11, starting transfers between devices, swapped(): lax.ppermute(value, 'tensor', [(source, source ^ mask) for source in rang...  15.8 us
    ppermute x11, waiting for transfers between devices, swapped(): lax.ppermute(value, 'tensor', [(source, source ^ mask) for source in rang...  6.48 us
    pallas_call x2, Pallas kernels, attend(): pl.pallas_call(functools.partial(attend_kernel, masks, weight_masks, len(...  6.03 us
    pallas_call x1, Pallas kernels, local(): pl.pallas_call(functools.partial(count_kernel, (pages, page_tokens, capac...  3.55 us
    ppermute x2, starting transfers between devices, local(): arrived.append(lax.ppermute(sent, ('inst', 'tensor'), pairs))  2.74 us
    ppermute x1, waiting for transfers between devices, local(): handed_over = lax.ppermute(after_first, 'section', [(0, 1), (1, 0)])  2.74 us
    pallas_call x1, Pallas kernels, local(): pl.pallas_call(functools.partial(project_away_kernel, heads_per, half), i...  1.71 us
    pallas_call x1, Pallas kernels, local(): pl.pallas_call(functools.partial(pick_kernel, capacity), out_shape=[jax.S...  1.59 us
  transfers between devices with their start and end apart: 14, of which 5 were waited for; matrix products, arithmetic and copies ran while one was open for 0% of the time, Pallas kernels for 22%

profile of v2, /device:TPU:0, one launch (start us, length us, event | category | flops | bytes accessed | tf_op | source)
XLA Modules:
  0.0 44.7 jit_solution(2792497678097467829)
XLA Ops:
  0.0 0.5 %collective-permute-start = (bf16[256,2048]{1,0:T(8,128)(2,1)}, bf16[256,2048]{1,0:T(8,128)(2,1)S(1)}, u32[]{:S(2)}, u32[]{:S(2)}) collective-permute-start(bf16[256,2048]{1,0:T(8,128)(2,1)} %bitcast.24), channel_id=1, source_target_pairs={{0,1},{1,0},{2,3},{3,2},{4,5},{5,4},{6,7},{7,6},{8,9},{9,8},{10,11... | collective-permute-start | bytes 3145736 | tf_op jit(solution)/shard_map/ppermute | solution.py:23
  0.5 1.6 %pick.1 = (bf16[1,32,1024]{2,1,0:T(8,128)(2,1)S(1)}, bf16[1,32,1024]{2,1,0:T(8,128)(2,1)S(1)}) custom-call(s32[2]{0:T(128)} %bitcast.34, bf16[8,32,2048]{2,1,0:T(8,128)(2,1)} %bitcast.25), custom_call_target="tpu_custom_call" | custom-call | tf_op jit(solution)/shard_map/pick/pallas_call | solution.py:311
  2.1 2.6 %collective-permute-start.1 = (bf16[32,1024]{1,0:T(8,128)(2,1)S(1)}, bf16[32,1024]{1,0:T(8,128)(2,1)S(1)}, u32[]{:S(2)}, u32[]{:S(2)}) collective-permute-start(bf16[32,1024]{1,0:T(8,128)(2,1)S(1)} %bitcast.23), channel_id=1, source_target_pairs={{0,8},{1,9},{2,10},{3,11},{4,12},{5,13},{6,14},{7,15},{8,0},{9,1},... | collective-permute-start | bytes 196616 | tf_op jit(solution)/shard_map/ppermute | solution.py:337
  4.6 0.2 collective-permute-start.2
  4.8 2.8 %collective-permute-start.3 = (bf16[32,1024]{1,0:T(8,128)(2,1)}, bf16[32,1024]{1,0:T(8,128)(2,1)S(1)}, u32[]{:S(2)}, u32[]{:S(2)}) collective-permute-start(bf16[32,1024]{1,0:T(8,128)(2,1)} %bitcast.30), channel_id=1, source_target_pairs={{0,4},{1,5},{2,6},{3,7},{4,0},{5,1},{6,2},{7,3},{8,12},{9,13},{10,... | collective-permute-start | bytes 196616 | tf_op jit(solution)/shard_map/ppermute | solution.py:23
  7.6 1.6 %collective-permute-start.4 = (bf16[32,1024]{1,0:T(8,128)(2,1)}, bf16[32,1024]{1,0:T(8,128)(2,1)S(1)}, u32[]{:S(2)}, u32[]{:S(2)}) collective-permute-start(bf16[32,1024]{1,0:T(8,128)(2,1)} %bitcast.31), channel_id=1, source_target_pairs={{0,2},{1,3},{2,0},{3,1},{4,6},{5,7},{6,4},{7,5},{8,10},{9,11},{10,... | collective-permute-start | bytes 196616 | tf_op jit(solution)/shard_map/ppermute | solution.py:23
  9.1 0.0 collective-permute-done.1.refs_4_.refs_6_
  9.1 2.1 %collective-permute-start.5 = (bf16[32,1024]{1,0:T(8,128)(2,1)}, bf16[32,1024]{1,0:T(8,128)(2,1)S(1)}, u32[]{:S(2)}, u32[]{:S(2)}) collective-permute-start(bf16[32,1024]{1,0:T(8,128)(2,1)} %bitcast.32), channel_id=1, source_target_pairs={{0,6},{1,7},{2,4},{3,5},{4,2},{5,3},{6,0},{7,1},{8,14},{9,15},{10,... | collective-permute-start | bytes 196616 | tf_op jit(solution)/shard_map/ppermute | solution.py:23
  11.3 3.6 %count_uses.1 = (f32[32,608]{1,0:T(8,128)S(1)}, bf16[4,1024,1024]{2,1,0:T(8,128)(2,1)S(1)}) custom-call(s32[4,8]{1,0:T(4,128)} %bitcast.36, s32[8]{0:T(128)} %lengths_hbm.1, s32[2]{0:T(128)} %bitcast.35, bf16[1,1024,8192]{2,1,0:T(8,128)(2,1)} %refs_9_.1), custom_call_target="tpu_custom_call" | custom-call | tf_op jit(solution)/shard_map/count_uses/pallas_call | solution.py:344
  14.8 0.0 collective-permute-done.2.refs_5_.refs_7_
  14.8 0.0 collective-permute-done.3.refs_1_
  14.9 0.6 %collective-permute-done.5.refs_3_ = bf16[32,1024]{1,0:T(8,128)(2,1)S(1)} collective-permute-done((bf16[32,1024]{1,0:T(8,128)(2,1)}, bf16[32,1024]{1,0:T(8,128)(2,1)S(1)}, u32[]{:S(2)}, u32[]{:S(2)}) %collective-permute-start.5) | collective-permute-done | bytes 65568 | tf_op jit(solution)/shard_map/ppermute | solution.py:23
  15.4 0.0 collective-permute-done.refs_3_.refs_5_
  15.4 2.9 %attend.3 = (bf16[32,1152]{1,0:T(8,128)(2,1)S(1)}, bf16[32,1152]{1,0:T(8,128)(2,1)S(1)}, bf16[32,1152]{1,0:T(8,128)(2,1)S(1)}, bf16[1,1024,1024]{2,1,0:T(8,128)(2,1)S(1)}) custom-call(f32[32,608]{1,0:T(8,128)S(1)} %get-tuple-element.20.refs_0_, bf16[32,1024]{1,0:T(8,128)(2,1)S(1)} %collective-permute-done.3.refs_1_, ...), custom_call_target="tpu_custom_call" | custom-call | tf_op jit(solution)/shard_map/attend/pallas_call | solution.py:364
  18.4 1.8 %collective-permute-start.6 = (bf16[32,1152]{1,0:T(8,128)(2,1)S(1)}, bf16[32,1152]{1,0:T(8,128)(2,1)S(1)}, u32[]{:S(2)}, u32[]{:S(2)}) collective-permute-start(bf16[32,1152]{1,0:T(8,128)(2,1)S(1)} %get-tuple-element.24), channel_id=1, source_target_pairs={{0,4},{1,5},{2,6},{3,7},{4,0},{5,1},{6,2},{7,3},{8,12},{9,13},{10,... | collective-permute-start | bytes 221192 | tf_op jit(solution)/shard_map/ppermute | solution.py:23
  20.2 1.0 %collective-permute-start.7 = (bf16[32,1152]{1,0:T(8,128)(2,1)S(1)}, bf16[32,1152]{1,0:T(8,128)(2,1)S(1)}, u32[]{:S(2)}, u32[]{:S(2)}) collective-permute-start(bf16[32,1152]{1,0:T(8,128)(2,1)S(1)} %get-tuple-element.25), channel_id=1, source_target_pairs={{0,2},{1,3},{2,0},{3,1},{4,6},{5,7},{6,4},{7,5},{8,10},{9,11},{10,... | collective-permute-start | bytes 221192 | tf_op jit(solution)/shard_map/ppermute | solution.py:23
  21.2 1.6 %collective-permute-start.8 = (bf16[32,1152]{1,0:T(8,128)(2,1)S(1)}, bf16[32,1152]{1,0:T(8,128)(2,1)S(1)}, u32[]{:S(2)}, u32[]{:S(2)}) collective-permute-start(bf16[32,1152]{1,0:T(8,128)(2,1)S(1)} %get-tuple-element.26), channel_id=1, source_target_pairs={{0,6},{1,7},{2,4},{3,5},{4,2},{5,3},{6,0},{7,1},{8,14},{9,15},{10,... | collective-permute-start | bytes 221192 | tf_op jit(solution)/shard_map/ppermute | solution.py:23
  22.8 3.1 %attend.2 = (bf16[32,1152]{1,0:T(8,128)(2,1)S(1)}, bf16[3,1024,1024]{2,1,0:T(8,128)(2,1)S(1)}) custom-call(f32[32,608]{1,0:T(8,128)S(1)} %get-tuple-element.20.refs_0_, bf16[32,1024]{1,0:T(8,128)(2,1)} %bitcast.33, bf16[256,2048]{1,0:T(8,128)(2,1)} %bitcast.27, bf16[256,2048]{1,0:T(8,128)(2,1)S(1)} %collective-permute-done.refs_3_.refs_5_, ...), custom_call_target="tpu_custom_call" | custom-call | tf_op jit(solution)/shard_map/attend/pallas_call | solution.py:364
  25.9 0.0 collective-permute-done.7.refs_2_
  26.0 1.4 %collective-permute-done.8.refs_3_ = bf16[32,1152]{1,0:T(8,128)(2,1)S(1)} collective-permute-done((bf16[32,1152]{1,0:T(8,128)(2,1)S(1)}, bf16[32,1152]{1,0:T(8,128)(2,1)S(1)}, u32[]{:S(2)}, u32[]{:S(2)}) %collective-permute-start.8) | collective-permute-done | bytes 73760 | tf_op jit(solution)/shard_map/ppermute | solution.py:23
  27.4 1.7 %project_away.1 = (bf16[4,32,1024]{2,1,0:T(8,128)(2,1)S(1)}, bf16[32,1024]{1,0:T(8,128)(2,1)S(1)}) custom-call(bf16[32,1152]{1,0:T(8,128)(2,1)S(1)} %get-tuple-element.23.refs_0_, bf16[32,1152]{1,0:T(8,128)(2,1)S(1)} %collective-permute-done.6.refs_1_, bf16[32,1152]{1,0:T(8,128)(2,1)S(1)} %collective-permute-done.7.refs_2_, ...), custom_call_target="tpu_custom_call" | custom-call | tf_op jit(solution)/shard_map/project_away/pallas_call | solution.py:389
  29.1 0.0 collective-permute-start.9
  29.2 1.5 %project_home.1.home = f32[4,32,1024]{2,1,0:T(8,128)S(1)} custom-call(bf16[32,1024]{1,0:T(8,128)(2,1)S(1)} %get-tuple-element.28.attended, bf16[1,1024,1024]{2,1,0:T(8,128)(2,1)S(1)} %get-tuple-element.29.refs_0_, bf16[3,1024,1024]{2,1,0:T(8,128)(2,1)S(1)} %get-tuple-element.30.refs_1_), custom_call_target="tpu_custom_call" | custom-call | tf_op jit(solution)/shard_map/project_home/pallas_call | solution.py:401
  30.8 1.9 %collective-permute-start.10 = (bf16[32,1024]{1,0:T(8,128)(2,1)S(1)}, bf16[32,1024]{1,0:T(8,128)(2,1)S(1)}, u32[]{:S(2)}, u32[]{:S(2)}) collective-permute-start(bf16[32,1024]{1,0:T(8,128)(2,1)S(1)} %get-tuple-element.32), channel_id=1, source_target_pairs={{0,4},{1,5},{2,6},{3,7},{4,0},{5,1},{6,2},{7,3},{8,12},{9,13},{10,... | collective-permute-start | bytes 196616 | tf_op jit(solution)/shard_map/ppermute | solution.py:23
  32.7 0.7 %collective-permute-start.11 = (bf16[32,1024]{1,0:T(8,128)(2,1)S(1)}, bf16[32,1024]{1,0:T(8,128)(2,1)S(1)}, u32[]{:S(2)}, u32[]{:S(2)}) collective-permute-start(bf16[32,1024]{1,0:T(8,128)(2,1)S(1)} %get-tuple-element.33), channel_id=1, source_target_pairs={{0,2},{1,3},{2,0},{3,1},{4,6},{5,7},{6,4},{7,5},{8,10},{9,11},{10,... | collective-permute-start | bytes 196616 | tf_op jit(solution)/shard_map/ppermute | solution.py:23
  33.4 1.8 %collective-permute-start.12 = (bf16[32,1024]{1,0:T(8,128)(2,1)S(1)}, bf16[32,1024]{1,0:T(8,128)(2,1)S(1)}, u32[]{:S(2)}, u32[]{:S(2)}) collective-permute-start(bf16[32,1024]{1,0:T(8,128)(2,1)S(1)} %get-tuple-element.34), channel_id=1, source_target_pairs={{0,6},{1,7},{2,4},{3,5},{4,2},{5,3},{6,0},{7,1},{8,14},{9,15},{10,... | collective-permute-start | bytes 196616 | tf_op jit(solution)/shard_map/ppermute | solution.py:23
  35.2 1.9 %collective-permute-done.10 = bf16[32,1024]{1,0:T(8,128)(2,1)S(1)} collective-permute-done((bf16[32,1024]{1,0:T(8,128)(2,1)S(1)}, bf16[32,1024]{1,0:T(8,128)(2,1)S(1)}, u32[]{:S(2)}, u32[]{:S(2)}) %collective-permute-start.10) | collective-permute-done | bytes 65568 | tf_op jit(solution)/shard_map/ppermute | solution.py:23
  37.1 2.5 %collective-permute-done.11 = bf16[32,1024]{1,0:T(8,128)(2,1)S(1)} collective-permute-done((bf16[32,1024]{1,0:T(8,128)(2,1)S(1)}, bf16[32,1024]{1,0:T(8,128)(2,1)S(1)}, u32[]{:S(2)}, u32[]{:S(2)}) %collective-permute-start.11) | collective-permute-done | bytes 65568 | tf_op jit(solution)/shard_map/ppermute | solution.py:23
  39.6 0.1 add_convert_fusion.1
  39.7 1.6 %collective-permute-start.13 = (bf16[32,1024]{1,0:T(8,128)(2,1)S(1)}, bf16[32,1024]{1,0:T(8,128)(2,1)S(1)}, u32[]{:S(2)}, u32[]{:S(2)}) collective-permute-start(bf16[32,1024]{1,0:T(8,128)(2,1)S(1)} %add_convert_fusion.1), channel_id=1, source_target_pairs={{0,16},{16,0},{1,17},{17,1},{2,18},{18,2},{3,19},{19,3},{4,20},{20... | collective-permute-start | bytes 196616 | tf_op jit(solution)/shard_map/ppermute | solution.py:421
  41.3 2.7 %collective-permute-done.13 = bf16[32,1024]{1,0:T(8,128)(2,1)S(1)} collective-permute-done((bf16[32,1024]{1,0:T(8,128)(2,1)S(1)}, bf16[32,1024]{1,0:T(8,128)(2,1)S(1)}, u32[]{:S(2)}, u32[]{:S(2)}) %collective-permute-start.13) | collective-permute-done | bytes 65568 | tf_op jit(solution)/shard_map/ppermute | solution.py:421
  44.0 0.7 %fusion.5 = bf16[1,32,1024]{2,1,0:T(8,128)(2,1)} fusion(bf16[32,1024]{1,0:T(8,128)(2,1)S(1)} %add_convert_fusion.1, bf16[32,1024]{1,0:T(8,128)(2,1)S(1)} %collective-permute-done.13, pred[]{:T(512)S(6)} %eq.3, bf16[32,1024]{1,0:T(8,128)(2,1)S(1)} %collective-permute-done.12, bf16[32,1024]{1,0:T(8,128)(2,1)S(1)} %collective-permute-done.11, ...), kind=kLoop, calls=%fused_computation.8 | loop fusion | flops 393216 | bytes 589825 | tf_op jit(solution)/shard_map/broadcast_in_dim | solution.py:424
  (7 shorter events, 0.1 us)
Async XLA Ops:
  0.0 15.4 %collective-permute-start = (bf16[256,2048]{1,0:T(8,128)(2,1)}, bf16[256,2048]{1,0:T(8,128)(2,1)S(1)}, u32[]{:S(2)}, u32[]{:S(2)}) collective-permute-start(bf16[256,2048]{1,0:T(8,128)(2,1)} %bitcast.24), channel_id=1, source_target_pairs={{0,1},{1,0},{2,3},{3,2},{4,5},{5,4},{6,7},{7,6},{8,9},{9,8},{10,11... | collective-permute-start | bytes 3145736 | tf_op jit(solution)/shard_map/ppermute | solution.py:23
  2.1 7.1 %collective-permute-start.1 = (bf16[32,1024]{1,0:T(8,128)(2,1)S(1)}, bf16[32,1024]{1,0:T(8,128)(2,1)S(1)}, u32[]{:S(2)}, u32[]{:S(2)}) collective-permute-start(bf16[32,1024]{1,0:T(8,128)(2,1)S(1)} %bitcast.23), channel_id=1, source_target_pairs={{0,8},{1,9},{2,10},{3,11},{4,12},{5,13},{6,14},{7,15},{8,0},{9,1},... | collective-permute-start | bytes 196616 | tf_op jit(solution)/shard_map/ppermute | solution.py:337
  4.6 10.2 %collective-permute-start.2 = (bf16[32,1024]{1,0:T(8,128)(2,1)S(1)}, bf16[32,1024]{1,0:T(8,128)(2,1)S(1)}, u32[]{:S(2)}, u32[]{:S(2)}) collective-permute-start(bf16[32,1024]{1,0:T(8,128)(2,1)S(1)} %bitcast.22), channel_id=1, source_target_pairs={{0,9},{1,8},{2,11},{3,10},{4,13},{5,12},{6,15},{7,14},{8,1},{9,0},... | collective-permute-start | bytes 196616 | tf_op jit(solution)/shard_map/ppermute | solution.py:337
  4.8 10.0 %collective-permute-start.3 = (bf16[32,1024]{1,0:T(8,128)(2,1)}, bf16[32,1024]{1,0:T(8,128)(2,1)S(1)}, u32[]{:S(2)}, u32[]{:S(2)}) collective-permute-start(bf16[32,1024]{1,0:T(8,128)(2,1)} %bitcast.30), channel_id=1, source_target_pairs={{0,4},{1,5},{2,6},{3,7},{4,0},{5,1},{6,2},{7,3},{8,12},{9,13},{10,... | collective-permute-start | bytes 196616 | tf_op jit(solution)/shard_map/ppermute | solution.py:23
  7.6 7.3 %collective-permute-start.4 = (bf16[32,1024]{1,0:T(8,128)(2,1)}, bf16[32,1024]{1,0:T(8,128)(2,1)S(1)}, u32[]{:S(2)}, u32[]{:S(2)}) collective-permute-start(bf16[32,1024]{1,0:T(8,128)(2,1)} %bitcast.31), channel_id=1, source_target_pairs={{0,2},{1,3},{2,0},{3,1},{4,6},{5,7},{6,4},{7,5},{8,10},{9,11},{10,... | collective-permute-start | bytes 196616 | tf_op jit(solution)/shard_map/ppermute | solution.py:23
  9.1 6.3 %collective-permute-start.5 = (bf16[32,1024]{1,0:T(8,128)(2,1)}, bf16[32,1024]{1,0:T(8,128)(2,1)S(1)}, u32[]{:S(2)}, u32[]{:S(2)}) collective-permute-start(bf16[32,1024]{1,0:T(8,128)(2,1)} %bitcast.32), channel_id=1, source_target_pairs={{0,6},{1,7},{2,4},{3,5},{4,2},{5,3},{6,0},{7,1},{8,14},{9,15},{10,... | collective-permute-start | bytes 196616 | tf_op jit(solution)/shard_map/ppermute | solution.py:23
  18.4 7.5 %collective-permute-start.6 = (bf16[32,1152]{1,0:T(8,128)(2,1)S(1)}, bf16[32,1152]{1,0:T(8,128)(2,1)S(1)}, u32[]{:S(2)}, u32[]{:S(2)}) collective-permute-start(bf16[32,1152]{1,0:T(8,128)(2,1)S(1)} %get-tuple-element.24), channel_id=1, source_target_pairs={{0,4},{1,5},{2,6},{3,7},{4,0},{5,1},{6,2},{7,3},{8,12},{9,13},{10,... | collective-permute-start | bytes 221192 | tf_op jit(solution)/shard_map/ppermute | solution.py:23
  20.2 5.8 %collective-permute-start.7 = (bf16[32,1152]{1,0:T(8,128)(2,1)S(1)}, bf16[32,1152]{1,0:T(8,128)(2,1)S(1)}, u32[]{:S(2)}, u32[]{:S(2)}) collective-permute-start(bf16[32,1152]{1,0:T(8,128)(2,1)S(1)} %get-tuple-element.25), channel_id=1, source_target_pairs={{0,2},{1,3},{2,0},{3,1},{4,6},{5,7},{6,4},{7,5},{8,10},{9,11},{10,... | collective-permute-start | bytes 221192 | tf_op jit(solution)/shard_map/ppermute | solution.py:23
  21.2 6.2 %collective-permute-start.8 = (bf16[32,1152]{1,0:T(8,128)(2,1)S(1)}, bf16[32,1152]{1,0:T(8,128)(2,1)S(1)}, u32[]{:S(2)}, u32[]{:S(2)}) collective-permute-start(bf16[32,1152]{1,0:T(8,128)(2,1)S(1)} %get-tuple-element.26), channel_id=1, source_target_pairs={{0,6},{1,7},{2,4},{3,5},{4,2},{5,3},{6,0},{7,1},{8,14},{9,15},{10,... | collective-permute-start | bytes 221192 | tf_op jit(solution)/shard_map/ppermute | solution.py:23
  27.4 12.2 %copy-start = (bf16[32,1024]{1,0:T(8,128)(2,1)S(1)}, bf16[32,1024]{1,0:T(8,128)(2,1)}, u32[]{:S(2)}) copy-start(bf16[32,1024]{1,0:T(8,128)(2,1)} %param.8) | copy-start | bytes 196612
  29.1 1.6 %collective-permute-start.9 = (bf16[4,32,1024]{2,1,0:T(8,128)(2,1)S(1)}, bf16[4,32,1024]{2,1,0:T(8,128)(2,1)S(1)}, u32[]{:S(2)}, u32[]{:S(2)}) collective-permute-start(bf16[4,32,1024]{2,1,0:T(8,128)(2,1)S(1)} %get-tuple-element.31), channel_id=1, source_target_pairs={{0,1},{1,0},{2,3},{3,2},{4,5},{5,4},{6,7},{7,6},{8,9},{9,8},{10,11... | collective-permute-start | bytes 786440 | tf_op jit(solution)/shard_map/ppermute | solution.py:23
  30.8 6.3 %collective-permute-start.10 = (bf16[32,1024]{1,0:T(8,128)(2,1)S(1)}, bf16[32,1024]{1,0:T(8,128)(2,1)S(1)}, u32[]{:S(2)}, u32[]{:S(2)}) collective-permute-start(bf16[32,1024]{1,0:T(8,128)(2,1)S(1)} %get-tuple-element.32), channel_id=1, source_target_pairs={{0,4},{1,5},{2,6},{3,7},{4,0},{5,1},{6,2},{7,3},{8,12},{9,13},{10,... | collective-permute-start | bytes 196616 | tf_op jit(solution)/shard_map/ppermute | solution.py:23
  32.7 7.0 %collective-permute-start.11 = (bf16[32,1024]{1,0:T(8,128)(2,1)S(1)}, bf16[32,1024]{1,0:T(8,128)(2,1)S(1)}, u32[]{:S(2)}, u32[]{:S(2)}) collective-permute-start(bf16[32,1024]{1,0:T(8,128)(2,1)S(1)} %get-tuple-element.33), channel_id=1, source_target_pairs={{0,2},{1,3},{2,0},{3,1},{4,6},{5,7},{6,4},{7,5},{8,10},{9,11},{10,... | collective-permute-start | bytes 196616 | tf_op jit(solution)/shard_map/ppermute | solution.py:23
  33.4 6.2 %collective-permute-start.12 = (bf16[32,1024]{1,0:T(8,128)(2,1)S(1)}, bf16[32,1024]{1,0:T(8,128)(2,1)S(1)}, u32[]{:S(2)}, u32[]{:S(2)}) collective-permute-start(bf16[32,1024]{1,0:T(8,128)(2,1)S(1)} %get-tuple-element.34), channel_id=1, source_target_pairs={{0,6},{1,7},{2,4},{3,5},{4,2},{5,3},{6,0},{7,1},{8,14},{9,15},{10,... | collective-permute-start | bytes 196616 | tf_op jit(solution)/shard_map/ppermute | solution.py:23
  39.7 4.3 %collective-permute-start.13 = (bf16[32,1024]{1,0:T(8,128)(2,1)S(1)}, bf16[32,1024]{1,0:T(8,128)(2,1)S(1)}, u32[]{:S(2)}, u32[]{:S(2)}) collective-permute-start(bf16[32,1024]{1,0:T(8,128)(2,1)S(1)} %add_convert_fusion.1), channel_id=1, source_target_pairs={{0,16},{16,0},{1,17},{17,1},{2,18},{18,2},{3,19},{19,3},{4,20},{20... | collective-permute-start | bytes 196616 | tf_op jit(solution)/shard_map/ppermute | solution.py:421

commit v3 on v2

v3 whole, which is shorter than its diff:
```python
import functools
import math

import jax
import jax.numpy as jnp
from jax import lax
from jax.experimental import pallas as pl
from jax.experimental.pallas import tpu as pltpu
from jax.sharding import PartitionSpec as P

HEADS = 64
KVH = 8
HD = 128
STEPS = 4
GROUP = HEADS // KVH
MASKED = -1e30
LOG2E = 1.4426950408889634
FACTOR = LOG2E / math.sqrt(HD)
MEGA = 1024 * 1024
LOAD_SHARES = (1, 3, 0, 0, 3, 1)


def swapped(value, mask):
    count = lax.axis_size("tensor")
    return lax.ppermute(value, "tensor", [(source, source ^ mask) for source in range(count)])


def in_hbm(value):
    return pltpu.with_memory_space_constraint(value, pltpu.HBM)


def place_kernel(place):
    place[0] = lax.axis_index("tensor")
    place[1] = lax.axis_index("inst")


def beside_copies(place):
    return pl.when(place[0] >= 0)


def weight_copies(place, weight, out, semaphores, masks):
    rank = place[0]
    chunk = out.shape[2]
    copies = []
    for at, mask in enumerate(masks):
        start = pl.multiple_of((rank ^ mask) * chunk, chunk)
        copies.append(
            pltpu.make_async_copy(
                weight.at[0, :, pl.ds(start, chunk)], out.at[at], semaphores.at[at]
            )
        )
    return copies


def pick_kernel(capacity, weight_masks, place, moves_hbm, pages, weight, *refs):
    outputs, refs = refs[:-5], refs[-5:]
    weight_out, moves, moves_semaphore, semaphores, weight_semaphores = refs
    moves_copy = pltpu.make_async_copy(moves_hbm, moves, moves_semaphore)
    load_copies = weight_copies(place, weight, weight_out, weight_semaphores, weight_masks)
    for copy in [moves_copy] + load_copies:
        copy.start()
    moves_copy.wait()
    tensor_count, inst_count = lax.axis_size("tensor"), lax.axis_size("inst")
    per = max(1, tensor_count // KVH)
    side = place[0] // per % 2
    copies = []
    for shift in range(1, inst_count):
        target = place[1] + shift
        target = jnp.where(target >= inst_count, target - inst_count, target)
        for slot in range(capacity):
            page = moves[target * capacity + slot]
            for other in range(2):
                out = outputs[2 * (shift - 1) + other]
                for pair in range(KVH // 2):
                    head = 2 * pair + (side if other == 0 else 1 - side)
                    start = pl.multiple_of(head * (2 * HD), 2 * HD)
                    copies.append(
                        pltpu.make_async_copy(
                            pages.at[page, :, pl.ds(start, 2 * HD)],
                            out.at[slot, :, 2 * HD * pair : 2 * HD * (pair + 1)],
                            semaphores.at[len(copies)],
                        )
                    )
    for copy in copies:
        copy.start()
    for copy in copies + load_copies:
        copy.wait()


def packed_level(level, lane, heads_per):
    top = level.astype(jnp.bfloat16).astype(jnp.float32)
    rest = level - top
    middle = rest.astype(jnp.bfloat16).astype(jnp.float32)
    level = jnp.where(lane < heads_per, top, jnp.where(lane < 2 * heads_per, middle, rest - middle))
    return level.astype(jnp.bfloat16)


def prepare_kernel(shape, weight_masks, place, table_hbm, lengths_hbm, moves_hbm, weight, *refs):
    owned, refs = refs[:3], refs[4:]
    bias_out, owned_out, refs = refs[0], refs[1:4], refs[4:]
    weight_out, table, lengths, moves, semaphores, weight_semaphores = refs
    pages, page_tokens, capacity = shape
    tensor_count, inst_count = lax.axis_size("tensor"), lax.axis_size("inst")
    tensor_rank, inst_rank = place[0], place[1]
    per = max(1, tensor_count // KVH)
    partner = tensor_rank ^ per
    rows, columns = bias_out.shape
    slots, requests = table.shape
    page_size = page_tokens * tensor_count
    copies = [
        pltpu.make_async_copy(source, target, semaphores.at[at])
        for at, (source, target) in enumerate(
            ((table_hbm, table), (lengths_hbm, lengths), (moves_hbm, moves))
        )
    ]
    load_copies = [
        pltpu.make_async_copy(source, target, semaphores.at[3 + at])
        for at, (source, target) in enumerate(zip(owned, owned_out))
    ] + weight_copies(place, weight, weight_out, weight_semaphores, weight_masks)
    for copy in copies + load_copies:
        copy.start()
    for copy in copies:
        copy.wait()

    @beside_copies(place)
    def _():
        row = lax.broadcasted_iota(jnp.int32, (rows, 1), 0)
        row_request, row_step = row // STEPS, row % STEPS
        row_length = jnp.zeros((rows, 1), jnp.int32)
        row_pages = [jnp.zeros((rows, 1), jnp.int32) for _ in range(slots)]
        for request in range(requests):
            here = row_request == request
            row_length = jnp.where(here, lengths[request], row_length)
            for slot in range(slots):
                page = table[slot, request]
                arrived = page - pages
                for own in range(capacity):
                    page = jnp.where(
                        arrived == inst_rank * capacity + own, moves[inst_rank * capacity + own], page
                    )
                row_pages[slot] = jnp.where(here, page, row_pages[slot])

        column = lax.broadcasted_iota(jnp.int32, (1, columns), 1)
        own_columns = pages * page_tokens
        block_columns = capacity * page_tokens
        moved = column - 2 * own_columns
        block = moved // block_columns
        source = inst_rank - block // 2 - 1
        source = jnp.where(source < 0, source + inst_count, source)
        resident = moved < 0
        page = jnp.where(
            resident,
            column % own_columns // page_tokens,
            pages + source * capacity + moved // page_tokens % capacity,
        )
        side = jnp.where(resident, column // own_columns, block % 2)
        token = jnp.where(side == 0, tensor_rank, partner) * page_tokens + column % page_tokens
        use = jnp.zeros((rows, columns), jnp.float32)
        for slot in range(slots):
            live = (row_pages[slot] == page) & (token + slot * page_size < row_length)
            use = use + jnp.where(live, 1.0, 0.0)
        fresh = column - (columns - rows)
        fresh_live = (fresh // STEPS == row_request) & (fresh % STEPS <= row_step)
        fresh_live = fresh_live & ((tensor_rank == 0) | (tensor_rank == per))
        use = jnp.where(fresh >= 0, jnp.where(fresh_live, 1.0, 0.0), use)
        bias_out[...] = jnp.where(use > 0.0, jnp.log2(jnp.maximum(use, 1.0)) / FACTOR, MASKED)

    for copy in load_copies:
        copy.wait()


def attend_kernel(masks, weight_masks, piece_count, after_count, *refs):
    place, bias_ref, refs = refs[0], refs[1], refs[2:]
    tensor_count, tensor_rank = lax.axis_size("tensor"), place[0]
    queries, refs = refs[: len(masks)], refs[len(masks) :]
    pieces, refs = refs[:piece_count], refs[piece_count + after_count :]
    if weight_masks:
        weight, *refs, weight_out, weight_semaphores = refs
    parts = refs
    per = max(1, tensor_count // KVH)
    rows = bias_ref.shape[0]
    heads_per = HEADS // tensor_count
    groups = len(masks) // per

    load_copies = []
    if weight_masks:
        load_copies = weight_copies(place, weight, weight_out, weight_semaphores, weight_masks)
    for copy in load_copies:
        copy.start()

    @beside_copies(place)
    def _():
        bias = bias_ref[...]
        lane = lax.broadcasted_iota(jnp.int32, (rows, HD), 1)
        for group in range(groups):
            kv_head = (tensor_rank ^ masks[group * per]) // per
            keys, values = [], []
            for piece in pieces:
                halved = piece.shape[1] < KVH * 2 * HD
                start = pl.multiple_of((kv_head // 2 if halved else kv_head) * (2 * HD), 2 * HD)
                keys.append(piece[:, pl.ds(start, HD)])
                values.append(piece[:, pl.ds(pl.multiple_of(start + HD, HD), HD)])
            blocks = []
            for block in queries[group * per : group * per + per]:
                blocks += [block[:, head * HD : (head + 1) * HD] for head in range(heads_per)]
            stacked = jnp.concatenate(blocks, axis=0)
            scores = lax.dot_general(
                stacked,
                jnp.concatenate(keys, axis=0),
                (((1,), (1,)), ((), ())),
                preferred_element_type=jnp.float32,
            )
            weights, totals, level = [], [], []
            for at in range(GROUP):
                shifted = scores[at * rows : (at + 1) * rows] + bias
                row_max = jnp.max(shifted, axis=1, keepdims=True)
                expo = jnp.exp2((shifted - row_max) * FACTOR)
                total = jnp.sum(expo, axis=1, keepdims=True)
                weights.append(expo.astype(jnp.bfloat16))
                totals.append(total)
                level.append(row_max * FACTOR + jnp.log2(total))
            weighted = jnp.dot(
                jnp.concatenate(weights, axis=0),
                jnp.concatenate(values, axis=0),
                preferred_element_type=jnp.float32,
            )
            for low in range(per):
                out = parts[group * per + low]
                levels = jnp.zeros((rows, HD), jnp.float32)
                for head in range(heads_per):
                    at = low * heads_per + head
                    attended = weighted[at * rows : (at + 1) * rows] / totals[at]
                    out[:, head * HD : (head + 1) * HD] = attended.astype(jnp.bfloat16)
                    levels = jnp.where(lane % heads_per == head, level[at], levels)
                out[:, heads_per * HD :] = packed_level(levels, lane, heads_per)

    for copy in load_copies:
        copy.wait()


def combined(parts, heads_per):
    levels = []
    for part in parts:
        level = part[:, heads_per * HD :].astype(jnp.float32)
        levels.append(
            level
            + pltpu.roll(level, HD - heads_per, 1)
            + pltpu.roll(level, HD - 2 * heads_per, 1)
        )
    top = functools.reduce(jnp.maximum, levels)
    shares = [jnp.exp2(level - top) for level in levels]
    total = sum(shares[1:], shares[0])
    shares = [share / total for share in shares]
    heads = []
    for head in range(heads_per):
        terms = [
            share[:, head : head + 1] * part[:, head * HD : (head + 1) * HD].astype(jnp.float32)
            for share, part in zip(shares, parts)
        ]
        heads.append(sum(terms[1:], terms[0]).astype(jnp.bfloat16))
    return jnp.concatenate(heads, axis=1)


def project(rows, weights, found, out):
    for at, (array, block) in enumerate(found):
        product = jnp.dot(rows, weights[array][block], preferred_element_type=jnp.float32)
        out[at] = product.astype(out.dtype)


def project_away_kernel(heads_per, part_count, found, weight_masks, place, *refs):
    parts, refs = refs[:part_count], refs[part_count:]
    load_copies = []
    if weight_masks:
        *refs, weight_out, weight_semaphores = refs
        weight, refs = refs[0], refs[1:]
        load_copies = weight_copies(place, weight, weight_out, weight_semaphores, weight_masks)
    *weights, out, attended = refs
    for copy in load_copies:
        copy.start()

    @beside_copies(place)
    def _():
        rows = combined(parts, heads_per)
        attended[...] = rows
        project(rows, weights, found, out)

    for copy in load_copies:
        copy.wait()


def project_home_kernel(found, attended, *refs):
    project(attended[...], refs[:-1], found, refs[-1])


def add_far_kernel(home, sibling, out):
    out[...] = (home[1] + sibling[1].astype(jnp.float32)).astype(out.dtype)


def add_own_kernel(home, sibling, far, out):
    own = home[0] + sibling[0].astype(jnp.float32)
    out[...] = own + far[...].astype(jnp.float32)


def project_near_kernel(found, attended, sibling, after, *refs):
    weights, outputs = refs[: len(refs) - len(found)], refs[len(refs) - len(found) :]
    rows = attended[...]
    for at, (array, block) in enumerate(found):
        product = jnp.dot(rows, weights[array][block], preferred_element_type=jnp.float32)
        total = product + sibling[at + 2].astype(jnp.float32)
        outputs[at][...] = total.astype(outputs[at].dtype)


def local(hidden_in, queries, new_kv, kv_pages, out_weight, move_pages, page_table, lengths):
    tensor_count = lax.axis_size("tensor")
    inst_count = lax.axis_size("inst")
    section_rank = lax.axis_index("section")
    per = max(1, tensor_count // KVH)
    heads_per = HEADS // tensor_count
    requests, slots = page_table.shape
    rows = requests * STEPS
    own_pages = kv_pages[0]
    pages, page_tokens, width = own_pages.shape
    capacity = move_pages.shape[2]
    moves = in_hbm(move_pages.reshape(-1))
    depth, features = out_weight.shape[1:]
    chunk = features // tensor_count
    half = tensor_count // 2
    vmem = pl.BlockSpec(memory_space=pltpu.VMEM)
    hbm = pl.BlockSpec(memory_space=pltpu.HBM)
    peers = [mask for mask in range(tensor_count) if mask & per == 0]

    if len(peers) == 4:
        peers = [0, 6, 4, 2]
    home_masks = [2 * mask for mask in range(half)]
    if half == 4:
        home_masks = [0, 6, 4, 2]
    away_masks = [mask ^ 1 for mask in home_masks]
    unit = tensor_count // 8
    loads, filled = [], 0
    for share in LOAD_SHARES:
        loads.append((away_masks + home_masks)[filled : filled + share * unit])
        filled += share * unit
    moved_weights = []

    def weight_parts(wanted):
        arrays = [
            (masks, array) for masks, array in zip(loads, moved_weights) if set(masks) & set(wanted)
        ]
        found = [
            (at, masks.index(mask))
            for mask in wanted
            for at, (masks, _) in enumerate(arrays)
            if mask in masks
        ]
        return [array for _, array in arrays], found

    weight = in_hbm(out_weight)

    def weight_shape(count):
        return pltpu.VMEM((count, depth, chunk), jnp.bfloat16)

    smem = pl.BlockSpec(memory_space=pltpu.SMEM)
    place = pl.pallas_call(
        place_kernel,
        out_shape=pltpu.SMEM((2,), jnp.int32),
        out_specs=smem,
        name="place",
    )()

    own_queries = queries[0]
    all_queries = {mask: swapped(own_queries, mask) for mask in peers[1:]}
    own_flat = own_pages.reshape(pages * page_tokens, width)
    partner_flat = swapped(own_flat, per)
    *leaving, moved = pl.pallas_call(
        functools.partial(pick_kernel, capacity, loads[0]),
        out_shape=[jax.ShapeDtypeStruct((capacity, page_tokens, width // 2), jnp.bfloat16)]
        * (2 * (inst_count - 1))
        + [weight_shape(len(loads[0]))],
        in_specs=[smem] + [hbm] * 3,
        out_specs=[vmem] * (2 * inst_count - 1),
        scratch_shapes=[
            pltpu.SMEM(moves.shape, jnp.int32),
            pltpu.SemaphoreType.DMA,
            pltpu.SemaphoreType.DMA(((inst_count - 1) * capacity * KVH,)),
            pltpu.SemaphoreType.DMA((len(loads[0]),)),
        ],
        compiler_params=pltpu.CompilerParams(vmem_limit_bytes=2 * MEGA),
        name="pick",
    )(place, moves, in_hbm(own_pages), weight)
    moved_weights.append(moved)
    arrived = []
    for shift in range(1, inst_count):
        for other in range(2):
            pairs = [
                (
                    inst * tensor_count + rank,
                    (inst + shift) % inst_count * tensor_count + (rank ^ (per * other)),
                )
                for inst in range(inst_count)
                for rank in range(tensor_count)
            ]
            sent = leaving[2 * (shift - 1) + other].reshape(capacity * page_tokens, width // 2)
            arrived.append(lax.ppermute(sent, ("inst", "tensor"), pairs))
    if page_tokens * capacity % 16:
        arrived = [jnp.concatenate(arrived, axis=0)]
    owned = [own_queries, own_flat, new_kv[0]]
    columns = 2 * own_flat.shape[0] + sum(piece.shape[0] for piece in arrived) + rows

    bias, all_queries[0], own_tokens, new_tokens, moved = pl.pallas_call(
        functools.partial(
            prepare_kernel, (pages, page_tokens, capacity), loads[1]
        ),
        out_shape=[jax.ShapeDtypeStruct((rows, columns), jnp.float32)]
        + [pltpu.VMEM(value.shape, value.dtype) for value in owned]
        + [weight_shape(len(loads[1]))],
        in_specs=[smem] + [hbm] * 7 + [vmem],
        out_specs=[vmem] * 5,
        scratch_shapes=[
            pltpu.SMEM((slots, requests), jnp.int32),
            pltpu.SMEM((requests,), jnp.int32),
            pltpu.SMEM(moves.shape, jnp.int32),
            pltpu.SemaphoreType.DMA((6,)),
            pltpu.SemaphoreType.DMA((len(loads[1]),)),
        ],
        compiler_params=pltpu.CompilerParams(vmem_limit_bytes=2 * MEGA),
        name="prepare",
    )(
        place,
        in_hbm(page_table.T),
        in_hbm(lengths),
        moves,
        weight,
        *[in_hbm(value) for value in owned],
        all_queries[peers[per]],
    )
    moved_weights.append(moved)
    pieces = [own_tokens, partner_flat, *arrived, new_tokens]

    part_shape = jax.ShapeDtypeStruct((rows, heads_per * HD + HD), jnp.bfloat16)

    def attend(masks, weight_masks, *after):
        loading = bool(weight_masks)
        results = pl.pallas_call(
            functools.partial(attend_kernel, masks, weight_masks, len(pieces), len(after)),
            out_shape=[part_shape] * len(masks) + [weight_shape(len(weight_masks))] * loading,
            in_specs=[smem] + [vmem] * (1 + len(masks) + len(pieces) + len(after)) + [hbm] * loading,
            out_specs=[vmem] * (len(masks) + loading),
            scratch_shapes=[pltpu.SemaphoreType.DMA((len(weight_masks),))] * loading,
            compiler_params=pltpu.CompilerParams(vmem_limit_bytes=8 * MEGA),
            name="attend",
        )(place, bias, *[all_queries[mask] for mask in masks], *pieces, *after, *[weight] * loading)
        moved_weights.append(results[-1] if loading else None)
        return dict(zip(masks, results))

    received, after = {}, []
    for masks, weight_masks in (
        (peers[per : 2 * per], loads[2]),
        (peers[2 * per :], loads[3]),
        (peers[:per], loads[4]),
    ):
        parts = attend(masks, weight_masks, *after)
        after = [received[peers[per]] if received else parts[masks[0]]]
        received.update({mask: swapped(part, mask) for mask, part in parts.items() if mask})
    received = [parts[0]] + [received[mask] for mask in peers[1:]]

    project_params = pltpu.CompilerParams(vmem_limit_bytes=4 * MEGA)
    loading = bool(loads[5])
    away_weights, found = weight_parts(away_masks)
    away, attended, *moved = pl.pallas_call(
        functools.partial(project_away_kernel, heads_per, half, found, loads[5]),
        in_specs=[smem] + [vmem] * half + [hbm] * loading + [vmem] * len(away_weights),
        out_specs=[vmem] * (2 + loading),
        out_shape=[
            jax.ShapeDtypeStruct((half, rows, chunk), jnp.bfloat16),
            jax.ShapeDtypeStruct((rows, depth), jnp.bfloat16),
        ]
        + [weight_shape(len(loads[5]))] * loading,
        scratch_shapes=[pltpu.SemaphoreType.DMA((len(loads[5]),))] * loading,
        compiler_params=project_params,
        name="project_away",
    )(place, *received, *[weight] * loading, *away_weights)
    moved_weights.extend(moved)
    sibling = swapped(away, 1)
    home_weights, found = weight_parts(home_masks[:2])
    home = pl.pallas_call(
        functools.partial(project_home_kernel, found),
        in_specs=[vmem] * (1 + len(home_weights)),
        out_specs=vmem,
        out_shape=jax.ShapeDtypeStruct((2, rows, chunk), jnp.float32),
        compiler_params=project_params,
        name="project_home",
    )(attended, *home_weights)
    sum_shape = jax.ShapeDtypeStruct((rows, chunk), jnp.bfloat16)
    far_sum = pl.pallas_call(
        add_far_kernel,
        in_specs=[vmem] * 2,
        out_specs=vmem,
        out_shape=sum_shape,
        compiler_params=pltpu.CompilerParams(vmem_limit_bytes=2 * MEGA),
        name="add_far",
    )(home, sibling)
    home_weights, found = weight_parts(home_masks[2:])
    near_sums = pl.pallas_call(
        functools.partial(project_near_kernel, found),
        in_specs=[vmem] * (3 + len(home_weights)),
        out_specs=[vmem] * (half - 2),
        out_shape=[sum_shape] * (half - 2),
        compiler_params=project_params,
        name="project_near",
    )(attended, sibling, far_sum, *home_weights)
    projected = pl.pallas_call(
        add_own_kernel,
        in_specs=[vmem] * 3,
        out_specs=vmem,
        out_shape=jax.ShapeDtypeStruct((rows, chunk), jnp.float32),
        compiler_params=pltpu.CompilerParams(vmem_limit_bytes=2 * MEGA),
        name="add_own",
    )(home, sibling, swapped(far_sum, home_masks[1]))
    for mask, total in zip(home_masks[2:], near_sums):
        projected = projected + swapped(total, mask).astype(jnp.float32)
    after_first = (hidden_in.astype(jnp.float32) + projected).astype(jnp.bfloat16)
    handed_over = lax.ppermute(after_first, "section", [(0, 1), (1, 0)])
    after_second = (handed_over.astype(jnp.float32) + projected).astype(jnp.bfloat16)
    result = jnp.where(section_rank == 0, after_first, after_second)
    return result[None]


def solution(mesh):
    return jax.shard_map(
        local,
        mesh=mesh,
        in_specs=(
            P("inst", "tensor"),
            P("section", "inst", "tensor"),
            P("section", "inst", None),
            P("section", "inst", "tensor", None),
            P("section", "tensor", None),
            P("inst", None, None),
            P("inst", None),
            P("inst"),
        ),
        out_specs=P("section", "inst", "tensor"),
        check_vma=False,
    )
```

time: 44.9 us -> 42 us (0.935)
  starting transfers between devices: 20.2 us -> 18.2 us
  Pallas kernels: 14.5 us -> 13.1 us
    pallas_call x2 -> x3, Pallas kernels: 6.03 us -> 4.55 us  [attend(): pl.pallas_call(functools.partial(attend_kernel, masks, weight_masks, len(...]
    ppermute x2, starting transfers between devices: 2.74 us -> 1.64 us  [local(): arrived.append(lax.ppermute(sent, ('inst', 'tensor'), pairs))]
    ppermute x11, starting transfers between devices: 15.8 us -> 14.9 us  [swapped(): lax.ppermute(value, 'tensor', [(source, source ^ mask) for source in rang...]
    pallas_call x5 -> x8, Pallas kernels: 8.43 us -> 8.58 us  [the longest x1 3.33 us: local(): pl.pallas_call(functools.partial(prepare_kernel, (pages, page_tokens, cap...]
  transfers between devices with their start and end apart: 14 -> 14, of which waited for: 5 -> 7; matrix products, arithmetic and copies ran while one was open for 0% -> 0% of each run, Pallas kernels for 22% -> 27%
where the time goes in v3:
time: 42 us; the launch traced here: 41.8 us
  starting transfers between devices  18.2 us (43%)
  Pallas kernels  13.1 us (31%)
  waiting for transfers between devices  9.63 us (23%)
  other arithmetic  0.71 us (2%)
    ppermute x11, starting transfers between devices, swapped(): lax.ppermute(value, 'tensor', [(source, source ^ mask) for source in rang...  14.9 us
    ppermute x11, waiting for transfers between devices, swapped(): lax.ppermute(value, 'tensor', [(source, source ^ mask) for source in rang...  6.88 us
    pallas_call x3, Pallas kernels, attend(): pl.pallas_call(functools.partial(attend_kernel, masks, weight_masks, len(...  4.55 us
    pallas_call x1, Pallas kernels, local(): pl.pallas_call(functools.partial(prepare_kernel, (pages, page_tokens, cap...  3.33 us
    ppermute x1, waiting for transfers between devices, local(): handed_over = lax.ppermute(after_first, 'section', [(0, 1), (1, 0)])  2.75 us
    pallas_call x1, Pallas kernels, local(): pl.pallas_call(functools.partial(pick_kernel, capacity, loads[0]), out_sh...  1.85 us
    pallas_call x1, Pallas kernels, local(): pl.pallas_call(functools.partial(project_away_kernel, heads_per, half, fo...  1.73 us
    ppermute x2, starting transfers between devices, local(): arrived.append(lax.ppermute(sent, ('inst', 'tensor'), pairs))  1.64 us
  transfers between devices with their start and end apart: 14, of which 7 were waited for; matrix products, arithmetic and copies ran while one was open for 0% of the time, Pallas kernels for 27%

profile of v3, /device:TPU:0, one launch (start us, length us, event | category | flops | bytes accessed | tf_op | source)
XLA Modules:
  0.0 41.8 jit_solution(18171539811481080166)
XLA Ops:
  0.0 0.5 %collective-permute-start.1 = (bf16[256,2048]{1,0:T(8,128)(2,1)}, bf16[256,2048]{1,0:T(8,128)(2,1)S(1)}, u32[]{:S(2)}, u32[]{:S(2)}) collective-permute-start(bf16[256,2048]{1,0:T(8,128)(2,1)} %bitcast.12), channel_id=1, source_target_pairs={{0,1},{1,0},{2,3},{3,2},{4,5},{5,4},{6,7},{7,6},{8,9},{9,8},{10,11... | collective-permute-start | bytes 3145736 | tf_op jit(solution)/shard_map/ppermute | solution.py:25
  0.5 4.6 %collective-permute-start = (bf16[32,1024]{1,0:T(8,128)(2,1)}, bf16[32,1024]{1,0:T(8,128)(2,1)S(1)}, u32[]{:S(2)}, u32[]{:S(2)}) collective-permute-start(bf16[32,1024]{1,0:T(8,128)(2,1)} %bitcast.16), channel_id=1, source_target_pairs={{0,6},{1,7},{2,4},{3,5},{4,2},{5,3},{6,0},{7,1},{8,14},{9,15},{10,... | collective-permute-start | bytes 196616 | tf_op jit(solution)/shard_map/ppermute | solution.py:25
  5.1 1.9 %pick.1 = (bf16[1,32,1024]{2,1,0:T(8,128)(2,1)S(1)}, bf16[1,32,1024]{2,1,0:T(8,128)(2,1)S(1)}, bf16[1,1024,1024]{2,1,0:T(8,128)(2,1)S(1)}) custom-call(s32[2]{0:T(128)S(4)} %place.1.refs_0_, s32[2]{0:T(128)} %bitcast.21, bf16[8,32,2048]{2,1,0:T(8,128)(2,1)} %bitcast.13, bf16[1,1024,8192]{2,1,0:T(8,128)(2,1)} %refs_4_.1), custom_call_target="tpu_custom_call" | custom-call | tf_op jit(solution)/shard_map/pick/pallas_call | solution.py:374
  6.9 1.6 %collective-permute-start.2 = (bf16[32,1024]{1,0:T(8,128)(2,1)S(1)}, bf16[32,1024]{1,0:T(8,128)(2,1)S(1)}, u32[]{:S(2)}, u32[]{:S(2)}) collective-permute-start(bf16[32,1024]{1,0:T(8,128)(2,1)S(1)} %bitcast.11), channel_id=1, source_target_pairs={{0,8},{1,9},{2,10},{3,11},{4,12},{5,13},{6,14},{7,15},{8,0},{9,1},... | collective-permute-start | bytes 196616 | tf_op jit(solution)/shard_map/ppermute | solution.py:403
  8.5 0.1 collective-permute-start.3
  8.6 0.8 %collective-permute-start.6 = (bf16[32,1024]{1,0:T(8,128)(2,1)S(1)}, bf16[32,1024]{1,0:T(8,128)(2,1)S(1)}, u32[]{:S(2)}, u32[]{:S(2)}) collective-permute-start(bf16[32,1024]{1,0:T(8,128)(2,1)S(1)} %bitcast.19), channel_id=1, source_target_pairs={{0,2},{1,3},{2,0},{3,1},{4,6},{5,7},{6,4},{7,5},{8,10},{9,11},{10,... | collective-permute-start | bytes 196616 | tf_op jit(solution)/shard_map/ppermute | solution.py:25
  9.4 3.3 %prepare.1 = (f32[32,608]{1,0:T(8,128)S(1)}, bf16[32,1024]{1,0:T(8,128)(2,1)S(1)}, bf16[256,2048]{1,0:T(8,128)(2,1)S(1)}, bf16[32,2048]{1,0:T(8,128)(2,1)S(1)}, bf16[3,1024,1024]{2,1,0:T(8,128)(2,1)S(1)}) custom-call(s32[2]{0:T(128)S(4)} %place.1.refs_0_, s32[4,8]{1,0:T(4,128)} %bitcast.20, s32[8]{0:T(128)} %lengths_hbm.1, s32[2]{0:T(128)} %bitcast.22, ...), custom_call_target="tpu_custom_call" | custom-call | tf_op jit(solution)/shard_map/prepare/pallas_call | solution.py:409
  12.8 0.0 collective-permute-done.2.refs_5_.refs_6_
  12.8 0.0 collective-permute-done.1.refs_4_.refs_5_
  12.8 0.6 %attend.3.refs_9_ = bf16[32,1152]{1,0:T(8,128)(2,1)S(1)} custom-call(s32[2]{0:T(128)S(4)} %place.1.refs_0_, f32[32,608]{1,0:T(8,128)S(1)} %get-tuple-element.22.refs_1_, bf16[32,1024]{1,0:T(8,128)(2,1)S(1)} %collective-permute-done.refs_3_.refs_2_, bf16[256,2048]{1,0:T(8,128)(2,1)S(1)} %get-tuple-element.24.refs_3_.refs_4_, ...), custom_call_target="tpu_custom_call" | custom-call | tf_op jit(solution)/shard_map/attend/pallas_call | solution.py:443
  13.4 3.6 %collective-permute-start.4 = (bf16[32,1152]{1,0:T(8,128)(2,1)S(1)}, bf16[32,1152]{1,0:T(8,128)(2,1)S(1)}, u32[]{:S(2)}, u32[]{:S(2)}) collective-permute-start(bf16[32,1152]{1,0:T(8,128)(2,1)S(1)} %attend.3.refs_9_), channel_id=1, source_target_pairs={{0,6},{1,7},{2,4},{3,5},{4,2},{5,3},{6,0},{7,1},{8,14},{9,15},{10,... | collective-permute-start | bytes 221192 | tf_op jit(solution)/shard_map/ppermute | solution.py:25
  17.0 0.0 collective-permute-done.5.refs_2_
  17.0 1.0 %attend.5 = (bf16[32,1152]{1,0:T(8,128)(2,1)S(1)}, bf16[32,1152]{1,0:T(8,128)(2,1)S(1)}) custom-call(s32[2]{0:T(128)S(4)} %place.1.refs_0_, f32[32,608]{1,0:T(8,128)S(1)} %get-tuple-element.22.refs_1_, bf16[32,1024]{1,0:T(8,128)(2,1)S(1)} %collective-permute-done.5.refs_2_, bf16[32,1024]{1,0:T(8,128)(2,1)S(1)} %collective-permute-done.6.refs_3_, ...), custom_call_target="tpu_custom_call" | custom-call | tf_op jit(solution)/shard_map/attend/pallas_call | solution.py:443
  18.1 0.1 collective-permute-start.7
  18.1 0.8 %collective-permute-start.8 = (bf16[32,1152]{1,0:T(8,128)(2,1)S(1)}, bf16[32,1152]{1,0:T(8,128)(2,1)S(1)}, u32[]{:S(2)}, u32[]{:S(2)}) collective-permute-start(bf16[32,1152]{1,0:T(8,128)(2,1)S(1)} %get-tuple-element.30), channel_id=1, source_target_pairs={{0,2},{1,3},{2,0},{3,1},{4,6},{5,7},{6,4},{7,5},{8,10},{9,11},{10,... | collective-permute-start | bytes 221192 | tf_op jit(solution)/shard_map/ppermute | solution.py:25
  19.0 0.8 %collective-permute-done.4.refs_8_.refs_1_ = bf16[32,1152]{1,0:T(8,128)(2,1)S(1)} collective-permute-done((bf16[32,1152]{1,0:T(8,128)(2,1)S(1)}, bf16[32,1152]{1,0:T(8,128)(2,1)S(1)}, u32[]{:S(2)}, u32[]{:S(2)}) %collective-permute-start.4) | collective-permute-done | bytes 73760 | tf_op jit(solution)/shard_map/ppermute | solution.py:25
  19.8 2.9 %attend.4 = (bf16[32,1152]{1,0:T(8,128)(2,1)S(1)}, bf16[3,1024,1024]{2,1,0:T(8,128)(2,1)S(1)}) custom-call(s32[2]{0:T(128)S(4)} %place.1.refs_0_, f32[32,608]{1,0:T(8,128)S(1)} %get-tuple-element.22.refs_1_, bf16[32,1024]{1,0:T(8,128)(2,1)S(1)} %get-tuple-element.23.refs_2_, bf16[256,2048]{1,0:T(8,128)(2,1)S(1)} %get-tuple-element.24.refs_3_.refs_4_, ...), custom_call_target="tpu_custom_call" | custom-call | tf_op jit(solution)/shard_map/attend/pallas_call | solution.py:443
  22.7 1.1 %collective-permute-done.7.refs_2_ = bf16[32,1152]{1,0:T(8,128)(2,1)S(1)} collective-permute-done((bf16[32,1152]{1,0:T(8,128)(2,1)S(1)}, bf16[32,1152]{1,0:T(8,128)(2,1)S(1)}, u32[]{:S(2)}, u32[]{:S(2)}) %collective-permute-start.7) | collective-permute-done | bytes 73760 | tf_op jit(solution)/shard_map/ppermute | solution.py:25
  23.7 1.7 %project_away.1 = (bf16[4,32,1024]{2,1,0:T(8,128)(2,1)S(1)}, bf16[32,1024]{1,0:T(8,128)(2,1)S(1)}, bf16[1,1024,1024]{2,1,0:T(8,128)(2,1)S(1)}) custom-call(s32[2]{0:T(128)S(4)} %place.1.refs_0_, bf16[32,1152]{1,0:T(8,128)(2,1)S(1)} %get-tuple-element.28.refs_0_, bf16[32,1152]{1,0:T(8,128)(2,1)S(1)} %collective-permute-done.4.refs_8_.refs_1_, ...), custom_call_target="tpu_custom_call" | custom-call | tf_op jit(solution)/shard_map/project_away/pallas_call | solution.py:469
  25.5 0.1 collective-permute-start.9
  25.5 0.8 %project_home.1.home = f32[2,32,1024]{2,1,0:T(8,128)S(1)} custom-call(bf16[32,1024]{1,0:T(8,128)(2,1)S(1)} %get-tuple-element.33.attended, bf16[3,1024,1024]{2,1,0:T(8,128)(2,1)S(1)} %get-tuple-element.34.refs_0_), custom_call_target="tpu_custom_call" | custom-call | tf_op jit(solution)/shard_map/project_home/pallas_call | solution.py:485
  26.4 0.7 %collective-permute-done.9.sibling = bf16[4,32,1024]{2,1,0:T(8,128)(2,1)S(1)} collective-permute-done((bf16[4,32,1024]{2,1,0:T(8,128)(2,1)S(1)}, bf16[4,32,1024]{2,1,0:T(8,128)(2,1)S(1)}, u32[]{:S(2)}, u32[]{:S(2)}) %collective-permute-start.9) | collective-permute-done | bytes 262176 | tf_op jit(solution)/shard_map/ppermute | solution.py:25
  27.1 3.1 %collective-permute-start.10 = (bf16[32,1024]{1,0:T(8,128)(2,1)S(1)}, bf16[32,1024]{1,0:T(8,128)(2,1)S(1)}, u32[]{:S(2)}, u32[]{:S(2)}) collective-permute-start(bf16[32,1024]{1,0:T(8,128)(2,1)S(1)} %add_far.1.after), channel_id=1, source_target_pairs={{0,6},{1,7},{2,4},{3,5},{4,2},{5,3},{6,0},{7,1},{8,14},{9,15},{10,... | collective-permute-start | bytes 196616 | tf_op jit(solution)/shard_map/ppermute | solution.py:25
  30.2 0.8 %project_near.1 = (bf16[32,1024]{1,0:T(8,128)(2,1)S(1)}, bf16[32,1024]{1,0:T(8,128)(2,1)S(1)}) custom-call(bf16[32,1024]{1,0:T(8,128)(2,1)S(1)} %get-tuple-element.33.attended, bf16[4,32,1024]{2,1,0:T(8,128)(2,1)S(1)} %collective-permute-done.9.sibling, bf16[32,1024]{1,0:T(8,128)(2,1)S(1)} %add_far.1.after, ...), custom_call_target="tpu_custom_call" | custom-call | tf_op jit(solution)/shard_map/project_near/pallas_call | solution.py:503
  31.0 0.0 collective-permute-start.11
  31.0 1.4 %collective-permute-start.12 = (bf16[32,1024]{1,0:T(8,128)(2,1)S(1)}, bf16[32,1024]{1,0:T(8,128)(2,1)S(1)}, u32[]{:S(2)}, u32[]{:S(2)}) collective-permute-start(bf16[32,1024]{1,0:T(8,128)(2,1)S(1)} %get-tuple-element.38), channel_id=1, source_target_pairs={{0,2},{1,3},{2,0},{3,1},{4,6},{5,7},{6,4},{7,5},{8,10},{9,11},{10,... | collective-permute-start | bytes 196616 | tf_op jit(solution)/shard_map/ppermute | solution.py:25
  32.4 1.1 %collective-permute-done.10.far = bf16[32,1024]{1,0:T(8,128)(2,1)S(1)} collective-permute-done((bf16[32,1024]{1,0:T(8,128)(2,1)S(1)}, bf16[32,1024]{1,0:T(8,128)(2,1)S(1)}, u32[]{:S(2)}, u32[]{:S(2)}) %collective-permute-start.10) | collective-permute-done | bytes 65568 | tf_op jit(solution)/shard_map/ppermute | solution.py:25
  33.5 2.8 %collective-permute-done.11 = bf16[32,1024]{1,0:T(8,128)(2,1)S(1)} collective-permute-done((bf16[32,1024]{1,0:T(8,128)(2,1)S(1)}, bf16[32,1024]{1,0:T(8,128)(2,1)S(1)}, u32[]{:S(2)}, u32[]{:S(2)}) %collective-permute-start.11) | collective-permute-done | bytes 65568 | tf_op jit(solution)/shard_map/ppermute | solution.py:25
  36.3 0.4 collective-permute-done.12
  36.8 1.6 %collective-permute-start.13 = (bf16[32,1024]{1,0:T(8,128)(2,1)S(1)}, bf16[32,1024]{1,0:T(8,128)(2,1)S(1)}, u32[]{:S(2)}, u32[]{:S(2)}) collective-permute-start(bf16[32,1024]{1,0:T(8,128)(2,1)S(1)} %add_convert_fusion.1), channel_id=1, source_target_pairs={{0,16},{16,0},{1,17},{17,1},{2,18},{18,2},{3,19},{19,3},{4,20},{20... | collective-permute-start | bytes 196616 | tf_op jit(solution)/shard_map/ppermute | solution.py:522
  38.3 2.8 %collective-permute-done.13 = bf16[32,1024]{1,0:T(8,128)(2,1)S(1)} collective-permute-done((bf16[32,1024]{1,0:T(8,128)(2,1)S(1)}, bf16[32,1024]{1,0:T(8,128)(2,1)S(1)}, u32[]{:S(2)}, u32[]{:S(2)}) %collective-permute-start.13) | collective-permute-done | bytes 65568 | tf_op jit(solution)/shard_map/ppermute | solution.py:522
  41.1 0.7 %fusion.1 = bf16[1,32,1024]{2,1,0:T(8,128)(2,1)} fusion(bf16[32,1024]{1,0:T(8,128)(2,1)S(1)} %collective-permute-done.13, pred[]{:T(512)S(6)} %eq.3, bf16[32,1024]{1,0:T(8,128)(2,1)S(1)} %collective-permute-done.12, f32[32,1024]{1,0:T(8,128)S(1)} %add_own.1, bf16[32,1024]{1,0:T(8,128)(2,1)S(1)} %collective-permute-done.11, bf16[32,1024]{1,0:T(8,128)(2,1)S(1)} %copy-done), kind=kLoop, calls=%fused_computation.4 | loop fusion | flops 360448 | bytes 458753 | tf_op jit(solution)/shard_map/broadcast_in_dim | solution.py:525
  (13 shorter events, 0.1 us)
Async XLA Ops:
  0.0 12.8 %collective-permute-start.1 = (bf16[256,2048]{1,0:T(8,128)(2,1)}, bf16[256,2048]{1,0:T(8,128)(2,1)S(1)}, u32[]{:S(2)}, u32[]{:S(2)}) collective-permute-start(bf16[256,2048]{1,0:T(8,128)(2,1)} %bitcast.12), channel_id=1, source_target_pairs={{0,1},{1,0},{2,3},{3,2},{4,5},{5,4},{6,7},{7,6},{8,9},{9,8},{10,11... | collective-permute-start | bytes 3145736 | tf_op jit(solution)/shard_map/ppermute | solution.py:25
  0.5 8.1 %collective-permute-start = (bf16[32,1024]{1,0:T(8,128)(2,1)}, bf16[32,1024]{1,0:T(8,128)(2,1)S(1)}, u32[]{:S(2)}, u32[]{:S(2)}) collective-permute-start(bf16[32,1024]{1,0:T(8,128)(2,1)} %bitcast.16), channel_id=1, source_target_pairs={{0,6},{1,7},{2,4},{3,5},{4,2},{5,3},{6,0},{7,1},{8,14},{9,15},{10,... | collective-permute-start | bytes 196616 | tf_op jit(solution)/shard_map/ppermute | solution.py:25
  5.1 3.5 %copy-start.1 = (bf16[1,32,1024]{2,1,0:T(8,128)(2,1)S(1)}, bf16[1,32,1024]{2,1,0:T(8,128)(2,1)}, u32[]{:S(2)}) copy-start(bf16[1,32,1024]{2,1,0:T(8,128)(2,1)} %param.9) | copy-start | bytes 196612
  6.9 5.8 %collective-permute-start.2 = (bf16[32,1024]{1,0:T(8,128)(2,1)S(1)}, bf16[32,1024]{1,0:T(8,128)(2,1)S(1)}, u32[]{:S(2)}, u32[]{:S(2)}) collective-permute-start(bf16[32,1024]{1,0:T(8,128)(2,1)S(1)} %bitcast.11), channel_id=1, source_target_pairs={{0,8},{1,9},{2,10},{3,11},{4,12},{5,13},{6,14},{7,15},{8,0},{9,1},... | collective-permute-start | bytes 196616 | tf_op jit(solution)/shard_map/ppermute | solution.py:403
  8.5 4.3 %collective-permute-start.3 = (bf16[32,1024]{1,0:T(8,128)(2,1)S(1)}, bf16[32,1024]{1,0:T(8,128)(2,1)S(1)}, u32[]{:S(2)}, u32[]{:S(2)}) collective-permute-start(bf16[32,1024]{1,0:T(8,128)(2,1)S(1)} %bitcast.10), channel_id=1, source_target_pairs={{0,9},{1,8},{2,11},{3,10},{4,13},{5,12},{6,15},{7,14},{8,1},{9,0},... | collective-permute-start | bytes 196616 | tf_op jit(solution)/shard_map/ppermute | solution.py:403
  8.6 8.5 %collective-permute-start.5 = (bf16[32,1024]{1,0:T(8,128)(2,1)S(1)}, bf16[32,1024]{1,0:T(8,128)(2,1)S(1)}, u32[]{:S(2)}, u32[]{:S(2)}) collective-permute-start(bf16[32,1024]{1,0:T(8,128)(2,1)S(1)} %bitcast.18), channel_id=1, source_target_pairs={{0,4},{1,5},{2,6},{3,7},{4,0},{5,1},{6,2},{7,3},{8,12},{9,13},{10,... | collective-permute-start | bytes 196616 | tf_op jit(solution)/shard_map/ppermute | solution.py:25
  8.6 8.5 %collective-permute-start.6 = (bf16[32,1024]{1,0:T(8,128)(2,1)S(1)}, bf16[32,1024]{1,0:T(8,128)(2,1)S(1)}, u32[]{:S(2)}, u32[]{:S(2)}) collective-permute-start(bf16[32,1024]{1,0:T(8,128)(2,1)S(1)} %bitcast.19), channel_id=1, source_target_pairs={{0,2},{1,3},{2,0},{3,1},{4,6},{5,7},{6,4},{7,5},{8,10},{9,11},{10,... | collective-permute-start | bytes 196616 | tf_op jit(solution)/shard_map/ppermute | solution.py:25
  13.4 6.3 %collective-permute-start.4 = (bf16[32,1152]{1,0:T(8,128)(2,1)S(1)}, bf16[32,1152]{1,0:T(8,128)(2,1)S(1)}, u32[]{:S(2)}, u32[]{:S(2)}) collective-permute-start(bf16[32,1152]{1,0:T(8,128)(2,1)S(1)} %attend.3.refs_9_), channel_id=1, source_target_pairs={{0,6},{1,7},{2,4},{3,5},{4,2},{5,3},{6,0},{7,1},{8,14},{9,15},{10,... | collective-permute-start | bytes 221192 | tf_op jit(solution)/shard_map/ppermute | solution.py:25
  18.1 5.7 %collective-permute-start.7 = (bf16[32,1152]{1,0:T(8,128)(2,1)S(1)}, bf16[32,1152]{1,0:T(8,128)(2,1)S(1)}, u32[]{:S(2)}, u32[]{:S(2)}) collective-permute-start(bf16[32,1152]{1,0:T(8,128)(2,1)S(1)} %get-tuple-element.29), channel_id=1, source_target_pairs={{0,4},{1,5},{2,6},{3,7},{4,0},{5,1},{6,2},{7,3},{8,12},{9,13},{10,... | collective-permute-start | bytes 221192 | tf_op jit(solution)/shard_map/ppermute | solution.py:25
  18.1 5.6 %collective-permute-start.8 = (bf16[32,1152]{1,0:T(8,128)(2,1)S(1)}, bf16[32,1152]{1,0:T(8,128)(2,1)S(1)}, u32[]{:S(2)}, u32[]{:S(2)}) collective-permute-start(bf16[32,1152]{1,0:T(8,128)(2,1)S(1)} %get-tuple-element.30), channel_id=1, source_target_pairs={{0,2},{1,3},{2,0},{3,1},{4,6},{5,7},{6,4},{7,5},{8,10},{9,11},{10,... | collective-permute-start | bytes 221192 | tf_op jit(solution)/shard_map/ppermute | solution.py:25
  25.5 1.6 %collective-permute-start.9 = (bf16[4,32,1024]{2,1,0:T(8,128)(2,1)S(1)}, bf16[4,32,1024]{2,1,0:T(8,128)(2,1)S(1)}, u32[]{:S(2)}, u32[]{:S(2)}) collective-permute-start(bf16[4,32,1024]{2,1,0:T(8,128)(2,1)S(1)} %get-tuple-element.35), channel_id=1, source_target_pairs={{0,1},{1,0},{2,3},{3,2},{4,5},{5,4},{6,7},{7,6},{8,9},{9,8},{10,11... | collective-permute-start | bytes 786440 | tf_op jit(solution)/shard_map/ppermute | solution.py:25
  26.4 10.4 %copy-start = (bf16[32,1024]{1,0:T(8,128)(2,1)S(1)}, bf16[32,1024]{1,0:T(8,128)(2,1)}, u32[]{:S(2)}) copy-start(bf16[32,1024]{1,0:T(8,128)(2,1)} %param.8) | copy-start | bytes 196612
  27.1 6.4 %collective-permute-start.10 = (bf16[32,1024]{1,0:T(8,128)(2,1)S(1)}, bf16[32,1024]{1,0:T(8,128)(2,1)S(1)}, u32[]{:S(2)}, u32[]{:S(2)}) collective-permute-start(bf16[32,1024]{1,0:T(8,128)(2,1)S(1)} %add_far.1.after), channel_id=1, source_target_pairs={{0,6},{1,7},{2,4},{3,5},{4,2},{5,3},{6,0},{7,1},{8,14},{9,15},{10,... | collective-permute-start | bytes 196616 | tf_op jit(solution)/shard_map/ppermute | solution.py:25
  31.0 5.3 %collective-permute-start.11 = (bf16[32,1024]{1,0:T(8,128)(2,1)S(1)}, bf16[32,1024]{1,0:T(8,128)(2,1)S(1)}, u32[]{:S(2)}, u32[]{:S(2)}) collective-permute-start(bf16[32,1024]{1,0:T(8,128)(2,1)S(1)} %get-tuple-element.37), channel_id=1, source_target_pairs={{0,4},{1,5},{2,6},{3,7},{4,0},{5,1},{6,2},{7,3},{8,12},{9,13},{10,... | collective-permute-start | bytes 196616 | tf_op jit(solution)/shard_map/ppermute | solution.py:25
  31.0 5.7 %collective-permute-start.12 = (bf16[32,1024]{1,0:T(8,128)(2,1)S(1)}, bf16[32,1024]{1,0:T(8,128)(2,1)S(1)}, u32[]{:S(2)}, u32[]{:S(2)}) collective-permute-start(bf16[32,1024]{1,0:T(8,128)(2,1)S(1)} %get-tuple-element.38), channel_id=1, source_target_pairs={{0,2},{1,3},{2,0},{3,1},{4,6},{5,7},{6,4},{7,5},{8,10},{9,11},{10,... | collective-permute-start | bytes 196616 | tf_op jit(solution)/shard_map/ppermute | solution.py:25
  36.8 4.3 %collective-permute-start.13 = (bf16[32,1024]{1,0:T(8,128)(2,1)S(1)}, bf16[32,1024]{1,0:T(8,128)(2,1)S(1)}, u32[]{:S(2)}, u32[]{:S(2)}) collective-permute-start(bf16[32,1024]{1,0:T(8,128)(2,1)S(1)} %add_convert_fusion.1), channel_id=1, source_target_pairs={{0,16},{16,0},{1,17},{17,1},{2,18},{18,2},{3,19},{19,3},{4,20},{20... | collective-permute-start | bytes 196616 | tf_op jit(solution)/shard_map/ppermute | solution.py:522

commit v4 on v3

--- a/solution.py
+++ b/solution.py
@@ -17,7 +17,7 @@
 LOG2E = 1.4426950408889634
 FACTOR = LOG2E / math.sqrt(HD)
 MEGA = 1024 * 1024
-LOAD_SHARES = (1, 3, 0, 0, 3, 1)
+LOAD_SHARES = (1, 1, 0, 1, 4, 1)
 
 
 def swapped(value, mask):

time: 42 us -> 40.8 us (0.971)
  waiting for transfers between devices: 9.63 us -> 8.54 us
    ppermute x11, waiting for transfers between devices: 6.88 us -> 4.54 us  [swapped(): lax.ppermute(value, 'tensor', [(source, source ^ mask) for source in rang...]
    pallas_call x1, Pallas kernels: 3.33 us -> 2.05 us  [local(): pl.pallas_call(functools.partial(prepare_kernel, (pages, page_tokens, cap...]
    ppermute x2, waiting for transfers between devices: 0.01 us -> 1.26 us  [local(): arrived.append(lax.ppermute(sent, ('inst', 'tensor'), pairs))]
    pallas_call x3, Pallas kernels: 4.55 us -> 5.74 us  [attend(): pl.pallas_call(functools.partial(attend_kernel, masks, weight_masks, len(...]
  transfers between devices with their start and end apart: 14 -> 14, of which waited for: 7 -> 6; matrix products, arithmetic and copies ran while one was open for 0% -> 0% of each run, Pallas kernels for 27% -> 28%
where the time goes in v4:
time: 40.8 us; the launch traced here: 40.6 us
  starting transfers between devices  18.2 us (45%)
  Pallas kernels  13.1 us (32%)
  waiting for transfers between devices  8.54 us (21%)
  other arithmetic  0.71 us (2%)
    ppermute x11, starting transfers between devices, swapped(): lax.ppermute(value, 'tensor', [(source, source ^ mask) for source in rang...  14.9 us
    pallas_call x3, Pallas kernels, attend(): pl.pallas_call(functools.partial(attend_kernel, masks, weight_masks, len(...  5.74 us
    ppermute x11, waiting for transfers between devices, swapped(): lax.ppermute(value, 'tensor', [(source, source ^ mask) for source in rang...  4.54 us
    ppermute x1, waiting for transfers between devices, local(): handed_over = lax.ppermute(after_first, 'section', [(0, 1), (1, 0)])  2.74 us
    pallas_call x1, Pallas kernels, local(): pl.pallas_call(functools.partial(prepare_kernel, (pages, page_tokens, cap...  2.05 us
    pallas_call x1, Pallas kernels, local(): pl.pallas_call(functools.partial(pick_kernel, capacity, loads[0]), out_sh...  1.85 us
    pallas_call x1, Pallas kernels, local(): pl.pallas_call(functools.partial(project_away_kernel, heads_per, half, fo...  1.75 us
    ppermute x2, starting transfers between devices, local(): arrived.append(lax.ppermute(sent, ('inst', 'tensor'), pairs))  1.64 us
  transfers between devices with their start and end apart: 14, of which 6 were waited for; matrix products, arithmetic and copies ran while one was open for 0% of the time, Pallas kernels for 28%

profile of v4, /device:TPU:0, one launch (start us, length us, event | category | flops | bytes accessed | tf_op | source)
XLA Modules:
  0.0 40.6 jit_solution(6247765692566236350)
XLA Ops:
  0.0 0.5 %collective-permute-start.1 = (bf16[256,2048]{1,0:T(8,128)(2,1)}, bf16[256,2048]{1,0:T(8,128)(2,1)S(1)}, u32[]{:S(2)}, u32[]{:S(2)}) collective-permute-start(bf16[256,2048]{1,0:T(8,128)(2,1)} %bitcast.12), channel_id=1, source_target_pairs={{0,1},{1,0},{2,3},{3,2},{4,5},{5,4},{6,7},{7,6},{8,9},{9,8},{10,11... | collective-permute-start | bytes 3145736 | tf_op jit(solution)/shard_map/ppermute | solution.py:25
  0.5 4.6 %collective-permute-start = (bf16[32,1024]{1,0:T(8,128)(2,1)}, bf16[32,1024]{1,0:T(8,128)(2,1)S(1)}, u32[]{:S(2)}, u32[]{:S(2)}) collective-permute-start(bf16[32,1024]{1,0:T(8,128)(2,1)} %bitcast.16), channel_id=1, source_target_pairs={{0,6},{1,7},{2,4},{3,5},{4,2},{5,3},{6,0},{7,1},{8,14},{9,15},{10,... | collective-permute-start | bytes 196616 | tf_op jit(solution)/shard_map/ppermute | solution.py:25
  5.1 1.9 %pick.1 = (bf16[1,32,1024]{2,1,0:T(8,128)(2,1)S(1)}, bf16[1,32,1024]{2,1,0:T(8,128)(2,1)S(1)}, bf16[1,1024,1024]{2,1,0:T(8,128)(2,1)S(1)}) custom-call(s32[2]{0:T(128)S(4)} %place.1.refs_0_, s32[2]{0:T(128)} %bitcast.21, bf16[8,32,2048]{2,1,0:T(8,128)(2,1)} %bitcast.13, bf16[1,1024,8192]{2,1,0:T(8,128)(2,1)} %refs_4_.1), custom_call_target="tpu_custom_call" | custom-call | tf_op jit(solution)/shard_map/pick/pallas_call | solution.py:374
  6.9 1.6 %collective-permute-start.2 = (bf16[32,1024]{1,0:T(8,128)(2,1)S(1)}, bf16[32,1024]{1,0:T(8,128)(2,1)S(1)}, u32[]{:S(2)}, u32[]{:S(2)}) collective-permute-start(bf16[32,1024]{1,0:T(8,128)(2,1)S(1)} %bitcast.11), channel_id=1, source_target_pairs={{0,8},{1,9},{2,10},{3,11},{4,12},{5,13},{6,14},{7,15},{8,0},{9,1},... | collective-permute-start | bytes 196616 | tf_op jit(solution)/shard_map/ppermute | solution.py:403
  8.5 0.1 collective-permute-start.3
  8.6 0.0 collective-permute-start.5
  8.6 0.0 collective-permute-done.refs_3_.refs_2_
  8.6 0.8 %collective-permute-start.6 = (bf16[32,1024]{1,0:T(8,128)(2,1)S(1)}, bf16[32,1024]{1,0:T(8,128)(2,1)S(1)}, u32[]{:S(2)}, u32[]{:S(2)}) collective-permute-start(bf16[32,1024]{1,0:T(8,128)(2,1)S(1)} %bitcast.19), channel_id=1, source_target_pairs={{0,2},{1,3},{2,0},{3,1},{4,6},{5,7},{6,4},{7,5},{8,10},{9,11},{10,... | collective-permute-start | bytes 196616 | tf_op jit(solution)/shard_map/ppermute | solution.py:25
  9.4 2.0 %prepare.1 = (f32[32,608]{1,0:T(8,128)S(1)}, bf16[32,1024]{1,0:T(8,128)(2,1)S(1)}, bf16[256,2048]{1,0:T(8,128)(2,1)S(1)}, bf16[32,2048]{1,0:T(8,128)(2,1)S(1)}, bf16[1,1024,1024]{2,1,0:T(8,128)(2,1)S(1)}) custom-call(s32[2]{0:T(128)S(4)} %place.1.refs_0_, s32[4,8]{1,0:T(4,128)} %bitcast.20, s32[8]{0:T(128)} %lengths_hbm.1, s32[2]{0:T(128)} %bitcast.22, ...), custom_call_target="tpu_custom_call" | custom-call | tf_op jit(solution)/shard_map/prepare/pallas_call | solution.py:409
  11.5 0.0 collective-permute-done.2.refs_5_.refs_6_
  11.5 1.3 %collective-permute-done.3.refs_6_.refs_7_ = bf16[32,1024]{1,0:T(8,128)(2,1)S(1)} collective-permute-done((bf16[32,1024]{1,0:T(8,128)(2,1)S(1)}, bf16[32,1024]{1,0:T(8,128)(2,1)S(1)}, u32[]{:S(2)}, u32[]{:S(2)}) %collective-permute-start.3) | collective-permute-done | bytes 65568 | tf_op jit(solution)/shard_map/ppermute | solution.py:403
  12.7 0.6 %attend.3.refs_9_ = bf16[32,1152]{1,0:T(8,128)(2,1)S(1)} custom-call(s32[2]{0:T(128)S(4)} %place.1.refs_0_, f32[32,608]{1,0:T(8,128)S(1)} %get-tuple-element.23.refs_1_, bf16[32,1024]{1,0:T(8,128)(2,1)S(1)} %collective-permute-done.refs_3_.refs_2_, bf16[256,2048]{1,0:T(8,128)(2,1)S(1)} %get-tuple-element.25.refs_3_.refs_4_, ...), custom_call_target="tpu_custom_call" | custom-call | tf_op jit(solution)/shard_map/attend/pallas_call | solution.py:443
  13.4 2.4 %collective-permute-start.4 = (bf16[32,1152]{1,0:T(8,128)(2,1)S(1)}, bf16[32,1152]{1,0:T(8,128)(2,1)S(1)}, u32[]{:S(2)}, u32[]{:S(2)}) collective-permute-start(bf16[32,1152]{1,0:T(8,128)(2,1)S(1)} %attend.3.refs_9_), channel_id=1, source_target_pairs={{0,6},{1,7},{2,4},{3,5},{4,2},{5,3},{6,0},{7,1},{8,14},{9,15},{10,... | collective-permute-start | bytes 221192 | tf_op jit(solution)/shard_map/ppermute | solution.py:25
  15.7 1.6 %attend.5 = (bf16[32,1152]{1,0:T(8,128)(2,1)S(1)}, bf16[32,1152]{1,0:T(8,128)(2,1)S(1)}, bf16[1,1024,1024]{2,1,0:T(8,128)(2,1)S(1)}) custom-call(s32[2]{0:T(128)S(4)} %place.1.refs_0_, f32[32,608]{1,0:T(8,128)S(1)} %get-tuple-element.23.refs_1_, bf16[32,1024]{1,0:T(8,128)(2,1)S(1)} %collective-permute-done.5.refs_2_, ...), custom_call_target="tpu_custom_call" | custom-call | tf_op jit(solution)/shard_map/attend/pallas_call | solution.py:443
  17.4 0.1 collective-permute-start.7
  17.4 2.1 %collective-permute-start.8 = (bf16[32,1152]{1,0:T(8,128)(2,1)S(1)}, bf16[32,1152]{1,0:T(8,128)(2,1)S(1)}, u32[]{:S(2)}, u32[]{:S(2)}) collective-permute-start(bf16[32,1152]{1,0:T(8,128)(2,1)S(1)} %get-tuple-element.31), channel_id=1, source_target_pairs={{0,2},{1,3},{2,0},{3,1},{4,6},{5,7},{6,4},{7,5},{8,10},{9,11},{10,... | collective-permute-start | bytes 221192 | tf_op jit(solution)/shard_map/ppermute | solution.py:25
  19.5 0.1 collective-permute-done.4.refs_8_.refs_1_
  19.6 3.5 %attend.4 = (bf16[32,1152]{1,0:T(8,128)(2,1)S(1)}, bf16[4,1024,1024]{2,1,0:T(8,128)(2,1)S(1)}) custom-call(s32[2]{0:T(128)S(4)} %place.1.refs_0_, f32[32,608]{1,0:T(8,128)S(1)} %get-tuple-element.23.refs_1_, bf16[32,1024]{1,0:T(8,128)(2,1)S(1)} %get-tuple-element.24.refs_2_, bf16[256,2048]{1,0:T(8,128)(2,1)S(1)} %get-tuple-element.25.refs_3_.refs_4_, ...), custom_call_target="tpu_custom_call" | custom-call | tf_op jit(solution)/shard_map/attend/pallas_call | solution.py:443
  23.2 0.0 collective-permute-done.8.refs_3_
  23.2 1.8 %project_away.1 = (bf16[4,32,1024]{2,1,0:T(8,128)(2,1)S(1)}, bf16[32,1024]{1,0:T(8,128)(2,1)S(1)}, bf16[1,1024,1024]{2,1,0:T(8,128)(2,1)S(1)}) custom-call(s32[2]{0:T(128)S(4)} %place.1.refs_0_, bf16[32,1152]{1,0:T(8,128)(2,1)S(1)} %get-tuple-element.29.refs_0_, bf16[32,1152]{1,0:T(8,128)(2,1)S(1)} %collective-permute-done.4.refs_8_.refs_1_, ...), custom_call_target="tpu_custom_call" | custom-call | tf_op jit(solution)/shard_map/project_away/pallas_call | solution.py:469
  25.0 0.1 collective-permute-start.9
  25.0 0.8 %project_home.1.home = f32[2,32,1024]{2,1,0:T(8,128)S(1)} custom-call(bf16[32,1024]{1,0:T(8,128)(2,1)S(1)} %get-tuple-element.36.attended, bf16[4,1024,1024]{2,1,0:T(8,128)(2,1)S(1)} %get-tuple-element.35.refs_8_.refs_0_), custom_call_target="tpu_custom_call" | custom-call | tf_op jit(solution)/shard_map/project_home/pallas_call | solution.py:485
  25.9 0.7 %collective-permute-done.9.sibling = bf16[4,32,1024]{2,1,0:T(8,128)(2,1)S(1)} collective-permute-done((bf16[4,32,1024]{2,1,0:T(8,128)(2,1)S(1)}, bf16[4,32,1024]{2,1,0:T(8,128)(2,1)S(1)}, u32[]{:S(2)}, u32[]{:S(2)}) %collective-permute-start.9) | collective-permute-done | bytes 262176 | tf_op jit(solution)/shard_map/ppermute | solution.py:25
  26.6 2.4 %collective-permute-start.10 = (bf16[32,1024]{1,0:T(8,128)(2,1)S(1)}, bf16[32,1024]{1,0:T(8,128)(2,1)S(1)}, u32[]{:S(2)}, u32[]{:S(2)}) collective-permute-start(bf16[32,1024]{1,0:T(8,128)(2,1)S(1)} %add_far.1.after), channel_id=1, source_target_pairs={{0,6},{1,7},{2,4},{3,5},{4,2},{5,3},{6,0},{7,1},{8,14},{9,15},{10,... | collective-permute-start | bytes 196616 | tf_op jit(solution)/shard_map/ppermute | solution.py:25
  29.0 0.8 %project_near.1 = (bf16[32,1024]{1,0:T(8,128)(2,1)S(1)}, bf16[32,1024]{1,0:T(8,128)(2,1)S(1)}) custom-call(bf16[32,1024]{1,0:T(8,128)(2,1)S(1)} %get-tuple-element.36.attended, bf16[4,32,1024]{2,1,0:T(8,128)(2,1)S(1)} %collective-permute-done.9.sibling, bf16[32,1024]{1,0:T(8,128)(2,1)S(1)} %add_far.1.after, ...), custom_call_target="tpu_custom_call" | custom-call | tf_op jit(solution)/shard_map/project_near/pallas_call | solution.py:503
  29.8 0.0 collective-permute-start.11
  29.9 2.0 %collective-permute-start.12 = (bf16[32,1024]{1,0:T(8,128)(2,1)S(1)}, bf16[32,1024]{1,0:T(8,128)(2,1)S(1)}, u32[]{:S(2)}, u32[]{:S(2)}) collective-permute-start(bf16[32,1024]{1,0:T(8,128)(2,1)S(1)} %get-tuple-element.40), channel_id=1, source_target_pairs={{0,2},{1,3},{2,0},{3,1},{4,6},{5,7},{6,4},{7,5},{8,10},{9,11},{10,... | collective-permute-start | bytes 196616 | tf_op jit(solution)/shard_map/ppermute | solution.py:25
  31.9 1.2 %collective-permute-done.10.far = bf16[32,1024]{1,0:T(8,128)(2,1)S(1)} collective-permute-done((bf16[32,1024]{1,0:T(8,128)(2,1)S(1)}, bf16[32,1024]{1,0:T(8,128)(2,1)S(1)}, u32[]{:S(2)}, u32[]{:S(2)}) %collective-permute-start.10) | collective-permute-done | bytes 65568 | tf_op jit(solution)/shard_map/ppermute | solution.py:25
  33.1 2.4 %collective-permute-done.11 = bf16[32,1024]{1,0:T(8,128)(2,1)S(1)} collective-permute-done((bf16[32,1024]{1,0:T(8,128)(2,1)S(1)}, bf16[32,1024]{1,0:T(8,128)(2,1)S(1)}, u32[]{:S(2)}, u32[]{:S(2)}) %collective-permute-start.11) | collective-permute-done | bytes 65568 | tf_op jit(solution)/shard_map/ppermute | solution.py:25
  35.6 1.6 %collective-permute-start.13 = (bf16[32,1024]{1,0:T(8,128)(2,1)S(1)}, bf16[32,1024]{1,0:T(8,128)(2,1)S(1)}, u32[]{:S(2)}, u32[]{:S(2)}) collective-permute-start(bf16[32,1024]{1,0:T(8,128)(2,1)S(1)} %add_convert_fusion.1), channel_id=1, source_target_pairs={{0,16},{16,0},{1,17},{17,1},{2,18},{18,2},{3,19},{19,3},{4,20},{20... | collective-permute-start | bytes 196616 | tf_op jit(solution)/shard_map/ppermute | solution.py:522
  37.2 2.7 %collective-permute-done.13 = bf16[32,1024]{1,0:T(8,128)(2,1)S(1)} collective-permute-done((bf16[32,1024]{1,0:T(8,128)(2,1)S(1)}, bf16[32,1024]{1,0:T(8,128)(2,1)S(1)}, u32[]{:S(2)}, u32[]{:S(2)}) %collective-permute-start.13) | collective-permute-done | bytes 65568 | tf_op jit(solution)/shard_map/ppermute | solution.py:522
  39.9 0.7 %fusion.1 = bf16[1,32,1024]{2,1,0:T(8,128)(2,1)} fusion(bf16[32,1024]{1,0:T(8,128)(2,1)S(1)} %collective-permute-done.13, pred[]{:T(512)S(6)} %eq.3, bf16[32,1024]{1,0:T(8,128)(2,1)S(1)} %collective-permute-done.12, f32[32,1024]{1,0:T(8,128)S(1)} %add_own.1, bf16[32,1024]{1,0:T(8,128)(2,1)S(1)} %collective-permute-done.11, bf16[32,1024]{1,0:T(8,128)(2,1)S(1)} %copy-done), kind=kLoop, calls=%fused_computation.4 | loop fusion | flops 360448 | bytes 458753 | tf_op jit(solution)/shard_map/broadcast_in_dim | solution.py:525
  (13 shorter events, 0.1 us)
Async XLA Ops:
  0.0 12.7 %collective-permute-start.1 = (bf16[256,2048]{1,0:T(8,128)(2,1)}, bf16[256,2048]{1,0:T(8,128)(2,1)S(1)}, u32[]{:S(2)}, u32[]{:S(2)}) collective-permute-start(bf16[256,2048]{1,0:T(8,128)(2,1)} %bitcast.12), channel_id=1, source_target_pairs={{0,1},{1,0},{2,3},{3,2},{4,5},{5,4},{6,7},{7,6},{8,9},{9,8},{10,11... | collective-permute-start | bytes 3145736 | tf_op jit(solution)/shard_map/ppermute | solution.py:25
  0.5 8.1 %collective-permute-start = (bf16[32,1024]{1,0:T(8,128)(2,1)}, bf16[32,1024]{1,0:T(8,128)(2,1)S(1)}, u32[]{:S(2)}, u32[]{:S(2)}) collective-permute-start(bf16[32,1024]{1,0:T(8,128)(2,1)} %bitcast.16), channel_id=1, source_target_pairs={{0,6},{1,7},{2,4},{3,5},{4,2},{5,3},{6,0},{7,1},{8,14},{9,15},{10,... | collective-permute-start | bytes 196616 | tf_op jit(solution)/shard_map/ppermute | solution.py:25
  5.1 3.5 %copy-start.1 = (bf16[1,32,1024]{2,1,0:T(8,128)(2,1)S(1)}, bf16[1,32,1024]{2,1,0:T(8,128)(2,1)}, u32[]{:S(2)}) copy-start(bf16[1,32,1024]{2,1,0:T(8,128)(2,1)} %param.9) | copy-start | bytes 196612
  6.9 4.6 %collective-permute-start.2 = (bf16[32,1024]{1,0:T(8,128)(2,1)S(1)}, bf16[32,1024]{1,0:T(8,128)(2,1)S(1)}, u32[]{:S(2)}, u32[]{:S(2)}) collective-permute-start(bf16[32,1024]{1,0:T(8,128)(2,1)S(1)} %bitcast.11), channel_id=1, source_target_pairs={{0,8},{1,9},{2,10},{3,11},{4,12},{5,13},{6,14},{7,15},{8,0},{9,1},... | collective-permute-start | bytes 196616 | tf_op jit(solution)/shard_map/ppermute | solution.py:403
  8.5 4.3 %collective-permute-start.3 = (bf16[32,1024]{1,0:T(8,128)(2,1)S(1)}, bf16[32,1024]{1,0:T(8,128)(2,1)S(1)}, u32[]{:S(2)}, u32[]{:S(2)}) collective-permute-start(bf16[32,1024]{1,0:T(8,128)(2,1)S(1)} %bitcast.10), channel_id=1, source_target_pairs={{0,9},{1,8},{2,11},{3,10},{4,13},{5,12},{6,15},{7,14},{8,1},{9,0},... | collective-permute-start | bytes 196616 | tf_op jit(solution)/shard_map/ppermute | solution.py:403
  8.6 7.2 %collective-permute-start.5 = (bf16[32,1024]{1,0:T(8,128)(2,1)S(1)}, bf16[32,1024]{1,0:T(8,128)(2,1)S(1)}, u32[]{:S(2)}, u32[]{:S(2)}) collective-permute-start(bf16[32,1024]{1,0:T(8,128)(2,1)S(1)} %bitcast.18), channel_id=1, source_target_pairs={{0,4},{1,5},{2,6},{3,7},{4,0},{5,1},{6,2},{7,3},{8,12},{9,13},{10,... | collective-permute-start | bytes 196616 | tf_op jit(solution)/shard_map/ppermute | solution.py:25
  8.6 7.2 %collective-permute-start.6 = (bf16[32,1024]{1,0:T(8,128)(2,1)S(1)}, bf16[32,1024]{1,0:T(8,128)(2,1)S(1)}, u32[]{:S(2)}, u32[]{:S(2)}) collective-permute-start(bf16[32,1024]{1,0:T(8,128)(2,1)S(1)} %bitcast.19), channel_id=1, source_target_pairs={{0,2},{1,3},{2,0},{3,1},{4,6},{5,7},{6,4},{7,5},{8,10},{9,11},{10,... | collective-permute-start | bytes 196616 | tf_op jit(solution)/shard_map/ppermute | solution.py:25
  13.4 6.3 %collective-permute-start.4 = (bf16[32,1152]{1,0:T(8,128)(2,1)S(1)}, bf16[32,1152]{1,0:T(8,128)(2,1)S(1)}, u32[]{:S(2)}, u32[]{:S(2)}) collective-permute-start(bf16[32,1152]{1,0:T(8,128)(2,1)S(1)} %attend.3.refs_9_), channel_id=1, source_target_pairs={{0,6},{1,7},{2,4},{3,5},{4,2},{5,3},{6,0},{7,1},{8,14},{9,15},{10,... | collective-permute-start | bytes 221192 | tf_op jit(solution)/shard_map/ppermute | solution.py:25
  17.4 5.8 %collective-permute-start.7 = (bf16[32,1152]{1,0:T(8,128)(2,1)S(1)}, bf16[32,1152]{1,0:T(8,128)(2,1)S(1)}, u32[]{:S(2)}, u32[]{:S(2)}) collective-permute-start(bf16[32,1152]{1,0:T(8,128)(2,1)S(1)} %get-tuple-element.30), channel_id=1, source_target_pairs={{0,4},{1,5},{2,6},{3,7},{4,0},{5,1},{6,2},{7,3},{8,12},{9,13},{10,... | collective-permute-start | bytes 221192 | tf_op jit(solution)/shard_map/ppermute | solution.py:25
  17.4 5.7 %collective-permute-start.8 = (bf16[32,1152]{1,0:T(8,128)(2,1)S(1)}, bf16[32,1152]{1,0:T(8,128)(2,1)S(1)}, u32[]{:S(2)}, u32[]{:S(2)}) collective-permute-start(bf16[32,1152]{1,0:T(8,128)(2,1)S(1)} %get-tuple-element.31), channel_id=1, source_target_pairs={{0,2},{1,3},{2,0},{3,1},{4,6},{5,7},{6,4},{7,5},{8,10},{9,11},{10,... | collective-permute-start | bytes 221192 | tf_op jit(solution)/shard_map/ppermute | solution.py:25
  25.0 1.6 %collective-permute-start.9 = (bf16[4,32,1024]{2,1,0:T(8,128)(2,1)S(1)}, bf16[4,32,1024]{2,1,0:T(8,128)(2,1)S(1)}, u32[]{:S(2)}, u32[]{:S(2)}) collective-permute-start(bf16[4,32,1024]{2,1,0:T(8,128)(2,1)S(1)} %get-tuple-element.37), channel_id=1, source_target_pairs={{0,1},{1,0},{2,3},{3,2},{4,5},{5,4},{6,7},{7,6},{8,9},{9,8},{10,11... | collective-permute-start | bytes 786440 | tf_op jit(solution)/shard_map/ppermute | solution.py:25
  26.6 6.5 %collective-permute-start.10 = (bf16[32,1024]{1,0:T(8,128)(2,1)S(1)}, bf16[32,1024]{1,0:T(8,128)(2,1)S(1)}, u32[]{:S(2)}, u32[]{:S(2)}) collective-permute-start(bf16[32,1024]{1,0:T(8,128)(2,1)S(1)} %add_far.1.after), channel_id=1, source_target_pairs={{0,6},{1,7},{2,4},{3,5},{4,2},{5,3},{6,0},{7,1},{8,14},{9,15},{10,... | collective-permute-start | bytes 196616 | tf_op jit(solution)/shard_map/ppermute | solution.py:25
  29.0 6.5 %copy-start = (bf16[32,1024]{1,0:T(8,128)(2,1)S(1)}, bf16[32,1024]{1,0:T(8,128)(2,1)}, u32[]{:S(2)}) copy-start(bf16[32,1024]{1,0:T(8,128)(2,1)} %param.8) | copy-start | bytes 196612
  29.8 5.7 %collective-permute-start.11 = (bf16[32,1024]{1,0:T(8,128)(2,1)S(1)}, bf16[32,1024]{1,0:T(8,128)(2,1)S(1)}, u32[]{:S(2)}, u32[]{:S(2)}) collective-permute-start(bf16[32,1024]{1,0:T(8,128)(2,1)S(1)} %get-tuple-element.39), channel_id=1, source_target_pairs={{0,4},{1,5},{2,6},{3,7},{4,0},{5,1},{6,2},{7,3},{8,12},{9,13},{10,... | collective-permute-start | bytes 196616 | tf_op jit(solution)/shard_map/ppermute | solution.py:25
  29.9 5.7 %collective-permute-start.12 = (bf16[32,1024]{1,0:T(8,128)(2,1)S(1)}, bf16[32,1024]{1,0:T(8,128)(2,1)S(1)}, u32[]{:S(2)}, u32[]{:S(2)}) collective-permute-start(bf16[32,1024]{1,0:T(8,128)(2,1)S(1)} %get-tuple-element.40), channel_id=1, source_target_pairs={{0,2},{1,3},{2,0},{3,1},{4,6},{5,7},{6,4},{7,5},{8,10},{9,11},{10,... | collective-permute-start | bytes 196616 | tf_op jit(solution)/shard_map/ppermute | solution.py:25
  35.6 4.3 %collective-permute-start.13 = (bf16[32,1024]{1,0:T(8,128)(2,1)S(1)}, bf16[32,1024]{1,0:T(8,128)(2,1)S(1)}, u32[]{:S(2)}, u32[]{:S(2)}) collective-permute-start(bf16[32,1024]{1,0:T(8,128)(2,1)S(1)} %add_convert_fusion.1), channel_id=1, source_target_pairs={{0,16},{16,0},{1,17},{17,1},{2,18},{18,2},{3,19},{19,3},{4,20},{20... | collective-permute-start | bytes 196616 | tf_op jit(solution)/shard_map/ppermute | solution.py:522

commit v5 on v4

--- a/solution.py
+++ b/solution.py
@@ -292,22 +292,25 @@
     project(attended[...], refs[:-1], found, refs[-1])
 
 
-def add_far_kernel(home, sibling, out):
-    out[...] = (home[1] + sibling[1].astype(jnp.float32)).astype(out.dtype)
-
-
-def add_own_kernel(home, sibling, far, out):
-    own = home[0] + sibling[0].astype(jnp.float32)
-    out[...] = own + far[...].astype(jnp.float32)
-
-
-def project_near_kernel(found, attended, sibling, after, *refs):
+def add_far_kernel(home, sibling, *outputs):
+    for at, out in enumerate(outputs):
+        out[...] = (home[at] + sibling[at].astype(jnp.float32)).astype(out.dtype)
+
+
+def project_near_kernel(found, first, attended, sibling, after, *refs):
     weights, outputs = refs[: len(refs) - len(found)], refs[len(refs) - len(found) :]
     rows = attended[...]
     for at, (array, block) in enumerate(found):
         product = jnp.dot(rows, weights[array][block], preferred_element_type=jnp.float32)
-        total = product + sibling[at + 2].astype(jnp.float32)
+        total = product + sibling[first + at].astype(jnp.float32)
         outputs[at][...] = total.astype(outputs[at].dtype)
+
+
+def add_own_kernel(own, *refs):
+    total = own[...]
+    for received in refs[:-1]:
+        total = total + received[...].astype(jnp.float32)
+    refs[-1][...] = total
 
 
 def local(hidden_in, queries, new_kv, kv_pages, out_weight, move_pages, page_table, lengths):
@@ -331,9 +334,11 @@
 
     if len(peers) == 4:
         peers = [0, 6, 4, 2]
-    home_masks = [2 * mask for mask in range(half)]
+    far = half // 2
+    home_masks = list(range(2, tensor_count, 2))
     if half == 4:
-        home_masks = [0, 6, 4, 2]
+        home_masks = [6, 4, 2]
+    home_masks.insert(far, 0)
     away_masks = [mask ^ 1 for mask in home_masks]
     unit = tensor_count // 8
     loads, filled = [], 0
@@ -481,42 +486,54 @@
     )(place, *received, *[weight] * loading, *away_weights)
     moved_weights.extend(moved)
     sibling = swapped(away, 1)
-    home_weights, found = weight_parts(home_masks[:2])
+    home_weights, found = weight_parts(home_masks[:far])
     home = pl.pallas_call(
         functools.partial(project_home_kernel, found),
         in_specs=[vmem] * (1 + len(home_weights)),
         out_specs=vmem,
-        out_shape=jax.ShapeDtypeStruct((2, rows, chunk), jnp.float32),
+        out_shape=jax.ShapeDtypeStruct((far, rows, chunk), jnp.float32),
         compiler_params=project_params,
-        name="project_home",
+        name="project_far",
     )(attended, *home_weights)
+    add_params = pltpu.CompilerParams(vmem_limit_bytes=2 * MEGA)
+    own_shape = jax.ShapeDtypeStruct((rows, chunk), jnp.float32)
     sum_shape = jax.ShapeDtypeStruct((rows, chunk), jnp.bfloat16)
-    far_sum = pl.pallas_call(
+    far_sums = pl.pallas_call(
         add_far_kernel,
         in_specs=[vmem] * 2,
-        out_specs=vmem,
-        out_shape=sum_shape,
-        compiler_params=pltpu.CompilerParams(vmem_limit_bytes=2 * MEGA),
+        out_specs=[vmem] * far,
+        out_shape=[sum_shape] * far,
+        compiler_params=add_params,
         name="add_far",
     )(home, sibling)
-    home_weights, found = weight_parts(home_masks[2:])
+    home_weights, found = weight_parts(home_masks[far + 1 :])
     near_sums = pl.pallas_call(
-        functools.partial(project_near_kernel, found),
+        functools.partial(project_near_kernel, found, far + 1),
         in_specs=[vmem] * (3 + len(home_weights)),
-        out_specs=[vmem] * (half - 2),
-        out_shape=[sum_shape] * (half - 2),
+        out_specs=[vmem] * len(found),
+        out_shape=[sum_shape] * len(found),
         compiler_params=project_params,
         name="project_near",
-    )(attended, sibling, far_sum, *home_weights)
+    )(attended, sibling, far_sums[0], *home_weights)
+    home_weights, found = weight_parts(home_masks[far : far + 1])
+    (own,) = pl.pallas_call(
+        functools.partial(project_near_kernel, found, far),
+        in_specs=[vmem] * (3 + len(home_weights)),
+        out_specs=[vmem],
+        out_shape=[own_shape],
+        compiler_params=project_params,
+        name="project_own",
+    )(attended, sibling, near_sums[0], *home_weights)
+    received = [swapped(total, mask) for mask, total in zip(home_masks, far_sums)]
     projected = pl.pallas_call(
         add_own_kernel,
-        in_specs=[vmem] * 3,
+        in_specs=[vmem] * (1 + far),
         out_specs=vmem,
-        out_shape=jax.ShapeDtypeStruct((rows, chunk), jnp.float32),
-        compiler_params=pltpu.CompilerParams(vmem_limit_bytes=2 * MEGA),
+        out_shape=own_shape,
+        compiler_params=add_params,
         name="add_own",
-    )(home, sibling, swapped(far_sum, home_masks[1]))
-    for mask, total in zip(home_masks[2:], near_sums):
+    )(own, *received)
+    for mask, total in zip(home_masks[far + 1 :], near_sums):
         projected = projected + swapped(total, mask).astype(jnp.float32)
     after_first = (hidden_in.astype(jnp.float32) + projected).astype(jnp.bfloat16)
     handed_over = lax.ppermute(after_first, "section", [(0, 1), (1, 0)])

time: 40.8 us -> 40.8 us (level)
    pallas_call x3 -> x4, Pallas kernels: 0.86 us -> 0.97 us  [the longest x1 0.46 us: local(): pl.pallas_call(functools.partial(project_near_kernel, found, far + 1), in...]
where the time goes in v5:
time: 40.8 us; the launch traced here: 40.6 us
  starting transfers between devices  18.2 us (45%)
  Pallas kernels  13.2 us (32%)
  waiting for transfers between devices  8.36 us (20%)
  other arithmetic  0.69 us (2%)
    ppermute x11, starting transfers between devices, swapped(): lax.ppermute(value, 'tensor', [(source, source ^ mask) for source in rang...  15 us
    pallas_call x3, Pallas kernels, attend(): pl.pallas_call(functools.partial(attend_kernel, masks, weight_masks, len(...  5.74 us
    ppermute x11, waiting for transfers between devices, swapped(): lax.ppermute(value, 'tensor', [(source, source ^ mask) for source in rang...  4.36 us
    ppermute x1, waiting for transfers between devices, local(): handed_over = lax.ppermute(after_first, 'section', [(0, 1), (1, 0)])  2.74 us
    pallas_call x1, Pallas kernels, local(): pl.pallas_call(functools.partial(prepare_kernel, (pages, page_tokens, cap...  2.05 us
    pallas_call x1, Pallas kernels, local(): pl.pallas_call(functools.partial(pick_kernel, capacity, loads[0]), out_sh...  1.85 us
    pallas_call x1, Pallas kernels, local(): pl.pallas_call(functools.partial(project_away_kernel, heads_per, half, fo...  1.75 us
    ppermute x2, starting transfers between devices, local(): arrived.append(lax.ppermute(sent, ('inst', 'tensor'), pairs))  1.64 us
  transfers between devices with their start and end apart: 14, of which 6 were waited for; matrix products, arithmetic and copies ran while one was open for 0% of the time, Pallas kernels for 28%

profile of v5, /device:TPU:0, one launch (start us, length us, event | category | flops | bytes accessed | tf_op | source)
XLA Modules:
  0.0 40.6 jit_solution(6485202971933118913)
XLA Ops:
  0.0 0.5 %collective-permute-start.1 = (bf16[256,2048]{1,0:T(8,128)(2,1)}, bf16[256,2048]{1,0:T(8,128)(2,1)S(1)}, u32[]{:S(2)}, u32[]{:S(2)}) collective-permute-start(bf16[256,2048]{1,0:T(8,128)(2,1)} %bitcast.12), channel_id=1, source_target_pairs={{0,1},{1,0},{2,3},{3,2},{4,5},{5,4},{6,7},{7,6},{8,9},{9,8},{10,11... | collective-permute-start | bytes 3145736 | tf_op jit(solution)/shard_map/ppermute | solution.py:25
  0.5 4.6 %collective-permute-start = (bf16[32,1024]{1,0:T(8,128)(2,1)}, bf16[32,1024]{1,0:T(8,128)(2,1)S(1)}, u32[]{:S(2)}, u32[]{:S(2)}) collective-permute-start(bf16[32,1024]{1,0:T(8,128)(2,1)} %bitcast.16), channel_id=1, source_target_pairs={{0,6},{1,7},{2,4},{3,5},{4,2},{5,3},{6,0},{7,1},{8,14},{9,15},{10,... | collective-permute-start | bytes 196616 | tf_op jit(solution)/shard_map/ppermute | solution.py:25
  5.1 1.9 %pick.1 = (bf16[1,32,1024]{2,1,0:T(8,128)(2,1)S(1)}, bf16[1,32,1024]{2,1,0:T(8,128)(2,1)S(1)}, bf16[1,1024,1024]{2,1,0:T(8,128)(2,1)S(1)}) custom-call(s32[2]{0:T(128)S(4)} %place.1.refs_0_, s32[2]{0:T(128)} %bitcast.21, bf16[8,32,2048]{2,1,0:T(8,128)(2,1)} %bitcast.13, bf16[1,1024,8192]{2,1,0:T(8,128)(2,1)} %refs_4_.1), custom_call_target="tpu_custom_call" | custom-call | tf_op jit(solution)/shard_map/pick/pallas_call | solution.py:379
  6.9 1.6 %collective-permute-start.2 = (bf16[32,1024]{1,0:T(8,128)(2,1)S(1)}, bf16[32,1024]{1,0:T(8,128)(2,1)S(1)}, u32[]{:S(2)}, u32[]{:S(2)}) collective-permute-start(bf16[32,1024]{1,0:T(8,128)(2,1)S(1)} %bitcast.11), channel_id=1, source_target_pairs={{0,8},{1,9},{2,10},{3,11},{4,12},{5,13},{6,14},{7,15},{8,0},{9,1},... | collective-permute-start | bytes 196616 | tf_op jit(solution)/shard_map/ppermute | solution.py:408
  8.5 0.1 collective-permute-start.3
  8.6 0.0 collective-permute-start.5
  8.6 0.0 collective-permute-done.refs_3_.refs_2_
  8.6 0.8 %collective-permute-start.6 = (bf16[32,1024]{1,0:T(8,128)(2,1)S(1)}, bf16[32,1024]{1,0:T(8,128)(2,1)S(1)}, u32[]{:S(2)}, u32[]{:S(2)}) collective-permute-start(bf16[32,1024]{1,0:T(8,128)(2,1)S(1)} %bitcast.19), channel_id=1, source_target_pairs={{0,2},{1,3},{2,0},{3,1},{4,6},{5,7},{6,4},{7,5},{8,10},{9,11},{10,... | collective-permute-start | bytes 196616 | tf_op jit(solution)/shard_map/ppermute | solution.py:25
  9.4 2.0 %prepare.1 = (f32[32,608]{1,0:T(8,128)S(1)}, bf16[32,1024]{1,0:T(8,128)(2,1)S(1)}, bf16[256,2048]{1,0:T(8,128)(2,1)S(1)}, bf16[32,2048]{1,0:T(8,128)(2,1)S(1)}, bf16[1,1024,1024]{2,1,0:T(8,128)(2,1)S(1)}) custom-call(s32[2]{0:T(128)S(4)} %place.1.refs_0_, s32[4,8]{1,0:T(4,128)} %bitcast.20, s32[8]{0:T(128)} %lengths_hbm.1, s32[2]{0:T(128)} %bitcast.22, ...), custom_call_target="tpu_custom_call" | custom-call | tf_op jit(solution)/shard_map/prepare/pallas_call | solution.py:414
  11.5 1.3 %collective-permute-done.3.refs_6_.refs_7_ = bf16[32,1024]{1,0:T(8,128)(2,1)S(1)} collective-permute-done((bf16[32,1024]{1,0:T(8,128)(2,1)S(1)}, bf16[32,1024]{1,0:T(8,128)(2,1)S(1)}, u32[]{:S(2)}, u32[]{:S(2)}) %collective-permute-start.3) | collective-permute-done | bytes 65568 | tf_op jit(solution)/shard_map/ppermute | solution.py:408
  12.7 0.0 collective-permute-done.1.refs_4_.refs_5_
  12.7 0.6 %attend.3.refs_9_ = bf16[32,1152]{1,0:T(8,128)(2,1)S(1)} custom-call(s32[2]{0:T(128)S(4)} %place.1.refs_0_, f32[32,608]{1,0:T(8,128)S(1)} %get-tuple-element.23.refs_1_, bf16[32,1024]{1,0:T(8,128)(2,1)S(1)} %collective-permute-done.refs_3_.refs_2_, bf16[256,2048]{1,0:T(8,128)(2,1)S(1)} %get-tuple-element.25.refs_3_.refs_4_, ...), custom_call_target="tpu_custom_call" | custom-call | tf_op jit(solution)/shard_map/attend/pallas_call | solution.py:448
  13.4 2.4 %collective-permute-start.4 = (bf16[32,1152]{1,0:T(8,128)(2,1)S(1)}, bf16[32,1152]{1,0:T(8,128)(2,1)S(1)}, u32[]{:S(2)}, u32[]{:S(2)}) collective-permute-start(bf16[32,1152]{1,0:T(8,128)(2,1)S(1)} %attend.3.refs_9_), channel_id=1, source_target_pairs={{0,6},{1,7},{2,4},{3,5},{4,2},{5,3},{6,0},{7,1},{8,14},{9,15},{10,... | collective-permute-start | bytes 221192 | tf_op jit(solution)/shard_map/ppermute | solution.py:25
  15.7 1.6 %attend.5 = (bf16[32,1152]{1,0:T(8,128)(2,1)S(1)}, bf16[32,1152]{1,0:T(8,128)(2,1)S(1)}, bf16[1,1024,1024]{2,1,0:T(8,128)(2,1)S(1)}) custom-call(s32[2]{0:T(128)S(4)} %place.1.refs_0_, f32[32,608]{1,0:T(8,128)S(1)} %get-tuple-element.23.refs_1_, bf16[32,1024]{1,0:T(8,128)(2,1)S(1)} %collective-permute-done.5.refs_2_, ...), custom_call_target="tpu_custom_call" | custom-call | tf_op jit(solution)/shard_map/attend/pallas_call | solution.py:448
  17.4 0.1 collective-permute-start.7
  17.4 2.1 %collective-permute-start.8 = (bf16[32,1152]{1,0:T(8,128)(2,1)S(1)}, bf16[32,1152]{1,0:T(8,128)(2,1)S(1)}, u32[]{:S(2)}, u32[]{:S(2)}) collective-permute-start(bf16[32,1152]{1,0:T(8,128)(2,1)S(1)} %get-tuple-element.31), channel_id=1, source_target_pairs={{0,2},{1,3},{2,0},{3,1},{4,6},{5,7},{6,4},{7,5},{8,10},{9,11},{10,... | collective-permute-start | bytes 221192 | tf_op jit(solution)/shard_map/ppermute | solution.py:25
  19.5 0.1 collective-permute-done.4.refs_8_.refs_1_
  19.6 3.5 %attend.4 = (bf16[32,1152]{1,0:T(8,128)(2,1)S(1)}, bf16[4,1024,1024]{2,1,0:T(8,128)(2,1)S(1)}) custom-call(s32[2]{0:T(128)S(4)} %place.1.refs_0_, f32[32,608]{1,0:T(8,128)S(1)} %get-tuple-element.23.refs_1_, bf16[32,1024]{1,0:T(8,128)(2,1)S(1)} %get-tuple-element.24.refs_2_, bf16[256,2048]{1,0:T(8,128)(2,1)S(1)} %get-tuple-element.25.refs_3_.refs_4_, ...), custom_call_target="tpu_custom_call" | custom-call | tf_op jit(solution)/shard_map/attend/pallas_call | solution.py:448
  23.2 0.0 collective-permute-done.8.refs_3_
  23.2 1.8 %project_away.1 = (bf16[4,32,1024]{2,1,0:T(8,128)(2,1)S(1)}, bf16[32,1024]{1,0:T(8,128)(2,1)S(1)}, bf16[1,1024,1024]{2,1,0:T(8,128)(2,1)S(1)}) custom-call(s32[2]{0:T(128)S(4)} %place.1.refs_0_, bf16[32,1152]{1,0:T(8,128)(2,1)S(1)} %get-tuple-element.29.refs_0_, bf16[32,1152]{1,0:T(8,128)(2,1)S(1)} %collective-permute-done.4.refs_8_.refs_1_, ...), custom_call_target="tpu_custom_call" | custom-call | tf_op jit(solution)/shard_map/project_away/pallas_call | solution.py:474
  25.0 0.1 collective-permute-start.9
  25.0 0.8 %project_far.1.home = f32[2,32,1024]{2,1,0:T(8,128)S(1)} custom-call(bf16[32,1024]{1,0:T(8,128)(2,1)S(1)} %get-tuple-element.36.attended, bf16[4,1024,1024]{2,1,0:T(8,128)(2,1)S(1)} %get-tuple-element.35.refs_8_.refs_0_), custom_call_target="tpu_custom_call" | custom-call | tf_op jit(solution)/shard_map/project_far/pallas_call | solution.py:490
  25.9 0.7 %collective-permute-done.9.sibling = bf16[4,32,1024]{2,1,0:T(8,128)(2,1)S(1)} collective-permute-done((bf16[4,32,1024]{2,1,0:T(8,128)(2,1)S(1)}, bf16[4,32,1024]{2,1,0:T(8,128)(2,1)S(1)}, u32[]{:S(2)}, u32[]{:S(2)}) %collective-permute-start.9) | collective-permute-done | bytes 262176 | tf_op jit(solution)/shard_map/ppermute | solution.py:25
  26.6 2.4 %collective-permute-start.10 = (bf16[32,1024]{1,0:T(8,128)(2,1)S(1)}, bf16[32,1024]{1,0:T(8,128)(2,1)S(1)}, u32[]{:S(2)}, u32[]{:S(2)}) collective-permute-start(bf16[32,1024]{1,0:T(8,128)(2,1)S(1)} %get-tuple-element.38.after), channel_id=1, source_target_pairs={{0,6},{1,7},{2,4},{3,5},{4,2},{5,3},{6,0},{7,1},{8,14},{9,15},{10,... | collective-permute-start | bytes 196616 | tf_op jit(solution)/shard_map/ppermute | solution.py:25
  29.0 0.5 %project_near.1.after = bf16[32,1024]{1,0:T(8,128)(2,1)S(1)} custom-call(bf16[32,1024]{1,0:T(8,128)(2,1)S(1)} %get-tuple-element.36.attended, bf16[4,32,1024]{2,1,0:T(8,128)(2,1)S(1)} %collective-permute-done.9.sibling, bf16[32,1024]{1,0:T(8,128)(2,1)S(1)} %get-tuple-element.38.after, bf16[1,1024,1024]{2,1,0:T(8,128)(2,1)S(1)} %get-tuple-element.39.refs_0_), custom_call_target="tpu_custom_call" | custom-call | tf_op jit(solution)/shard_map/project_near/pallas_call | solution.py:510
  29.5 2.1 %collective-permute-start.12 = (bf16[32,1024]{1,0:T(8,128)(2,1)S(1)}, bf16[32,1024]{1,0:T(8,128)(2,1)S(1)}, u32[]{:S(2)}, u32[]{:S(2)}) collective-permute-start(bf16[32,1024]{1,0:T(8,128)(2,1)S(1)} %project_near.1.after), channel_id=1, source_target_pairs={{0,2},{1,3},{2,0},{3,1},{4,6},{5,7},{6,4},{7,5},{8,10},{9,11},{10,... | collective-permute-start | bytes 196616 | tf_op jit(solution)/shard_map/ppermute | solution.py:25
  31.6 0.5 %project_own.1.own = f32[32,1024]{1,0:T(8,128)S(1)} custom-call(bf16[32,1024]{1,0:T(8,128)(2,1)S(1)} %get-tuple-element.36.attended, bf16[4,32,1024]{2,1,0:T(8,128)(2,1)S(1)} %collective-permute-done.9.sibling, bf16[32,1024]{1,0:T(8,128)(2,1)S(1)} %project_near.1.after, bf16[4,1024,1024]{2,1,0:T(8,128)(2,1)S(1)} %get-tuple-element.35.refs_8_.refs_0_), custom_call_target="tpu_custom_call" | custom-call | tf_op jit(solution)/shard_map/project_own/pallas_call | solution.py:519
  32.0 1.4 %collective-permute-done.10.refs_0_ = bf16[32,1024]{1,0:T(8,128)(2,1)S(1)} collective-permute-done((bf16[32,1024]{1,0:T(8,128)(2,1)S(1)}, bf16[32,1024]{1,0:T(8,128)(2,1)S(1)}, u32[]{:S(2)}, u32[]{:S(2)}) %collective-permute-start.10) | collective-permute-done | bytes 65568 | tf_op jit(solution)/shard_map/ppermute | solution.py:25
  33.4 2.1 %collective-permute-done.11.refs_1_ = bf16[32,1024]{1,0:T(8,128)(2,1)S(1)} collective-permute-done((bf16[32,1024]{1,0:T(8,128)(2,1)S(1)}, bf16[32,1024]{1,0:T(8,128)(2,1)S(1)}, u32[]{:S(2)}, u32[]{:S(2)}) %collective-permute-start.11) | collective-permute-done | bytes 65568 | tf_op jit(solution)/shard_map/ppermute | solution.py:25
  35.6 1.6 %collective-permute-start.13 = (bf16[32,1024]{1,0:T(8,128)(2,1)S(1)}, bf16[32,1024]{1,0:T(8,128)(2,1)S(1)}, u32[]{:S(2)}, u32[]{:S(2)}) collective-permute-start(bf16[32,1024]{1,0:T(8,128)(2,1)S(1)} %add_convert_fusion.1), channel_id=1, source_target_pairs={{0,16},{16,0},{1,17},{17,1},{2,18},{18,2},{3,19},{19,3},{4,20},{20... | collective-permute-start | bytes 196616 | tf_op jit(solution)/shard_map/ppermute | solution.py:539
  37.2 2.7 %collective-permute-done.13 = bf16[32,1024]{1,0:T(8,128)(2,1)S(1)} collective-permute-done((bf16[32,1024]{1,0:T(8,128)(2,1)S(1)}, bf16[32,1024]{1,0:T(8,128)(2,1)S(1)}, u32[]{:S(2)}, u32[]{:S(2)}) %collective-permute-start.13) | collective-permute-done | bytes 65568 | tf_op jit(solution)/shard_map/ppermute | solution.py:539
  39.9 0.7 %fusion.1 = bf16[1,32,1024]{2,1,0:T(8,128)(2,1)} fusion(bf16[32,1024]{1,0:T(8,128)(2,1)S(1)} %add_convert_fusion.1, f32[32,1024]{1,0:T(8,128)S(1)} %add_own.1, bf16[32,1024]{1,0:T(8,128)(2,1)S(1)} %collective-permute-done.12, bf16[32,1024]{1,0:T(8,128)(2,1)S(1)} %collective-permute-done.13, pred[]{:T(512)S(6)} %eq.3), kind=kLoop, calls=%fused_computation.4 | loop fusion | flops 196608 | bytes 393217 | tf_op jit(solution)/shard_map/broadcast_in_dim | solution.py:542
  (14 shorter events, 0.1 us)
Async XLA Ops:
  0.0 12.7 %collective-permute-start.1 = (bf16[256,2048]{1,0:T(8,128)(2,1)}, bf16[256,2048]{1,0:T(8,128)(2,1)S(1)}, u32[]{:S(2)}, u32[]{:S(2)}) collective-permute-start(bf16[256,2048]{1,0:T(8,128)(2,1)} %bitcast.12), channel_id=1, source_target_pairs={{0,1},{1,0},{2,3},{3,2},{4,5},{5,4},{6,7},{7,6},{8,9},{9,8},{10,11... | collective-permute-start | bytes 3145736 | tf_op jit(solution)/shard_map/ppermute | solution.py:25
  0.5 8.1 %collective-permute-start = (bf16[32,1024]{1,0:T(8,128)(2,1)}, bf16[32,1024]{1,0:T(8,128)(2,1)S(1)}, u32[]{:S(2)}, u32[]{:S(2)}) collective-permute-start(bf16[32,1024]{1,0:T(8,128)(2,1)} %bitcast.16), channel_id=1, source_target_pairs={{0,6},{1,7},{2,4},{3,5},{4,2},{5,3},{6,0},{7,1},{8,14},{9,15},{10,... | collective-permute-start | bytes 196616 | tf_op jit(solution)/shard_map/ppermute | solution.py:25
  5.1 3.5 %copy-start = (bf16[1,32,1024]{2,1,0:T(8,128)(2,1)S(1)}, bf16[1,32,1024]{2,1,0:T(8,128)(2,1)}, u32[]{:S(2)}) copy-start(bf16[1,32,1024]{2,1,0:T(8,128)(2,1)} %param.9) | copy-start | bytes 196612
  6.9 4.6 %collective-permute-start.2 = (bf16[32,1024]{1,0:T(8,128)(2,1)S(1)}, bf16[32,1024]{1,0:T(8,128)(2,1)S(1)}, u32[]{:S(2)}, u32[]{:S(2)}) collective-permute-start(bf16[32,1024]{1,0:T(8,128)(2,1)S(1)} %bitcast.11), channel_id=1, source_target_pairs={{0,8},{1,9},{2,10},{3,11},{4,12},{5,13},{6,14},{7,15},{8,0},{9,1},... | collective-permute-start | bytes 196616 | tf_op jit(solution)/shard_map/ppermute | solution.py:408
  8.5 4.3 %collective-permute-start.3 = (bf16[32,1024]{1,0:T(8,128)(2,1)S(1)}, bf16[32,1024]{1,0:T(8,128)(2,1)S(1)}, u32[]{:S(2)}, u32[]{:S(2)}) collective-permute-start(bf16[32,1024]{1,0:T(8,128)(2,1)S(1)} %bitcast.10), channel_id=1, source_target_pairs={{0,9},{1,8},{2,11},{3,10},{4,13},{5,12},{6,15},{7,14},{8,1},{9,0},... | collective-permute-start | bytes 196616 | tf_op jit(solution)/shard_map/ppermute | solution.py:408
  8.6 7.2 %collective-permute-start.5 = (bf16[32,1024]{1,0:T(8,128)(2,1)S(1)}, bf16[32,1024]{1,0:T(8,128)(2,1)S(1)}, u32[]{:S(2)}, u32[]{:S(2)}) collective-permute-start(bf16[32,1024]{1,0:T(8,128)(2,1)S(1)} %bitcast.18), channel_id=1, source_target_pairs={{0,4},{1,5},{2,6},{3,7},{4,0},{5,1},{6,2},{7,3},{8,12},{9,13},{10,... | collective-permute-start | bytes 196616 | tf_op jit(solution)/shard_map/ppermute | solution.py:25
  8.6 7.2 %collective-permute-start.6 = (bf16[32,1024]{1,0:T(8,128)(2,1)S(1)}, bf16[32,1024]{1,0:T(8,128)(2,1)S(1)}, u32[]{:S(2)}, u32[]{:S(2)}) collective-permute-start(bf16[32,1024]{1,0:T(8,128)(2,1)S(1)} %bitcast.19), channel_id=1, source_target_pairs={{0,2},{1,3},{2,0},{3,1},{4,6},{5,7},{6,4},{7,5},{8,10},{9,11},{10,... | collective-permute-start | bytes 196616 | tf_op jit(solution)/shard_map/ppermute | solution.py:25
  13.4 6.3 %collective-permute-start.4 = (bf16[32,1152]{1,0:T(8,128)(2,1)S(1)}, bf16[32,1152]{1,0:T(8,128)(2,1)S(1)}, u32[]{:S(2)}, u32[]{:S(2)}) collective-permute-start(bf16[32,1152]{1,0:T(8,128)(2,1)S(1)} %attend.3.refs_9_), channel_id=1, source_target_pairs={{0,6},{1,7},{2,4},{3,5},{4,2},{5,3},{6,0},{7,1},{8,14},{9,15},{10,... | collective-permute-start | bytes 221192 | tf_op jit(solution)/shard_map/ppermute | solution.py:25
  17.4 5.8 %collective-permute-start.7 = (bf16[32,1152]{1,0:T(8,128)(2,1)S(1)}, bf16[32,1152]{1,0:T(8,128)(2,1)S(1)}, u32[]{:S(2)}, u32[]{:S(2)}) collective-permute-start(bf16[32,1152]{1,0:T(8,128)(2,1)S(1)} %get-tuple-element.30), channel_id=1, source_target_pairs={{0,4},{1,5},{2,6},{3,7},{4,0},{5,1},{6,2},{7,3},{8,12},{9,13},{10,... | collective-permute-start | bytes 221192 | tf_op jit(solution)/shard_map/ppermute | solution.py:25
  17.4 5.7 %collective-permute-start.8 = (bf16[32,1152]{1,0:T(8,128)(2,1)S(1)}, bf16[32,1152]{1,0:T(8,128)(2,1)S(1)}, u32[]{:S(2)}, u32[]{:S(2)}) collective-permute-start(bf16[32,1152]{1,0:T(8,128)(2,1)S(1)} %get-tuple-element.31), channel_id=1, source_target_pairs={{0,2},{1,3},{2,0},{3,1},{4,6},{5,7},{6,4},{7,5},{8,10},{9,11},{10,... | collective-permute-start | bytes 221192 | tf_op jit(solution)/shard_map/ppermute | solution.py:25
  25.0 1.6 %collective-permute-start.9 = (bf16[4,32,1024]{2,1,0:T(8,128)(2,1)S(1)}, bf16[4,32,1024]{2,1,0:T(8,128)(2,1)S(1)}, u32[]{:S(2)}, u32[]{:S(2)}) collective-permute-start(bf16[4,32,1024]{2,1,0:T(8,128)(2,1)S(1)} %get-tuple-element.37), channel_id=1, source_target_pairs={{0,1},{1,0},{2,3},{3,2},{4,5},{5,4},{6,7},{7,6},{8,9},{9,8},{10,11... | collective-permute-start | bytes 786440 | tf_op jit(solution)/shard_map/ppermute | solution.py:25
  26.6 6.8 %collective-permute-start.10 = (bf16[32,1024]{1,0:T(8,128)(2,1)S(1)}, bf16[32,1024]{1,0:T(8,128)(2,1)S(1)}, u32[]{:S(2)}, u32[]{:S(2)}) collective-permute-start(bf16[32,1024]{1,0:T(8,128)(2,1)S(1)} %get-tuple-element.38.after), channel_id=1, source_target_pairs={{0,6},{1,7},{2,4},{3,5},{4,2},{5,3},{6,0},{7,1},{8,14},{9,15},{10,... | collective-permute-start | bytes 196616 | tf_op jit(solution)/shard_map/ppermute | solution.py:25
  29.0 6.5 %collective-permute-start.11 = (bf16[32,1024]{1,0:T(8,128)(2,1)S(1)}, bf16[32,1024]{1,0:T(8,128)(2,1)S(1)}, u32[]{:S(2)}, u32[]{:S(2)}) collective-permute-start(bf16[32,1024]{1,0:T(8,128)(2,1)S(1)} %get-tuple-element.40), channel_id=1, source_target_pairs={{0,4},{1,5},{2,6},{3,7},{4,0},{5,1},{6,2},{7,3},{8,12},{9,13},{10,... | collective-permute-start | bytes 196616 | tf_op jit(solution)/shard_map/ppermute | solution.py:25
  29.5 6.0 %copy-start.1 = (bf16[32,1024]{1,0:T(8,128)(2,1)S(1)}, bf16[32,1024]{1,0:T(8,128)(2,1)}, u32[]{:S(2)}) copy-start(bf16[32,1024]{1,0:T(8,128)(2,1)} %param.8) | copy-start | bytes 196612
  29.5 6.0 %collective-permute-start.12 = (bf16[32,1024]{1,0:T(8,128)(2,1)S(1)}, bf16[32,1024]{1,0:T(8,128)(2,1)S(1)}, u32[]{:S(2)}, u32[]{:S(2)}) collective-permute-start(bf16[32,1024]{1,0:T(8,128)(2,1)S(1)} %project_near.1.after), channel_id=1, source_target_pairs={{0,2},{1,3},{2,0},{3,1},{4,6},{5,7},{6,4},{7,5},{8,10},{9,11},{10,... | collective-permute-start | bytes 196616 | tf_op jit(solution)/shard_map/ppermute | solution.py:25
  35.6 4.3 %collective-permute-start.13 = (bf16[32,1024]{1,0:T(8,128)(2,1)S(1)}, bf16[32,1024]{1,0:T(8,128)(2,1)S(1)}, u32[]{:S(2)}, u32[]{:S(2)}) collective-permute-start(bf16[32,1024]{1,0:T(8,128)(2,1)S(1)} %add_convert_fusion.1), channel_id=1, source_target_pairs={{0,16},{16,0},{1,17},{17,1},{2,18},{18,2},{3,19},{19,3},{4,20},{20... | collective-permute-start | bytes 196616 | tf_op jit(solution)/shard_map/ppermute | solution.py:539

commit v6 on v5

--- a/solution.py
+++ b/solution.py
@@ -185,8 +185,8 @@
     load_copies = []
     if weight_masks:
         load_copies = weight_copies(place, weight, weight_out, weight_semaphores, weight_masks)
-    for copy in load_copies:
-        copy.start()
+    for at, copy in enumerate(load_copies):
+        copy.start(priority=at % 2)
 
     @beside_copies(place)
     def _():
@@ -275,8 +275,8 @@
         weight, refs = refs[0], refs[1:]
         load_copies = weight_copies(place, weight, weight_out, weight_semaphores, weight_masks)
     *weights, out, attended = refs
-    for copy in load_copies:
-        copy.start()
+    for at, copy in enumerate(load_copies):
+        copy.start(priority=at % 2)
 
     @beside_copies(place)
     def _():

time: 40.8 us -> 40.8 us (level)
  no operation moved by 1% of the time
where the time goes in v6:
time: 40.8 us; the launch traced here: 40.6 us
  starting transfers between devices  18.2 us (45%)
  Pallas kernels  13.2 us (32%)
  waiting for transfers between devices  8.35 us (20%)
  other arithmetic  0.69 us (2%)
    ppermute x11, starting transfers between devices, swapped(): lax.ppermute(value, 'tensor', [(source, source ^ mask) for source in rang...  15 us
    pallas_call x3, Pallas kernels, attend(): pl.pallas_call(functools.partial(attend_kernel, masks, weight_masks, len(...  5.76 us
    ppermute x11, waiting for transfers between devices, swapped(): lax.ppermute(value, 'tensor', [(source, source ^ mask) for source in rang...  4.35 us
    ppermute x1, waiting for transfers between devices, local(): handed_over = lax.ppermute(after_first, 'section', [(0, 1), (1, 0)])  2.75 us
    pallas_call x1, Pallas kernels, local(): pl.pallas_call(functools.partial(prepare_kernel, (pages, page_tokens, cap...  2.05 us
    pallas_call x1, Pallas kernels, local(): pl.pallas_call(functools.partial(pick_kernel, capacity, loads[0]), out_sh...  1.85 us
    pallas_call x1, Pallas kernels, local(): pl.pallas_call(functools.partial(project_away_kernel, heads_per, half, fo...  1.75 us
    ppermute x2, starting transfers between devices, local(): arrived.append(lax.ppermute(sent, ('inst', 'tensor'), pairs))  1.64 us
  transfers between devices with their start and end apart: 14, of which 6 were waited for; matrix products, arithmetic and copies ran while one was open for 0% of the time, Pallas kernels for 28%

profile of v6, /device:TPU:0, one launch (start us, length us, event | category | flops | bytes accessed | tf_op | source)
XLA Modules:
  0.0 40.6 jit_solution(6708225675665819361)
XLA Ops:
  0.0 0.5 %collective-permute-start.1 = (bf16[256,2048]{1,0:T(8,128)(2,1)}, bf16[256,2048]{1,0:T(8,128)(2,1)S(1)}, u32[]{:S(2)}, u32[]{:S(2)}) collective-permute-start(bf16[256,2048]{1,0:T(8,128)(2,1)} %bitcast.12), channel_id=1, source_target_pairs={{0,1},{1,0},{2,3},{3,2},{4,5},{5,4},{6,7},{7,6},{8,9},{9,8},{10,11... | collective-permute-start | bytes 3145736 | tf_op jit(solution)/shard_map/ppermute | solution.py:25
  0.5 4.6 %collective-permute-start = (bf16[32,1024]{1,0:T(8,128)(2,1)}, bf16[32,1024]{1,0:T(8,128)(2,1)S(1)}, u32[]{:S(2)}, u32[]{:S(2)}) collective-permute-start(bf16[32,1024]{1,0:T(8,128)(2,1)} %bitcast.16), channel_id=1, source_target_pairs={{0,6},{1,7},{2,4},{3,5},{4,2},{5,3},{6,0},{7,1},{8,14},{9,15},{10,... | collective-permute-start | bytes 196616 | tf_op jit(solution)/shard_map/ppermute | solution.py:25
  5.1 1.9 %pick.1 = (bf16[1,32,1024]{2,1,0:T(8,128)(2,1)S(1)}, bf16[1,32,1024]{2,1,0:T(8,128)(2,1)S(1)}, bf16[1,1024,1024]{2,1,0:T(8,128)(2,1)S(1)}) custom-call(s32[2]{0:T(128)S(4)} %place.1.refs_0_, s32[2]{0:T(128)} %bitcast.21, bf16[8,32,2048]{2,1,0:T(8,128)(2,1)} %bitcast.13, bf16[1,1024,8192]{2,1,0:T(8,128)(2,1)} %refs_4_.1), custom_call_target="tpu_custom_call" | custom-call | tf_op jit(solution)/shard_map/pick/pallas_call | solution.py:379
  6.9 1.6 %collective-permute-start.2 = (bf16[32,1024]{1,0:T(8,128)(2,1)S(1)}, bf16[32,1024]{1,0:T(8,128)(2,1)S(1)}, u32[]{:S(2)}, u32[]{:S(2)}) collective-permute-start(bf16[32,1024]{1,0:T(8,128)(2,1)S(1)} %bitcast.11), channel_id=1, source_target_pairs={{0,8},{1,9},{2,10},{3,11},{4,12},{5,13},{6,14},{7,15},{8,0},{9,1},... | collective-permute-start | bytes 196616 | tf_op jit(solution)/shard_map/ppermute | solution.py:408
  8.5 0.1 collective-permute-start.3
  8.6 0.8 %collective-permute-start.6 = (bf16[32,1024]{1,0:T(8,128)(2,1)S(1)}, bf16[32,1024]{1,0:T(8,128)(2,1)S(1)}, u32[]{:S(2)}, u32[]{:S(2)}) collective-permute-start(bf16[32,1024]{1,0:T(8,128)(2,1)S(1)} %bitcast.19), channel_id=1, source_target_pairs={{0,2},{1,3},{2,0},{3,1},{4,6},{5,7},{6,4},{7,5},{8,10},{9,11},{10,... | collective-permute-start | bytes 196616 | tf_op jit(solution)/shard_map/ppermute | solution.py:25
  9.4 2.0 %prepare.1 = (f32[32,608]{1,0:T(8,128)S(1)}, bf16[32,1024]{1,0:T(8,128)(2,1)S(1)}, bf16[256,2048]{1,0:T(8,128)(2,1)S(1)}, bf16[32,2048]{1,0:T(8,128)(2,1)S(1)}, bf16[1,1024,1024]{2,1,0:T(8,128)(2,1)S(1)}) custom-call(s32[2]{0:T(128)S(4)} %place.1.refs_0_, s32[4,8]{1,0:T(4,128)} %bitcast.20, s32[8]{0:T(128)} %lengths_hbm.1, s32[2]{0:T(128)} %bitcast.22, ...), custom_call_target="tpu_custom_call" | custom-call | tf_op jit(solution)/shard_map/prepare/pallas_call | solution.py:414
  11.5 0.0 collective-permute-done.2.refs_5_.refs_6_
  11.5 1.3 %collective-permute-done.3.refs_6_.refs_7_ = bf16[32,1024]{1,0:T(8,128)(2,1)S(1)} collective-permute-done((bf16[32,1024]{1,0:T(8,128)(2,1)S(1)}, bf16[32,1024]{1,0:T(8,128)(2,1)S(1)}, u32[]{:S(2)}, u32[]{:S(2)}) %collective-permute-start.3) | collective-permute-done | bytes 65568 | tf_op jit(solution)/shard_map/ppermute | solution.py:408
  12.7 0.0 collective-permute-done.1.refs_4_.refs_5_
  12.7 0.6 %attend.3.refs_9_ = bf16[32,1152]{1,0:T(8,128)(2,1)S(1)} custom-call(s32[2]{0:T(128)S(4)} %place.1.refs_0_, f32[32,608]{1,0:T(8,128)S(1)} %get-tuple-element.23.refs_1_, bf16[32,1024]{1,0:T(8,128)(2,1)S(1)} %collective-permute-done.refs_3_.refs_2_, bf16[256,2048]{1,0:T(8,128)(2,1)S(1)} %get-tuple-element.25.refs_3_.refs_4_, ...), custom_call_target="tpu_custom_call" | custom-call | tf_op jit(solution)/shard_map/attend/pallas_call | solution.py:448
  13.4 2.4 %collective-permute-start.4 = (bf16[32,1152]{1,0:T(8,128)(2,1)S(1)}, bf16[32,1152]{1,0:T(8,128)(2,1)S(1)}, u32[]{:S(2)}, u32[]{:S(2)}) collective-permute-start(bf16[32,1152]{1,0:T(8,128)(2,1)S(1)} %attend.3.refs_9_), channel_id=1, source_target_pairs={{0,6},{1,7},{2,4},{3,5},{4,2},{5,3},{6,0},{7,1},{8,14},{9,15},{10,... | collective-permute-start | bytes 221192 | tf_op jit(solution)/shard_map/ppermute | solution.py:25
  15.7 0.0 collective-permute-done.5.refs_2_
  15.7 1.6 %attend.5 = (bf16[32,1152]{1,0:T(8,128)(2,1)S(1)}, bf16[32,1152]{1,0:T(8,128)(2,1)S(1)}, bf16[1,1024,1024]{2,1,0:T(8,128)(2,1)S(1)}) custom-call(s32[2]{0:T(128)S(4)} %place.1.refs_0_, f32[32,608]{1,0:T(8,128)S(1)} %get-tuple-element.23.refs_1_, bf16[32,1024]{1,0:T(8,128)(2,1)S(1)} %collective-permute-done.5.refs_2_, ...), custom_call_target="tpu_custom_call" | custom-call | tf_op jit(solution)/shard_map/attend/pallas_call | solution.py:448
  17.4 0.1 collective-permute-start.7
  17.4 2.1 %collective-permute-start.8 = (bf16[32,1152]{1,0:T(8,128)(2,1)S(1)}, bf16[32,1152]{1,0:T(8,128)(2,1)S(1)}, u32[]{:S(2)}, u32[]{:S(2)}) collective-permute-start(bf16[32,1152]{1,0:T(8,128)(2,1)S(1)} %get-tuple-element.31), channel_id=1, source_target_pairs={{0,2},{1,3},{2,0},{3,1},{4,6},{5,7},{6,4},{7,5},{8,10},{9,11},{10,... | collective-permute-start | bytes 221192 | tf_op jit(solution)/shard_map/ppermute | solution.py:25
  19.5 0.1 collective-permute-done.4.refs_8_.refs_1_
  19.6 3.5 %attend.4 = (bf16[32,1152]{1,0:T(8,128)(2,1)S(1)}, bf16[4,1024,1024]{2,1,0:T(8,128)(2,1)S(1)}) custom-call(s32[2]{0:T(128)S(4)} %place.1.refs_0_, f32[32,608]{1,0:T(8,128)S(1)} %get-tuple-element.23.refs_1_, bf16[32,1024]{1,0:T(8,128)(2,1)S(1)} %get-tuple-element.24.refs_2_, bf16[256,2048]{1,0:T(8,128)(2,1)S(1)} %get-tuple-element.25.refs_3_.refs_4_, ...), custom_call_target="tpu_custom_call" | custom-call | tf_op jit(solution)/shard_map/attend/pallas_call | solution.py:448
  23.2 0.0 collective-permute-done.8.refs_3_
  23.2 1.8 %project_away.1 = (bf16[4,32,1024]{2,1,0:T(8,128)(2,1)S(1)}, bf16[32,1024]{1,0:T(8,128)(2,1)S(1)}, bf16[1,1024,1024]{2,1,0:T(8,128)(2,1)S(1)}) custom-call(s32[2]{0:T(128)S(4)} %place.1.refs_0_, bf16[32,1152]{1,0:T(8,128)(2,1)S(1)} %get-tuple-element.29.refs_0_, bf16[32,1152]{1,0:T(8,128)(2,1)S(1)} %collective-permute-done.4.refs_8_.refs_1_, ...), custom_call_target="tpu_custom_call" | custom-call | tf_op jit(solution)/shard_map/project_away/pallas_call | solution.py:474
  25.0 0.1 collective-permute-start.9
  25.1 0.8 %project_far.1.home = f32[2,32,1024]{2,1,0:T(8,128)S(1)} custom-call(bf16[32,1024]{1,0:T(8,128)(2,1)S(1)} %get-tuple-element.36.attended, bf16[4,1024,1024]{2,1,0:T(8,128)(2,1)S(1)} %get-tuple-element.35.refs_8_.refs_0_), custom_call_target="tpu_custom_call" | custom-call | tf_op jit(solution)/shard_map/project_far/pallas_call | solution.py:490
  25.9 0.7 %collective-permute-done.9.sibling = bf16[4,32,1024]{2,1,0:T(8,128)(2,1)S(1)} collective-permute-done((bf16[4,32,1024]{2,1,0:T(8,128)(2,1)S(1)}, bf16[4,32,1024]{2,1,0:T(8,128)(2,1)S(1)}, u32[]{:S(2)}, u32[]{:S(2)}) %collective-permute-start.9) | collective-permute-done | bytes 262176 | tf_op jit(solution)/shard_map/ppermute | solution.py:25
  26.6 2.4 %collective-permute-start.10 = (bf16[32,1024]{1,0:T(8,128)(2,1)S(1)}, bf16[32,1024]{1,0:T(8,128)(2,1)S(1)}, u32[]{:S(2)}, u32[]{:S(2)}) collective-permute-start(bf16[32,1024]{1,0:T(8,128)(2,1)S(1)} %get-tuple-element.38.after), channel_id=1, source_target_pairs={{0,6},{1,7},{2,4},{3,5},{4,2},{5,3},{6,0},{7,1},{8,14},{9,15},{10,... | collective-permute-start | bytes 196616 | tf_op jit(solution)/shard_map/ppermute | solution.py:25
  29.0 0.5 %project_near.1.after = bf16[32,1024]{1,0:T(8,128)(2,1)S(1)} custom-call(bf16[32,1024]{1,0:T(8,128)(2,1)S(1)} %get-tuple-element.36.attended, bf16[4,32,1024]{2,1,0:T(8,128)(2,1)S(1)} %collective-permute-done.9.sibling, bf16[32,1024]{1,0:T(8,128)(2,1)S(1)} %get-tuple-element.38.after, bf16[1,1024,1024]{2,1,0:T(8,128)(2,1)S(1)} %get-tuple-element.39.refs_0_), custom_call_target="tpu_custom_call" | custom-call | tf_op jit(solution)/shard_map/project_near/pallas_call | solution.py:510
  29.5 2.1 %collective-permute-start.12 = (bf16[32,1024]{1,0:T(8,128)(2,1)S(1)}, bf16[32,1024]{1,0:T(8,128)(2,1)S(1)}, u32[]{:S(2)}, u32[]{:S(2)}) collective-permute-start(bf16[32,1024]{1,0:T(8,128)(2,1)S(1)} %project_near.1.after), channel_id=1, source_target_pairs={{0,2},{1,3},{2,0},{3,1},{4,6},{5,7},{6,4},{7,5},{8,10},{9,11},{10,... | collective-permute-start | bytes 196616 | tf_op jit(solution)/shard_map/ppermute | solution.py:25
  31.6 0.5 %project_own.1.own = f32[32,1024]{1,0:T(8,128)S(1)} custom-call(bf16[32,1024]{1,0:T(8,128)(2,1)S(1)} %get-tuple-element.36.attended, bf16[4,32,1024]{2,1,0:T(8,128)(2,1)S(1)} %collective-permute-done.9.sibling, bf16[32,1024]{1,0:T(8,128)(2,1)S(1)} %project_near.1.after, bf16[4,1024,1024]{2,1,0:T(8,128)(2,1)S(1)} %get-tuple-element.35.refs_8_.refs_0_), custom_call_target="tpu_custom_call" | custom-call | tf_op jit(solution)/shard_map/project_own/pallas_call | solution.py:519
  32.0 1.4 %collective-permute-done.10.refs_0_ = bf16[32,1024]{1,0:T(8,128)(2,1)S(1)} collective-permute-done((bf16[32,1024]{1,0:T(8,128)(2,1)S(1)}, bf16[32,1024]{1,0:T(8,128)(2,1)S(1)}, u32[]{:S(2)}, u32[]{:S(2)}) %collective-permute-start.10) | collective-permute-done | bytes 65568 | tf_op jit(solution)/shard_map/ppermute | solution.py:25
  33.4 2.1 %collective-permute-done.11.refs_1_ = bf16[32,1024]{1,0:T(8,128)(2,1)S(1)} collective-permute-done((bf16[32,1024]{1,0:T(8,128)(2,1)S(1)}, bf16[32,1024]{1,0:T(8,128)(2,1)S(1)}, u32[]{:S(2)}, u32[]{:S(2)}) %collective-permute-start.11) | collective-permute-done | bytes 65568 | tf_op jit(solution)/shard_map/ppermute | solution.py:25
  35.6 1.6 %collective-permute-start.13 = (bf16[32,1024]{1,0:T(8,128)(2,1)S(1)}, bf16[32,1024]{1,0:T(8,128)(2,1)S(1)}, u32[]{:S(2)}, u32[]{:S(2)}) collective-permute-start(bf16[32,1024]{1,0:T(8,128)(2,1)S(1)} %add_convert_fusion.1), channel_id=1, source_target_pairs={{0,16},{16,0},{1,17},{17,1},{2,18},{18,2},{3,19},{19,3},{4,20},{20... | collective-permute-start | bytes 196616 | tf_op jit(solution)/shard_map/ppermute | solution.py:539
  37.2 2.7 %collective-permute-done.13 = bf16[32,1024]{1,0:T(8,128)(2,1)S(1)} collective-permute-done((bf16[32,1024]{1,0:T(8,128)(2,1)S(1)}, bf16[32,1024]{1,0:T(8,128)(2,1)S(1)}, u32[]{:S(2)}, u32[]{:S(2)}) %collective-permute-start.13) | collective-permute-done | bytes 65568 | tf_op jit(solution)/shard_map/ppermute | solution.py:539
  39.9 0.7 %fusion.1 = bf16[1,32,1024]{2,1,0:T(8,128)(2,1)} fusion(bf16[32,1024]{1,0:T(8,128)(2,1)S(1)} %add_convert_fusion.1, f32[32,1024]{1,0:T(8,128)S(1)} %add_own.1, bf16[32,1024]{1,0:T(8,128)(2,1)S(1)} %collective-permute-done.12, bf16[32,1024]{1,0:T(8,128)(2,1)S(1)} %collective-permute-done.13, pred[]{:T(512)S(6)} %eq.3), kind=kLoop, calls=%fused_computation.4 | loop fusion | flops 196608 | bytes 393217 | tf_op jit(solution)/shard_map/broadcast_in_dim | solution.py:542
  (14 shorter events, 0.1 us)
Async XLA Ops:
  0.0 12.7 %collective-permute-start.1 = (bf16[256,2048]{1,0:T(8,128)(2,1)}, bf16[256,2048]{1,0:T(8,128)(2,1)S(1)}, u32[]{:S(2)}, u32[]{:S(2)}) collective-permute-start(bf16[256,2048]{1,0:T(8,128)(2,1)} %bitcast.12), channel_id=1, source_target_pairs={{0,1},{1,0},{2,3},{3,2},{4,5},{5,4},{6,7},{7,6},{8,9},{9,8},{10,11... | collective-permute-start | bytes 3145736 | tf_op jit(solution)/shard_map/ppermute | solution.py:25
  0.5 8.1 %collective-permute-start = (bf16[32,1024]{1,0:T(8,128)(2,1)}, bf16[32,1024]{1,0:T(8,128)(2,1)S(1)}, u32[]{:S(2)}, u32[]{:S(2)}) collective-permute-start(bf16[32,1024]{1,0:T(8,128)(2,1)} %bitcast.16), channel_id=1, source_target_pairs={{0,6},{1,7},{2,4},{3,5},{4,2},{5,3},{6,0},{7,1},{8,14},{9,15},{10,... | collective-permute-start | bytes 196616 | tf_op jit(solution)/shard_map/ppermute | solution.py:25
  5.1 3.5 %copy-start = (bf16[1,32,1024]{2,1,0:T(8,128)(2,1)S(1)}, bf16[1,32,1024]{2,1,0:T(8,128)(2,1)}, u32[]{:S(2)}) copy-start(bf16[1,32,1024]{2,1,0:T(8,128)(2,1)} %param.9) | copy-start | bytes 196612
  6.9 4.6 %collective-permute-start.2 = (bf16[32,1024]{1,0:T(8,128)(2,1)S(1)}, bf16[32,1024]{1,0:T(8,128)(2,1)S(1)}, u32[]{:S(2)}, u32[]{:S(2)}) collective-permute-start(bf16[32,1024]{1,0:T(8,128)(2,1)S(1)} %bitcast.11), channel_id=1, source_target_pairs={{0,8},{1,9},{2,10},{3,11},{4,12},{5,13},{6,14},{7,15},{8,0},{9,1},... | collective-permute-start | bytes 196616 | tf_op jit(solution)/shard_map/ppermute | solution.py:408
  8.5 4.3 %collective-permute-start.3 = (bf16[32,1024]{1,0:T(8,128)(2,1)S(1)}, bf16[32,1024]{1,0:T(8,128)(2,1)S(1)}, u32[]{:S(2)}, u32[]{:S(2)}) collective-permute-start(bf16[32,1024]{1,0:T(8,128)(2,1)S(1)} %bitcast.10), channel_id=1, source_target_pairs={{0,9},{1,8},{2,11},{3,10},{4,13},{5,12},{6,15},{7,14},{8,1},{9,0},... | collective-permute-start | bytes 196616 | tf_op jit(solution)/shard_map/ppermute | solution.py:408
  8.6 7.2 %collective-permute-start.5 = (bf16[32,1024]{1,0:T(8,128)(2,1)S(1)}, bf16[32,1024]{1,0:T(8,128)(2,1)S(1)}, u32[]{:S(2)}, u32[]{:S(2)}) collective-permute-start(bf16[32,1024]{1,0:T(8,128)(2,1)S(1)} %bitcast.18), channel_id=1, source_target_pairs={{0,4},{1,5},{2,6},{3,7},{4,0},{5,1},{6,2},{7,3},{8,12},{9,13},{10,... | collective-permute-start | bytes 196616 | tf_op jit(solution)/shard_map/ppermute | solution.py:25
  8.6 7.2 %collective-permute-start.6 = (bf16[32,1024]{1,0:T(8,128)(2,1)S(1)}, bf16[32,1024]{1,0:T(8,128)(2,1)S(1)}, u32[]{:S(2)}, u32[]{:S(2)}) collective-permute-start(bf16[32,1024]{1,0:T(8,128)(2,1)S(1)} %bitcast.19), channel_id=1, source_target_pairs={{0,2},{1,3},{2,0},{3,1},{4,6},{5,7},{6,4},{7,5},{8,10},{9,11},{10,... | collective-permute-start | bytes 196616 | tf_op jit(solution)/shard_map/ppermute | solution.py:25
  13.4 6.3 %collective-permute-start.4 = (bf16[32,1152]{1,0:T(8,128)(2,1)S(1)}, bf16[32,1152]{1,0:T(8,128)(2,1)S(1)}, u32[]{:S(2)}, u32[]{:S(2)}) collective-permute-start(bf16[32,1152]{1,0:T(8,128)(2,1)S(1)} %attend.3.refs_9_), channel_id=1, source_target_pairs={{0,6},{1,7},{2,4},{3,5},{4,2},{5,3},{6,0},{7,1},{8,14},{9,15},{10,... | collective-permute-start | bytes 221192 | tf_op jit(solution)/shard_map/ppermute | solution.py:25
  17.4 5.8 %collective-permute-start.7 = (bf16[32,1152]{1,0:T(8,128)(2,1)S(1)}, bf16[32,1152]{1,0:T(8,128)(2,1)S(1)}, u32[]{:S(2)}, u32[]{:S(2)}) collective-permute-start(bf16[32,1152]{1,0:T(8,128)(2,1)S(1)} %get-tuple-element.30), channel_id=1, source_target_pairs={{0,4},{1,5},{2,6},{3,7},{4,0},{5,1},{6,2},{7,3},{8,12},{9,13},{10,... | collective-permute-start | bytes 221192 | tf_op jit(solution)/shard_map/ppermute | solution.py:25
  17.4 5.8 %collective-permute-start.8 = (bf16[32,1152]{1,0:T(8,128)(2,1)S(1)}, bf16[32,1152]{1,0:T(8,128)(2,1)S(1)}, u32[]{:S(2)}, u32[]{:S(2)}) collective-permute-start(bf16[32,1152]{1,0:T(8,128)(2,1)S(1)} %get-tuple-element.31), channel_id=1, source_target_pairs={{0,2},{1,3},{2,0},{3,1},{4,6},{5,7},{6,4},{7,5},{8,10},{9,11},{10,... | collective-permute-start | bytes 221192 | tf_op jit(solution)/shard_map/ppermute | solution.py:25
  25.0 1.6 %collective-permute-start.9 = (bf16[4,32,1024]{2,1,0:T(8,128)(2,1)S(1)}, bf16[4,32,1024]{2,1,0:T(8,128)(2,1)S(1)}, u32[]{:S(2)}, u32[]{:S(2)}) collective-permute-start(bf16[4,32,1024]{2,1,0:T(8,128)(2,1)S(1)} %get-tuple-element.37), channel_id=1, source_target_pairs={{0,1},{1,0},{2,3},{3,2},{4,5},{5,4},{6,7},{7,6},{8,9},{9,8},{10,11... | collective-permute-start | bytes 786440 | tf_op jit(solution)/shard_map/ppermute | solution.py:25
  26.6 6.8 %collective-permute-start.10 = (bf16[32,1024]{1,0:T(8,128)(2,1)S(1)}, bf16[32,1024]{1,0:T(8,128)(2,1)S(1)}, u32[]{:S(2)}, u32[]{:S(2)}) collective-permute-start(bf16[32,1024]{1,0:T(8,128)(2,1)S(1)} %get-tuple-element.38.after), channel_id=1, source_target_pairs={{0,6},{1,7},{2,4},{3,5},{4,2},{5,3},{6,0},{7,1},{8,14},{9,15},{10,... | collective-permute-start | bytes 196616 | tf_op jit(solution)/shard_map/ppermute | solution.py:25
  29.0 6.5 %collective-permute-start.11 = (bf16[32,1024]{1,0:T(8,128)(2,1)S(1)}, bf16[32,1024]{1,0:T(8,128)(2,1)S(1)}, u32[]{:S(2)}, u32[]{:S(2)}) collective-permute-start(bf16[32,1024]{1,0:T(8,128)(2,1)S(1)} %get-tuple-element.40), channel_id=1, source_target_pairs={{0,4},{1,5},{2,6},{3,7},{4,0},{5,1},{6,2},{7,3},{8,12},{9,13},{10,... | collective-permute-start | bytes 196616 | tf_op jit(solution)/shard_map/ppermute | solution.py:25
  29.5 6.1 %copy-start.1 = (bf16[32,1024]{1,0:T(8,128)(2,1)S(1)}, bf16[32,1024]{1,0:T(8,128)(2,1)}, u32[]{:S(2)}) copy-start(bf16[32,1024]{1,0:T(8,128)(2,1)} %param.8) | copy-start | bytes 196612
  29.5 6.0 %collective-permute-start.12 = (bf16[32,1024]{1,0:T(8,128)(2,1)S(1)}, bf16[32,1024]{1,0:T(8,128)(2,1)S(1)}, u32[]{:S(2)}, u32[]{:S(2)}) collective-permute-start(bf16[32,1024]{1,0:T(8,128)(2,1)S(1)} %project_near.1.after), channel_id=1, source_target_pairs={{0,2},{1,3},{2,0},{3,1},{4,6},{5,7},{6,4},{7,5},{8,10},{9,11},{10,... | collective-permute-start | bytes 196616 | tf_op jit(solution)/shard_map/ppermute | solution.py:25
  35.6 4.3 %collective-permute-start.13 = (bf16[32,1024]{1,0:T(8,128)(2,1)S(1)}, bf16[32,1024]{1,0:T(8,128)(2,1)S(1)}, u32[]{:S(2)}, u32[]{:S(2)}) collective-permute-start(bf16[32,1024]{1,0:T(8,128)(2,1)S(1)} %add_convert_fusion.1), channel_id=1, source_target_pairs={{0,16},{16,0},{1,17},{17,1},{2,18},{18,2},{3,19},{19,3},{4,20},{20... | collective-permute-start | bytes 196616 | tf_op jit(solution)/shard_map/ppermute | solution.py:539

commit v7 on v5

--- a/solution.py
+++ b/solution.py
@@ -337,7 +337,7 @@
     far = half // 2
     home_masks = list(range(2, tensor_count, 2))
     if half == 4:
-        home_masks = [6, 4, 2]
+        home_masks = [4, 6, 2]
     home_masks.insert(far, 0)
     away_masks = [mask ^ 1 for mask in home_masks]
     unit = tensor_count // 8

time: 40.8 us -> 41.1 us (level)
  waiting for transfers between devices: 8.36 us -> 9.63 us
  starting transfers between devices: 18.2 us -> 17.3 us
    ppermute x11, waiting for transfers between devices: 4.36 us -> 5.63 us  [swapped(): lax.ppermute(value, 'tensor', [(source, source ^ mask) for source in rang...]
    ppermute x11, starting transfers between devices: 15 us -> 14.1 us  [swapped(): lax.ppermute(value, 'tensor', [(source, source ^ mask) for source in rang...]
where the time goes in v7:
time: 41.1 us; the launch traced here: 40.9 us
  starting transfers between devices  17.3 us (42%)
  Pallas kernels  13.2 us (32%)
  waiting for transfers between devices  9.63 us (23%)
  other arithmetic  0.69 us (2%)
    ppermute x11, starting transfers between devices, swapped(): lax.ppermute(value, 'tensor', [(source, source ^ mask) for source in rang...  14.1 us
    pallas_call x3, Pallas kernels, attend(): pl.pallas_call(functools.partial(attend_kernel, masks, weight_masks, len(...  5.74 us
    ppermute x11, waiting for transfers between devices, swapped(): lax.ppermute(value, 'tensor', [(source, source ^ mask) for source in rang...  5.63 us
    ppermute x1, waiting for transfers between devices, local(): handed_over = lax.ppermute(after_first, 'section', [(0, 1), (1, 0)])  2.75 us
    pallas_call x1, Pallas kernels, local(): pl.pallas_call(functools.partial(prepare_kernel, (pages, page_tokens, cap...  2.05 us
    pallas_call x1, Pallas kernels, local(): pl.pallas_call(functools.partial(pick_kernel, capacity, loads[0]), out_sh...  1.85 us
    pallas_call x1, Pallas kernels, local(): pl.pallas_call(functools.partial(project_away_kernel, heads_per, half, fo...  1.75 us
    ppermute x2, starting transfers between devices, local(): arrived.append(lax.ppermute(sent, ('inst', 'tensor'), pairs))  1.64 us
  transfers between devices with their start and end apart: 14, of which 6 were waited for; matrix products, arithmetic and copies ran while one was open for 0% of the time, Pallas kernels for 28%

profile of v7, /device:TPU:0, one launch (start us, length us, event | category | flops | bytes accessed | tf_op | source)
XLA Modules:
  0.0 40.9 jit_solution(9974790990737686250)
XLA Ops:
  0.0 0.5 %collective-permute-start.1 = (bf16[256,2048]{1,0:T(8,128)(2,1)}, bf16[256,2048]{1,0:T(8,128)(2,1)S(1)}, u32[]{:S(2)}, u32[]{:S(2)}) collective-permute-start(bf16[256,2048]{1,0:T(8,128)(2,1)} %bitcast.12), channel_id=1, source_target_pairs={{0,1},{1,0},{2,3},{3,2},{4,5},{5,4},{6,7},{7,6},{8,9},{9,8},{10,11... | collective-permute-start | bytes 3145736 | tf_op jit(solution)/shard_map/ppermute | solution.py:25
  0.5 4.6 %collective-permute-start = (bf16[32,1024]{1,0:T(8,128)(2,1)}, bf16[32,1024]{1,0:T(8,128)(2,1)S(1)}, u32[]{:S(2)}, u32[]{:S(2)}) collective-permute-start(bf16[32,1024]{1,0:T(8,128)(2,1)} %bitcast.16), channel_id=1, source_target_pairs={{0,6},{1,7},{2,4},{3,5},{4,2},{5,3},{6,0},{7,1},{8,14},{9,15},{10,... | collective-permute-start | bytes 196616 | tf_op jit(solution)/shard_map/ppermute | solution.py:25
  5.1 1.9 %pick.1 = (bf16[1,32,1024]{2,1,0:T(8,128)(2,1)S(1)}, bf16[1,32,1024]{2,1,0:T(8,128)(2,1)S(1)}, bf16[1,1024,1024]{2,1,0:T(8,128)(2,1)S(1)}) custom-call(s32[2]{0:T(128)S(4)} %place.1.refs_0_, s32[2]{0:T(128)} %bitcast.21, bf16[8,32,2048]{2,1,0:T(8,128)(2,1)} %bitcast.13, bf16[1,1024,8192]{2,1,0:T(8,128)(2,1)} %refs_4_.1), custom_call_target="tpu_custom_call" | custom-call | tf_op jit(solution)/shard_map/pick/pallas_call | solution.py:379
  6.9 1.6 %collective-permute-start.2 = (bf16[32,1024]{1,0:T(8,128)(2,1)S(1)}, bf16[32,1024]{1,0:T(8,128)(2,1)S(1)}, u32[]{:S(2)}, u32[]{:S(2)}) collective-permute-start(bf16[32,1024]{1,0:T(8,128)(2,1)S(1)} %bitcast.11), channel_id=1, source_target_pairs={{0,8},{1,9},{2,10},{3,11},{4,12},{5,13},{6,14},{7,15},{8,0},{9,1},... | collective-permute-start | bytes 196616 | tf_op jit(solution)/shard_map/ppermute | solution.py:408
  8.5 0.1 collective-permute-start.3
  8.6 0.0 collective-permute-start.5
  8.6 0.0 collective-permute-done.refs_3_.refs_2_
  8.6 0.8 %collective-permute-start.6 = (bf16[32,1024]{1,0:T(8,128)(2,1)S(1)}, bf16[32,1024]{1,0:T(8,128)(2,1)S(1)}, u32[]{:S(2)}, u32[]{:S(2)}) collective-permute-start(bf16[32,1024]{1,0:T(8,128)(2,1)S(1)} %bitcast.19), channel_id=1, source_target_pairs={{0,2},{1,3},{2,0},{3,1},{4,6},{5,7},{6,4},{7,5},{8,10},{9,11},{10,... | collective-permute-start | bytes 196616 | tf_op jit(solution)/shard_map/ppermute | solution.py:25
  9.4 2.0 %prepare.1 = (f32[32,608]{1,0:T(8,128)S(1)}, bf16[32,1024]{1,0:T(8,128)(2,1)S(1)}, bf16[256,2048]{1,0:T(8,128)(2,1)S(1)}, bf16[32,2048]{1,0:T(8,128)(2,1)S(1)}, bf16[1,1024,1024]{2,1,0:T(8,128)(2,1)S(1)}) custom-call(s32[2]{0:T(128)S(4)} %place.1.refs_0_, s32[4,8]{1,0:T(4,128)} %bitcast.20, s32[8]{0:T(128)} %lengths_hbm.1, s32[2]{0:T(128)} %bitcast.22, ...), custom_call_target="tpu_custom_call" | custom-call | tf_op jit(solution)/shard_map/prepare/pallas_call | solution.py:414
  11.5 1.3 %collective-permute-done.3.refs_6_.refs_7_ = bf16[32,1024]{1,0:T(8,128)(2,1)S(1)} collective-permute-done((bf16[32,1024]{1,0:T(8,128)(2,1)S(1)}, bf16[32,1024]{1,0:T(8,128)(2,1)S(1)}, u32[]{:S(2)}, u32[]{:S(2)}) %collective-permute-start.3) | collective-permute-done | bytes 65568 | tf_op jit(solution)/shard_map/ppermute | solution.py:408
  12.7 0.6 %attend.3.refs_9_ = bf16[32,1152]{1,0:T(8,128)(2,1)S(1)} custom-call(s32[2]{0:T(128)S(4)} %place.1.refs_0_, f32[32,608]{1,0:T(8,128)S(1)} %get-tuple-element.23.refs_1_, bf16[32,1024]{1,0:T(8,128)(2,1)S(1)} %collective-permute-done.refs_3_.refs_2_, bf16[256,2048]{1,0:T(8,128)(2,1)S(1)} %get-tuple-element.25.refs_3_.refs_4_, ...), custom_call_target="tpu_custom_call" | custom-call | tf_op jit(solution)/shard_map/attend/pallas_call | solution.py:448
  13.4 2.4 %collective-permute-start.4 = (bf16[32,1152]{1,0:T(8,128)(2,1)S(1)}, bf16[32,1152]{1,0:T(8,128)(2,1)S(1)}, u32[]{:S(2)}, u32[]{:S(2)}) collective-permute-start(bf16[32,1152]{1,0:T(8,128)(2,1)S(1)} %attend.3.refs_9_), channel_id=1, source_target_pairs={{0,6},{1,7},{2,4},{3,5},{4,2},{5,3},{6,0},{7,1},{8,14},{9,15},{10,... | collective-permute-start | bytes 221192 | tf_op jit(solution)/shard_map/ppermute | solution.py:25
  15.7 1.6 %attend.5 = (bf16[32,1152]{1,0:T(8,128)(2,1)S(1)}, bf16[32,1152]{1,0:T(8,128)(2,1)S(1)}, bf16[1,1024,1024]{2,1,0:T(8,128)(2,1)S(1)}) custom-call(s32[2]{0:T(128)S(4)} %place.1.refs_0_, f32[32,608]{1,0:T(8,128)S(1)} %get-tuple-element.23.refs_1_, bf16[32,1024]{1,0:T(8,128)(2,1)S(1)} %collective-permute-done.5.refs_2_, ...), custom_call_target="tpu_custom_call" | custom-call | tf_op jit(solution)/shard_map/attend/pallas_call | solution.py:448
  17.4 0.1 collective-permute-start.7
  17.4 2.1 %collective-permute-start.8 = (bf16[32,1152]{1,0:T(8,128)(2,1)S(1)}, bf16[32,1152]{1,0:T(8,128)(2,1)S(1)}, u32[]{:S(2)}, u32[]{:S(2)}) collective-permute-start(bf16[32,1152]{1,0:T(8,128)(2,1)S(1)} %get-tuple-element.31), channel_id=1, source_target_pairs={{0,2},{1,3},{2,0},{3,1},{4,6},{5,7},{6,4},{7,5},{8,10},{9,11},{10,... | collective-permute-start | bytes 221192 | tf_op jit(solution)/shard_map/ppermute | solution.py:25
  19.5 0.1 collective-permute-done.4.refs_8_.refs_1_
  19.6 3.5 %attend.4 = (bf16[32,1152]{1,0:T(8,128)(2,1)S(1)}, bf16[4,1024,1024]{2,1,0:T(8,128)(2,1)S(1)}) custom-call(s32[2]{0:T(128)S(4)} %place.1.refs_0_, f32[32,608]{1,0:T(8,128)S(1)} %get-tuple-element.23.refs_1_, bf16[32,1024]{1,0:T(8,128)(2,1)S(1)} %get-tuple-element.24.refs_2_, bf16[256,2048]{1,0:T(8,128)(2,1)S(1)} %get-tuple-element.25.refs_3_.refs_4_, ...), custom_call_target="tpu_custom_call" | custom-call | tf_op jit(solution)/shard_map/attend/pallas_call | solution.py:448
  23.2 0.0 collective-permute-done.8.refs_3_
  23.2 1.8 %project_away.1 = (bf16[4,32,1024]{2,1,0:T(8,128)(2,1)S(1)}, bf16[32,1024]{1,0:T(8,128)(2,1)S(1)}, bf16[1,1024,1024]{2,1,0:T(8,128)(2,1)S(1)}) custom-call(s32[2]{0:T(128)S(4)} %place.1.refs_0_, bf16[32,1152]{1,0:T(8,128)(2,1)S(1)} %get-tuple-element.29.refs_0_, bf16[32,1152]{1,0:T(8,128)(2,1)S(1)} %collective-permute-done.4.refs_8_.refs_1_, ...), custom_call_target="tpu_custom_call" | custom-call | tf_op jit(solution)/shard_map/project_away/pallas_call | solution.py:474
  25.0 0.1 collective-permute-start.9
  25.0 0.8 %project_far.1.home = f32[2,32,1024]{2,1,0:T(8,128)S(1)} custom-call(bf16[32,1024]{1,0:T(8,128)(2,1)S(1)} %get-tuple-element.36.attended, bf16[4,1024,1024]{2,1,0:T(8,128)(2,1)S(1)} %get-tuple-element.35.refs_8_.refs_0_), custom_call_target="tpu_custom_call" | custom-call | tf_op jit(solution)/shard_map/project_far/pallas_call | solution.py:490
  25.9 0.7 %collective-permute-done.9.sibling = bf16[4,32,1024]{2,1,0:T(8,128)(2,1)S(1)} collective-permute-done((bf16[4,32,1024]{2,1,0:T(8,128)(2,1)S(1)}, bf16[4,32,1024]{2,1,0:T(8,128)(2,1)S(1)}, u32[]{:S(2)}, u32[]{:S(2)}) %collective-permute-start.9) | collective-permute-done | bytes 262176 | tf_op jit(solution)/shard_map/ppermute | solution.py:25
  26.6 1.6 %collective-permute-start.10 = (bf16[32,1024]{1,0:T(8,128)(2,1)S(1)}, bf16[32,1024]{1,0:T(8,128)(2,1)S(1)}, u32[]{:S(2)}, u32[]{:S(2)}) collective-permute-start(bf16[32,1024]{1,0:T(8,128)(2,1)S(1)} %get-tuple-element.38.after), channel_id=1, source_target_pairs={{0,4},{1,5},{2,6},{3,7},{4,0},{5,1},{6,2},{7,3},{8,12},{9,13},{10,... | collective-permute-start | bytes 196616 | tf_op jit(solution)/shard_map/ppermute | solution.py:25
  28.1 1.5 %collective-permute-start.11 = (bf16[32,1024]{1,0:T(8,128)(2,1)S(1)}, bf16[32,1024]{1,0:T(8,128)(2,1)S(1)}, u32[]{:S(2)}, u32[]{:S(2)}) collective-permute-start(bf16[32,1024]{1,0:T(8,128)(2,1)S(1)} %get-tuple-element.40), channel_id=1, source_target_pairs={{0,6},{1,7},{2,4},{3,5},{4,2},{5,3},{6,0},{7,1},{8,14},{9,15},{10,... | collective-permute-start | bytes 196616 | tf_op jit(solution)/shard_map/ppermute | solution.py:25
  29.7 0.5 %project_near.1.after = bf16[32,1024]{1,0:T(8,128)(2,1)S(1)} custom-call(bf16[32,1024]{1,0:T(8,128)(2,1)S(1)} %get-tuple-element.36.attended, bf16[4,32,1024]{2,1,0:T(8,128)(2,1)S(1)} %collective-permute-done.9.sibling, bf16[32,1024]{1,0:T(8,128)(2,1)S(1)} %get-tuple-element.38.after, bf16[1,1024,1024]{2,1,0:T(8,128)(2,1)S(1)} %get-tuple-element.39.refs_0_), custom_call_target="tpu_custom_call" | custom-call | tf_op jit(solution)/shard_map/project_near/pallas_call | solution.py:510
  30.1 0.5 %collective-permute-start.12 = (bf16[32,1024]{1,0:T(8,128)(2,1)S(1)}, bf16[32,1024]{1,0:T(8,128)(2,1)S(1)}, u32[]{:S(2)}, u32[]{:S(2)}) collective-permute-start(bf16[32,1024]{1,0:T(8,128)(2,1)S(1)} %project_near.1.after), channel_id=1, source_target_pairs={{0,2},{1,3},{2,0},{3,1},{4,6},{5,7},{6,4},{7,5},{8,10},{9,11},{10,... | collective-permute-start | bytes 196616 | tf_op jit(solution)/shard_map/ppermute | solution.py:25
  30.7 0.5 %project_own.1.own = f32[32,1024]{1,0:T(8,128)S(1)} custom-call(bf16[32,1024]{1,0:T(8,128)(2,1)S(1)} %get-tuple-element.36.attended, bf16[4,32,1024]{2,1,0:T(8,128)(2,1)S(1)} %collective-permute-done.9.sibling, bf16[32,1024]{1,0:T(8,128)(2,1)S(1)} %project_near.1.after, bf16[4,1024,1024]{2,1,0:T(8,128)(2,1)S(1)} %get-tuple-element.35.refs_8_.refs_0_), custom_call_target="tpu_custom_call" | custom-call | tf_op jit(solution)/shard_map/project_own/pallas_call | solution.py:519
  31.1 3.6 %collective-permute-done.10.refs_0_ = bf16[32,1024]{1,0:T(8,128)(2,1)S(1)} collective-permute-done((bf16[32,1024]{1,0:T(8,128)(2,1)S(1)}, bf16[32,1024]{1,0:T(8,128)(2,1)S(1)}, u32[]{:S(2)}, u32[]{:S(2)}) %collective-permute-start.10) | collective-permute-done | bytes 65568 | tf_op jit(solution)/shard_map/ppermute | solution.py:25
  34.7 1.2 %collective-permute-done.12 = bf16[32,1024]{1,0:T(8,128)(2,1)S(1)} collective-permute-done((bf16[32,1024]{1,0:T(8,128)(2,1)S(1)}, bf16[32,1024]{1,0:T(8,128)(2,1)S(1)}, u32[]{:S(2)}, u32[]{:S(2)}) %collective-permute-start.12) | collective-permute-done | bytes 65568 | tf_op jit(solution)/shard_map/ppermute | solution.py:25
  35.9 1.6 %collective-permute-start.13 = (bf16[32,1024]{1,0:T(8,128)(2,1)S(1)}, bf16[32,1024]{1,0:T(8,128)(2,1)S(1)}, u32[]{:S(2)}, u32[]{:S(2)}) collective-permute-start(bf16[32,1024]{1,0:T(8,128)(2,1)S(1)} %add_convert_fusion.1), channel_id=1, source_target_pairs={{0,16},{16,0},{1,17},{17,1},{2,18},{18,2},{3,19},{19,3},{4,20},{20... | collective-permute-start | bytes 196616 | tf_op jit(solution)/shard_map/ppermute | solution.py:539
  37.5 2.7 %collective-permute-done.13 = bf16[32,1024]{1,0:T(8,128)(2,1)S(1)} collective-permute-done((bf16[32,1024]{1,0:T(8,128)(2,1)S(1)}, bf16[32,1024]{1,0:T(8,128)(2,1)S(1)}, u32[]{:S(2)}, u32[]{:S(2)}) %collective-permute-start.13) | collective-permute-done | bytes 65568 | tf_op jit(solution)/shard_map/ppermute | solution.py:539
  40.3 0.7 %fusion.1 = bf16[1,32,1024]{2,1,0:T(8,128)(2,1)} fusion(bf16[32,1024]{1,0:T(8,128)(2,1)S(1)} %add_convert_fusion.1, f32[32,1024]{1,0:T(8,128)S(1)} %add_own.1, bf16[32,1024]{1,0:T(8,128)(2,1)S(1)} %collective-permute-done.12, bf16[32,1024]{1,0:T(8,128)(2,1)S(1)} %collective-permute-done.13, pred[]{:T(512)S(6)} %eq.3), kind=kLoop, calls=%fused_computation.4 | loop fusion | flops 196608 | bytes 393217 | tf_op jit(solution)/shard_map/broadcast_in_dim | solution.py:542
  (14 shorter events, 0.1 us)
Async XLA Ops:
  0.0 12.7 %collective-permute-start.1 = (bf16[256,2048]{1,0:T(8,128)(2,1)}, bf16[256,2048]{1,0:T(8,128)(2,1)S(1)}, u32[]{:S(2)}, u32[]{:S(2)}) collective-permute-start(bf16[256,2048]{1,0:T(8,128)(2,1)} %bitcast.12), channel_id=1, source_target_pairs={{0,1},{1,0},{2,3},{3,2},{4,5},{5,4},{6,7},{7,6},{8,9},{9,8},{10,11... | collective-permute-start | bytes 3145736 | tf_op jit(solution)/shard_map/ppermute | solution.py:25
  0.5 8.1 %collective-permute-start = (bf16[32,1024]{1,0:T(8,128)(2,1)}, bf16[32,1024]{1,0:T(8,128)(2,1)S(1)}, u32[]{:S(2)}, u32[]{:S(2)}) collective-permute-start(bf16[32,1024]{1,0:T(8,128)(2,1)} %bitcast.16), channel_id=1, source_target_pairs={{0,6},{1,7},{2,4},{3,5},{4,2},{5,3},{6,0},{7,1},{8,14},{9,15},{10,... | collective-permute-start | bytes 196616 | tf_op jit(solution)/shard_map/ppermute | solution.py:25
  5.1 3.5 %copy-start = (bf16[1,32,1024]{2,1,0:T(8,128)(2,1)S(1)}, bf16[1,32,1024]{2,1,0:T(8,128)(2,1)}, u32[]{:S(2)}) copy-start(bf16[1,32,1024]{2,1,0:T(8,128)(2,1)} %param.9) | copy-start | bytes 196612
  6.9 4.6 %collective-permute-start.2 = (bf16[32,1024]{1,0:T(8,128)(2,1)S(1)}, bf16[32,1024]{1,0:T(8,128)(2,1)S(1)}, u32[]{:S(2)}, u32[]{:S(2)}) collective-permute-start(bf16[32,1024]{1,0:T(8,128)(2,1)S(1)} %bitcast.11), channel_id=1, source_target_pairs={{0,8},{1,9},{2,10},{3,11},{4,12},{5,13},{6,14},{7,15},{8,0},{9,1},... | collective-permute-start | bytes 196616 | tf_op jit(solution)/shard_map/ppermute | solution.py:408
  8.5 4.3 %collective-permute-start.3 = (bf16[32,1024]{1,0:T(8,128)(2,1)S(1)}, bf16[32,1024]{1,0:T(8,128)(2,1)S(1)}, u32[]{:S(2)}, u32[]{:S(2)}) collective-permute-start(bf16[32,1024]{1,0:T(8,128)(2,1)S(1)} %bitcast.10), channel_id=1, source_target_pairs={{0,9},{1,8},{2,11},{3,10},{4,13},{5,12},{6,15},{7,14},{8,1},{9,0},... | collective-permute-start | bytes 196616 | tf_op jit(solution)/shard_map/ppermute | solution.py:408
  8.6 7.2 %collective-permute-start.5 = (bf16[32,1024]{1,0:T(8,128)(2,1)S(1)}, bf16[32,1024]{1,0:T(8,128)(2,1)S(1)}, u32[]{:S(2)}, u32[]{:S(2)}) collective-permute-start(bf16[32,1024]{1,0:T(8,128)(2,1)S(1)} %bitcast.18), channel_id=1, source_target_pairs={{0,4},{1,5},{2,6},{3,7},{4,0},{5,1},{6,2},{7,3},{8,12},{9,13},{10,... | collective-permute-start | bytes 196616 | tf_op jit(solution)/shard_map/ppermute | solution.py:25
  8.6 7.2 %collective-permute-start.6 = (bf16[32,1024]{1,0:T(8,128)(2,1)S(1)}, bf16[32,1024]{1,0:T(8,128)(2,1)S(1)}, u32[]{:S(2)}, u32[]{:S(2)}) collective-permute-start(bf16[32,1024]{1,0:T(8,128)(2,1)S(1)} %bitcast.19), channel_id=1, source_target_pairs={{0,2},{1,3},{2,0},{3,1},{4,6},{5,7},{6,4},{7,5},{8,10},{9,11},{10,... | collective-permute-start | bytes 196616 | tf_op jit(solution)/shard_map/ppermute | solution.py:25
  13.4 6.3 %collective-permute-start.4 = (bf16[32,1152]{1,0:T(8,128)(2,1)S(1)}, bf16[32,1152]{1,0:T(8,128)(2,1)S(1)}, u32[]{:S(2)}, u32[]{:S(2)}) collective-permute-start(bf16[32,1152]{1,0:T(8,128)(2,1)S(1)} %attend.3.refs_9_), channel_id=1, source_target_pairs={{0,6},{1,7},{2,4},{3,5},{4,2},{5,3},{6,0},{7,1},{8,14},{9,15},{10,... | collective-permute-start | bytes 221192 | tf_op jit(solution)/shard_map/ppermute | solution.py:25
  17.4 5.8 %collective-permute-start.7 = (bf16[32,1152]{1,0:T(8,128)(2,1)S(1)}, bf16[32,1152]{1,0:T(8,128)(2,1)S(1)}, u32[]{:S(2)}, u32[]{:S(2)}) collective-permute-start(bf16[32,1152]{1,0:T(8,128)(2,1)S(1)} %get-tuple-element.30), channel_id=1, source_target_pairs={{0,4},{1,5},{2,6},{3,7},{4,0},{5,1},{6,2},{7,3},{8,12},{9,13},{10,... | collective-permute-start | bytes 221192 | tf_op jit(solution)/shard_map/ppermute | solution.py:25
  17.4 5.7 %collective-permute-start.8 = (bf16[32,1152]{1,0:T(8,128)(2,1)S(1)}, bf16[32,1152]{1,0:T(8,128)(2,1)S(1)}, u32[]{:S(2)}, u32[]{:S(2)}) collective-permute-start(bf16[32,1152]{1,0:T(8,128)(2,1)S(1)} %get-tuple-element.31), channel_id=1, source_target_pairs={{0,2},{1,3},{2,0},{3,1},{4,6},{5,7},{6,4},{7,5},{8,10},{9,11},{10,... | collective-permute-start | bytes 221192 | tf_op jit(solution)/shard_map/ppermute | solution.py:25
  25.0 1.6 %collective-permute-start.9 = (bf16[4,32,1024]{2,1,0:T(8,128)(2,1)S(1)}, bf16[4,32,1024]{2,1,0:T(8,128)(2,1)S(1)}, u32[]{:S(2)}, u32[]{:S(2)}) collective-permute-start(bf16[4,32,1024]{2,1,0:T(8,128)(2,1)S(1)} %get-tuple-element.37), channel_id=1, source_target_pairs={{0,1},{1,0},{2,3},{3,2},{4,5},{5,4},{6,7},{7,6},{8,9},{9,8},{10,11... | collective-permute-start | bytes 786440 | tf_op jit(solution)/shard_map/ppermute | solution.py:25
  26.6 8.1 %collective-permute-start.10 = (bf16[32,1024]{1,0:T(8,128)(2,1)S(1)}, bf16[32,1024]{1,0:T(8,128)(2,1)S(1)}, u32[]{:S(2)}, u32[]{:S(2)}) collective-permute-start(bf16[32,1024]{1,0:T(8,128)(2,1)S(1)} %get-tuple-element.38.after), channel_id=1, source_target_pairs={{0,4},{1,5},{2,6},{3,7},{4,0},{5,1},{6,2},{7,3},{8,12},{9,13},{10,... | collective-permute-start | bytes 196616 | tf_op jit(solution)/shard_map/ppermute | solution.py:25
  28.1 6.5 %collective-permute-start.11 = (bf16[32,1024]{1,0:T(8,128)(2,1)S(1)}, bf16[32,1024]{1,0:T(8,128)(2,1)S(1)}, u32[]{:S(2)}, u32[]{:S(2)}) collective-permute-start(bf16[32,1024]{1,0:T(8,128)(2,1)S(1)} %get-tuple-element.40), channel_id=1, source_target_pairs={{0,6},{1,7},{2,4},{3,5},{4,2},{5,3},{6,0},{7,1},{8,14},{9,15},{10,... | collective-permute-start | bytes 196616 | tf_op jit(solution)/shard_map/ppermute | solution.py:25
  30.1 5.8 %copy-start.1 = (bf16[32,1024]{1,0:T(8,128)(2,1)S(1)}, bf16[32,1024]{1,0:T(8,128)(2,1)}, u32[]{:S(2)}) copy-start(bf16[32,1024]{1,0:T(8,128)(2,1)} %param.8) | copy-start | bytes 196612
  30.1 5.8 %collective-permute-start.12 = (bf16[32,1024]{1,0:T(8,128)(2,1)S(1)}, bf16[32,1024]{1,0:T(8,128)(2,1)S(1)}, u32[]{:S(2)}, u32[]{:S(2)}) collective-permute-start(bf16[32,1024]{1,0:T(8,128)(2,1)S(1)} %project_near.1.after), channel_id=1, source_target_pairs={{0,2},{1,3},{2,0},{3,1},{4,6},{5,7},{6,4},{7,5},{8,10},{9,11},{10,... | collective-permute-start | bytes 196616 | tf_op jit(solution)/shard_map/ppermute | solution.py:25
  35.9 4.3 %collective-permute-start.13 = (bf16[32,1024]{1,0:T(8,128)(2,1)S(1)}, bf16[32,1024]{1,0:T(8,128)(2,1)S(1)}, u32[]{:S(2)}, u32[]{:S(2)}) collective-permute-start(bf16[32,1024]{1,0:T(8,128)(2,1)S(1)} %add_convert_fusion.1), channel_id=1, source_target_pairs={{0,16},{16,0},{1,17},{17,1},{2,18},{18,2},{3,19},{19,3},{4,20},{20... | collective-permute-start | bytes 196616 | tf_op jit(solution)/shard_map/ppermute | solution.py:539
